TPU v7x, 32 devices: a whole 2x2x4 slice. The times are simulated.
32 devices in a mesh: expert: 8 (over z, x), dp: 4 (over y, core).
Axes of the slice: x: 2, y: 2, z: 4, core: 2. Of those that a mesh axis runs over, the one named last changes fastest.
Arguments:
- tokens: bfloat16 [4096, 2048], P(('expert', 'dp')), may hold values from -6 to 6
- cotangent: bfloat16 [4096, 2048], P(('expert', 'dp')), may hold values from -6 to 6
- expert_ids: int32 [4096, 4], P(('expert', 'dp')), may hold values from 0 to 7, all different within a row; in each aligned block of 128 rows (0 to 127, 128 to 255, ...) at most 72 rows name the same one
- gate_probs: float32 [4096, 4], P(('expert', 'dp')), may hold values from 0.05 to 1
- w_gate: bfloat16 [8, 2048, 768], P('expert', 'dp'), may hold values from -0.125 to 0.125
- w_up: bfloat16 [8, 2048, 768], P('expert', 'dp'), may hold values from -0.125 to 0.125
- w_down: bfloat16 [8, 768, 2048], P('expert', 'dp'), may hold values from -0.21875 to 0.21875
Outputs:
- grad_tokens: bfloat16 [4096, 2048], P(('expert', 'dp'))
- grad_gate: bfloat16 [8, 2048, 768], P('expert', 'dp')
- grad_up: bfloat16 [8, 2048, 768], P('expert', 'dp')
- grad_down: bfloat16 [8, 768, 2048], P('expert', 'dp')
Inputs may be any that keep to these rules, and one draw needn't show every extreme that they name: `expert_ids`: the 4 experts of a token differ. Among the rows of one device no expert is named more than 72 times, a bound that some block reaches.
All inputs are finite; a program needn't handle non-finite values.
Results may differ from a plain program's by a relative error of at most 0.0064.
Values may be sent and summed in bfloat16 or wider, within the bound.
No kernel may reach another device: no remote copies, remote signals or barrier semaphores. Data moves between devices by JAX's collectives and lax.ppermute only.
A program may use at most 128 MiB of HBM per device.

v0:
```python
import jax
import jax.numpy as jnp
from jax import lax
from jax.sharding import PartitionSpec as P


def silu_parts(pre_gate):
    sigma = jax.nn.sigmoid(pre_gate)
    return (pre_gate * sigma, sigma * (1.0 + pre_gate * (1.0 - sigma)))


def shards(tokens, cotangent, expert_ids, gate_probs, w_gate, w_up, w_down):
    tok_rows, top_count = expert_ids.shape
    width = tokens.shape[1]
    owners = lax.axis_size("expert")
    slot_cap = (tok_rows * top_count * 9 + 8 * owners - 1) // (8 * owners)
    entries = tok_rows * top_count
    flat_ids = expert_ids.reshape(-1)
    one_hot = (flat_ids[:, None] == jnp.arange(owners, dtype=jnp.int32)[None, :]).astype(jnp.int32)
    ranks = jnp.sum((jnp.cumsum(one_hot, axis=0) - 1) * one_hot, axis=1)
    slots = flat_ids * slot_cap + ranks
    source = (
        jnp.zeros((owners * slot_cap,), jnp.int32)
        .at[slots]
        .set(jnp.arange(entries, dtype=jnp.int32) // top_count)
    )
    filled = jnp.zeros((owners * slot_cap,), jnp.bool_).at[slots].set(True)
    slot_probs = jnp.zeros((owners * slot_cap,), jnp.float32).at[slots].set(gate_probs.reshape(-1))
    send_rows = jnp.where(filled[:, None], tokens[source], jnp.zeros((), jnp.bfloat16)).reshape(
        owners, slot_cap, width
    )
    send_cot = (
        (slot_probs[:, None] * cotangent[source].astype(jnp.float32))
        .astype(jnp.bfloat16)
        .reshape(owners, slot_cap, width)
    )
    full_gate, full_up, full_down = (
        lax.all_gather(w_gate, "dp", axis=1, tiled=True),
        lax.all_gather(w_up, "dp", axis=1, tiled=True),
        lax.all_gather(w_down, "dp", axis=1, tiled=True),
    )
    gate_full = full_gate[0]
    up_full = full_up[0]
    down_full = full_down[0]
    got_rows, got_cot = (
        lax.all_to_all(send_rows, "expert", split_axis=0, concat_axis=0, tiled=True),
        lax.all_to_all(send_cot, "expert", split_axis=0, concat_axis=0, tiled=True),
    )
    rows = got_rows.reshape(-1, width)
    pre_gate = jnp.dot(rows, gate_full, preferred_element_type=jnp.float32)
    pre_up = jnp.dot(rows, up_full, preferred_element_type=jnp.float32)
    pre_gate, pre_up = (pre_gate, pre_up)
    scaled = got_cot.reshape(-1, width)
    act_value, act_slope = silu_parts(pre_gate)
    activ = (act_value * pre_up).astype(jnp.bfloat16)
    grad_act = jnp.dot(scaled, down_full.T, preferred_element_type=jnp.float32)
    grad_pre_gate = (grad_act * pre_up * act_slope).astype(jnp.bfloat16)
    grad_pre_up = (grad_act * act_value).astype(jnp.bfloat16)
    slot_grad = jnp.dot(grad_pre_gate, gate_full.T, preferred_element_type=jnp.float32)
    slot_grad = (
        slot_grad + jnp.dot(grad_pre_up, up_full.T, preferred_element_type=jnp.float32)
    ).astype(jnp.bfloat16)
    returned = lax.all_to_all(
        slot_grad.reshape(owners, slot_cap, width),
        "expert",
        split_axis=0,
        concat_axis=0,
        tiled=True,
    ).reshape(-1, width)
    per_entry = returned[slots].astype(jnp.float32).reshape(tok_rows, top_count, width)
    grad_tokens = jnp.sum(per_entry, axis=1).astype(jnp.bfloat16)
    part_gate = jnp.dot(rows.T, grad_pre_gate, preferred_element_type=jnp.float32)
    part_up = jnp.dot(rows.T, grad_pre_up, preferred_element_type=jnp.float32)
    part_down = jnp.dot(activ.T, scaled, preferred_element_type=jnp.float32)
    sum_gate, sum_up, sum_down = (
        lax.psum_scatter(part_gate, "dp", scatter_dimension=0, tiled=True),
        lax.psum_scatter(part_up, "dp", scatter_dimension=0, tiled=True),
        lax.psum_scatter(part_down, "dp", scatter_dimension=0, tiled=True),
    )
    return (
        grad_tokens,
        sum_gate.astype(jnp.bfloat16)[None],
        sum_up.astype(jnp.bfloat16)[None],
        sum_down.astype(jnp.bfloat16)[None],
    )


def solution(mesh):
    placed = (
        P(("expert", "dp"), None),
        P(("expert", "dp"), None),
        P(("expert", "dp"), None),
        P(("expert", "dp"), None),
        P("expert", "dp", None),
        P("expert", "dp", None),
        P("expert", "dp", None),
    )
    return jax.shard_map(
        shards,
        mesh=mesh,
        in_specs=placed,
        out_specs=(
            P(("expert", "dp"), None),
            P("expert", "dp", None),
            P("expert", "dp", None),
            P("expert", "dp", None),
        ),
        check_vma=False,
    )
```

profile of v0, /device:TPU:0, one launch (start us, length us, event | category | flops | bytes accessed | tf_op | source)
XLA Modules:
  0.0 344.1 jit_solution(8382207834299747241)
XLA Ops:
  7.2 0.0 copy-start
  7.2 0.0 all-gather.8.cloned.1.call-start
  7.2 0.7 all-gather.8.cloned.1.call-update
  7.9 0.0 all-gather.6.cloned.1.call-start
  8.0 0.7 all-gather.6.cloned.1.call-update
  8.7 0.7 broadcast_multiply_fusion
  9.4 0.8 copy.12
  10.1 0.1 eq.29
  10.2 0.1 eq.25
  10.4 1.1 reduce-window.6
  11.5 0.2 slice_reduce_fusion
  11.8 0.1 fusion.16
  11.9 0.1 copy.11
  12.0 0.1 mul.53
  12.1 2.4 scatter_custom_fusion.1
  14.6 2.4 scatter_custom_fusion.2
  17.0 0.1 broadcast_in_dim.47
  17.1 0.0 copy-done
  17.1 3.4 gather_fusion.1
  20.6 1.6 broadcast_select_fusion
  22.2 7.4 %all-to-all-start.1 = ((bf16[8,72,2048]{2,1,0:T(8,128)(2,1)}), bf16[8,72,2048]{2,1,0:T(8,128)(2,1)}, u32[]{:S(2)}, u32[]{:S(2)}) async-start(bf16[8,72,2048]{2,1,0:T(8,128)(2,1)} %broadcast_select_fusion), calls=%async_computation.1 | async-start | bytes 4718592 | tf_op jit(solution)/shard_map/all_to_all | solution.py:46
  29.6 0.0 all-gather.4.cloned.1.call-start
  29.6 0.7 all-gather.4.cloned.1.call-update
  30.3 0.0 copy-done.2
  30.3 0.0 copy-start.3
  30.3 3.4 gather_fusion
  33.7 0.0 copy-done.3
  33.7 0.1 copy.14
  33.8 0.1 reshape.126
  34.0 2.4 scatter_custom_fusion
  36.4 0.1 mul.55
  36.5 1.9 fusion
  38.4 45.1 %all-to-all-done.1 = bf16[8,72,2048]{2,1,0:T(8,128)(2,1)} async-done(((bf16[8,72,2048]{2,1,0:T(8,128)(2,1)}), bf16[8,72,2048]{2,1,0:T(8,128)(2,1)}, u32[]{:S(2)}, u32[]{:S(2)}) %all-to-all-start.1) | async-done | bytes 2359328 | tf_op jit(solution)/shard_map/all_to_all | solution.py:46
  83.5 3.6 %all-to-all-start = ((bf16[8,72,2048]{2,1,0:T(8,128)(2,1)}), bf16[8,72,2048]{2,1,0:T(8,128)(2,1)S(1)}, u32[]{:S(2)}, u32[]{:S(2)}) async-start(bf16[8,72,2048]{2,1,0:T(8,128)(2,1)} %fusion), calls=%async_computation | async-start | bytes 4718592 | tf_op jit(solution)/shard_map/all_to_all | solution.py:47
  87.2 0.2 reduce-scatter.4.cloned.1.call-start
  87.4 0.0 all-gather.8.cloned.1.call-done
  87.4 5.9 %fusion.3 = f32[576,768]{1,0:T(8,128)} fusion(bf16[576,2048]{1,0:T(8,128)(2,1)} %bitcast.8, bf16[1,2048,768]{2,1,0:T(8,128)(2,1)} %all-gather.8.cloned.1.call-done), kind=kOutput, calls=%fused_computation.11 | convolution fusion | flops 1811939328 | bytes 7274496 | tf_op jit(solution)/shard_map/dot_general | solution.py:50
  93.3 5.8 %fusion.7 = f32[576,768]{1,0:T(8,128)} fusion(bf16[576,2048]{1,0:T(8,128)(2,1)} %bitcast.8, bf16[1,2048,768]{2,1,0:T(8,128)(2,1)} %all-gather.6.cloned.1.call-done), kind=kOutput, calls=%fused_computation.15 | convolution fusion | flops 1811939328 | bytes 7274496 | tf_op jit(solution)/shard_map/dot_general | solution.py:51
  99.1 42.1 %all-to-all-done = bf16[8,72,2048]{2,1,0:T(8,128)(2,1)S(1)} async-done(((bf16[8,72,2048]{2,1,0:T(8,128)(2,1)}), bf16[8,72,2048]{2,1,0:T(8,128)(2,1)S(1)}, u32[]{:S(2)}, u32[]{:S(2)}) %all-to-all-start) | async-done | bytes 2359328 | tf_op jit(solution)/shard_map/all_to_all | solution.py:47
  141.2 6.4 %multiply_convert_fusion.1 = (bf16[576,768]{1,0:T(8,128)(2,1)}, bf16[576,768]{1,0:T(8,128)(2,1)S(1)}) fusion(f32[576,768]{1,0:T(8,128)} %fusion.3, f32[576,768]{1,0:T(8,128)} %fusion.7, bf16[576,2048]{1,0:T(8,128)(2,1)S(1)} %bitcast.51, bf16[1,768,2048]{2,1,0:T(8,128)(2,1)} %all-gather.4.cloned.1.call-done), kind=kOutput, calls=%fused_computation.21 | convolution fusion | flops 1817690112 | bytes 10813440 | tf_op jit(solution)/shard_map/dot_general | solution.py:56
  147.6 0.9 copy-done.6
  148.5 7.0 %fusion.28 = f32[2048,768]{1,0:T(8,128)} fusion(bf16[576,2048]{1,0:T(8,128)(2,1)} %bitcast.8, bf16[576,768]{1,0:T(8,128)(2,1)S(1)} %get-tuple-element.5), kind=kOutput, calls=%fused_computation.54 | convolution fusion | flops 1811939328 | bytes 9535488 | tf_op jit(solution)/shard_map/dot_general | solution.py:72
  155.5 0.0 reduce-scatter.4.cloned.1.call-update
  155.5 0.0 reduce-scatter.6.cloned.1.call-start
  155.6 7.2 %fusion.29 = f32[2048,768]{1,0:T(8,128)} fusion(bf16[576,2048]{1,0:T(8,128)(2,1)} %bitcast.8, bf16[576,768]{1,0:T(8,128)(2,1)} %get-tuple-element.4), kind=kOutput, calls=%fused_computation.55 | convolution fusion | flops 1811939328 | bytes 9535488 | tf_op jit(solution)/shard_map/dot_general | solution.py:73
  162.8 0.0 reduce-scatter.6.cloned.1.call-update
  162.8 0.3 reduce-scatter.8.cloned.1.call-start
  163.1 7.7 %fusion.14 = f32[768,2048]{1,0:T(8,128)} fusion(bf16[576,2048]{1,0:T(8,128)(2,1)S(1)} %bitcast.52, f32[576,768]{1,0:T(8,128)} %fusion.7, f32[576,768]{1,0:T(8,128)} %fusion.3), kind=kOutput, calls=%fused_computation.25 | convolution fusion | flops 1814593536 | bytes 12189696 | tf_op jit(solution)/shard_map/dot_general | solution.py:74
  170.8 0.0 reduce-scatter.8.cloned.1.call-update
  170.8 1.1 copy-done.7
  172.0 4.1 %fusion.1 = f32[576,2048]{1,0:T(8,128)S(1)} fusion(bf16[576,768]{1,0:T(8,128)(2,1)S(1)} %copy-done.7, bf16[1,2048,768]{2,1,0:T(8,128)(2,1)} %all-gather.8.cloned.1.call-done), kind=kOutput, calls=%fused_computation.9 | convolution fusion | flops 1811939328 | bytes 8749056 | tf_op jit(solution)/shard_map/dot_general | solution.py:59
  176.0 0.0 copy-done.4
  176.0 0.0 copy-done.5
  176.1 3.4 add_convert_fusion
  179.5 4.0 %all-to-all-start.2 = ((bf16[8,72,2048]{2,1,0:T(8,128)(2,1)}), bf16[8,72,2048]{2,1,0:T(8,128)(2,1)S(1)}, u32[]{:S(2)}, u32[]{:S(2)}) async-start(bf16[8,72,2048]{2,1,0:T(8,128)(2,1)} %bitcast.53), calls=%async_computation.2 | async-start | bytes 4718592 | tf_op jit(solution)/shard_map/all_to_all | solution.py:63
  183.5 53.8 %all-to-all-done.2 = bf16[8,72,2048]{2,1,0:T(8,128)(2,1)S(1)} async-done(((bf16[8,72,2048]{2,1,0:T(8,128)(2,1)}), bf16[8,72,2048]{2,1,0:T(8,128)(2,1)S(1)}, u32[]{:S(2)}, u32[]{:S(2)}) %all-to-all-start.2) | async-done | bytes 2359328 | tf_op jit(solution)/shard_map/all_to_all | solution.py:63
  237.4 3.3 gather_fusion.2
  240.7 2.7 gather.17
  243.4 3.9 %reduce_sum.25 = bf16[128,2048]{1,0:T(8,128)(2,1)} reduce(bf16[128,4,2048]{2,1,0:T(4,128)(2,1)S(1)} %gather.17, bf16[]{:T(256)} %constant.43.clone.1), dimensions={1}, to_apply=%region_6.7 | reduce | flops 786432 | bytes 2621442 | tf_op jit(solution)/shard_map/reduce_sum | solution.py:71
  247.3 2.4 convert_bitcast_fusion.2
  249.7 24.4 %reduce-scatter.6.cloned.1.call-done = f32[512,768]{1,0:T(8,128)} async-done(((f32[2048,768]{1,0:T(8,128)}), f32[512,768]{1,0:T(8,128)}) %reduce-scatter.6.cloned.1.call-update) | async-done | bytes 1572880 | tf_op jit(solution)/shard_map/reduce_scatter | solution.py:77
  274.1 2.4 convert_bitcast_fusion.1
  276.5 58.4 %reduce-scatter.8.cloned.1.call-done = f32[192,2048]{1,0:T(8,128)} async-done(((f32[768,2048]{1,0:T(8,128)}), f32[192,2048]{1,0:T(8,128)}) %reduce-scatter.8.cloned.1.call-update) | async-done | bytes 1572880 | tf_op jit(solution)/shard_map/reduce_scatter | solution.py:78
  334.8 2.4 convert_bitcast_fusion
  (19 shorter events, 0.1 us)
Async XLA Ops:
  7.2 10.0 %copy-start = (bf16[128,2048]{1,0:T(8,128)(2,1)S(1)}, bf16[128,2048]{1,0:T(8,128)(2,1)}, u32[]{:S(2)}) copy-start(bf16[128,2048]{1,0:T(8,128)(2,1)} %param.7) | copy-start | bytes 1572868
  7.2 80.2 %all-gather.8.cloned.1.call-start = ((), (), s32[]{:S(2)}) async-start(), calls=%async_computation.8 | async-start | bytes 3932160 | tf_op jit(solution)/shard_map/all_gather | solution.py:38
  7.9 85.4 %all-gather.6.cloned.1.call-start = ((), (), s32[]{:S(2)}) async-start(), calls=%async_computation.7 | async-start | bytes 3932160 | tf_op jit(solution)/shard_map/all_gather | solution.py:39
  22.2 8.1 %copy-start.2 = (bf16[128,2048]{1,0:T(8,128)(2,1)S(1)}, bf16[128,2048]{1,0:T(8,128)(2,1)}, u32[]{:S(2)}) copy-start(bf16[128,2048]{1,0:T(8,128)(2,1)} %param.8) | copy-start | bytes 1572868
  22.2 61.3 %all-to-all-start.1 = ((bf16[8,72,2048]{2,1,0:T(8,128)(2,1)}), bf16[8,72,2048]{2,1,0:T(8,128)(2,1)}, u32[]{:S(2)}, u32[]{:S(2)}) async-start(bf16[8,72,2048]{2,1,0:T(8,128)(2,1)} %broadcast_select_fusion), calls=%async_computation.1 | async-start | bytes 4718592 | tf_op jit(solution)/shard_map/all_to_all | solution.py:46
  29.6 111.6 %all-gather.4.cloned.1.call-start = ((), (), s32[]{:S(2)}) async-start(), calls=%async_computation.6 | async-start | bytes 3932160 | tf_op jit(solution)/shard_map/all_gather | solution.py:40
  30.3 3.4 copy-start.3
  83.5 57.7 %all-to-all-start = ((bf16[8,72,2048]{2,1,0:T(8,128)(2,1)}), bf16[8,72,2048]{2,1,0:T(8,128)(2,1)S(1)}, u32[]{:S(2)}, u32[]{:S(2)}) async-start(bf16[8,72,2048]{2,1,0:T(8,128)(2,1)} %fusion), calls=%async_computation | async-start | bytes 4718592 | tf_op jit(solution)/shard_map/all_to_all | solution.py:47
  87.2 160.1 %reduce-scatter.4.cloned.1.call-start = ((), (), s32[]{:S(2)}) async-start(), calls=%async_computation.9 | async-start | bytes 7864320 | tf_op jit(solution)/shard_map/reduce_scatter | solution.py:76
  147.6 0.9 copy-start.6
  155.5 118.5 %reduce-scatter.6.cloned.1.call-start = ((), (), s32[]{:S(2)}) async-start(), calls=%async_computation.10 | async-start | bytes 7864320 | tf_op jit(solution)/shard_map/reduce_scatter | solution.py:77
  162.8 172.0 %reduce-scatter.8.cloned.1.call-start = ((), (), s32[]{:S(2)}) async-start(), calls=%async_computation.11 | async-start | bytes 7864320 | tf_op jit(solution)/shard_map/reduce_scatter | solution.py:78
  170.8 1.2 copy-start.7
  172.0 4.1 %copy-start.4 = (bf16[1,2048,768]{2,1,0:T(8,128)(2,1)S(1)}, bf16[1,2048,768]{2,1,0:T(8,128)(2,1)}, u32[]{:S(2)}) copy-start(bf16[1,2048,768]{2,1,0:T(8,128)(2,1)} %all-gather.6.cloned.1.call-done) | copy-start | bytes 9437188
  172.0 4.1 %copy-start.5 = (bf16[576,768]{1,0:T(8,128)(2,1)S(1)}, bf16[576,768]{1,0:T(8,128)(2,1)}, u32[]{:S(2)}) copy-start(bf16[576,768]{1,0:T(8,128)(2,1)} %get-tuple-element.4) | copy-start | bytes 2654212
  179.5 57.9 %all-to-all-start.2 = ((bf16[8,72,2048]{2,1,0:T(8,128)(2,1)}), bf16[8,72,2048]{2,1,0:T(8,128)(2,1)S(1)}, u32[]{:S(2)}, u32[]{:S(2)}) async-start(bf16[8,72,2048]{2,1,0:T(8,128)(2,1)} %bitcast.53), calls=%async_computation.2 | async-start | bytes 4718592 | tf_op jit(solution)/shard_map/all_to_all | solution.py:63
  247.3 90.0 %copy-start.1 = (bf16[128,2048]{1,0:T(8,128)(2,1)S(1)}, bf16[128,2048]{1,0:T(8,128)(2,1)}, u32[]{:S(2)}) copy-start(bf16[128,2048]{1,0:T(8,128)(2,1)} %param.7) | copy-start | bytes 1572868
Sparse Core Ops, SparseCore 0:
  9.6 31.2 all-gather.7
  42.4 28.5 all-gather.5
  72.6 28.5 all-gather.3
  155.7 57.4 reduce-scatter.3
  215.7 58.3 reduce-scatter.5
  276.5 58.3 reduce-scatter.7
where the time goes:
time: 345 us; the launch traced here: 344 us
  waiting for transfers between devices  226 us (66%)
  matrix products  47.5 us (14%)
  local copies, waits for them, and re-layouts  24.1 us (7%)
  other arithmetic  16.5 us (5%)
  starting transfers between devices  15.7 us (5%)
  between operations  14.3 us (4%)
    reduce_scatter x1, waiting for transfers between devices, shards(): lax.psum_scatter(part_down, 'dp', scatter_dimension=0, tiled=True)  58.4 us
    all_to_all x1, waiting for transfers between devices, shards(): lax.all_to_all(slot_grad.reshape(owners, slot_cap, width), 'expert', spli...  53.8 us
    all_to_all x1, waiting for transfers between devices, shards(): lax.all_to_all(send_rows, 'expert', split_axis=0, concat_axis=0, tiled=True)  45.1 us
    all_to_all x1, waiting for transfers between devices, shards(): lax.all_to_all(send_cot, 'expert', split_axis=0, concat_axis=0, tiled=True)  42.1 us
    reduce_scatter x1, waiting for transfers between devices, shards(): lax.psum_scatter(part_up, 'dp', scatter_dimension=0, tiled=True)  24.4 us
    dot_general x1, matrix products, shards(): part_down = jnp.dot(activ.T, scaled, preferred_element_type=jnp.float32)  7.69 us
    all_to_all x1, starting transfers between devices, shards(): lax.all_to_all(send_rows, 'expert', split_axis=0, concat_axis=0, tiled=True)  7.38 us
    dot_general x1, matrix products, shards(): part_up = jnp.dot(rows.T, grad_pre_up, preferred_element_type=jnp.float32)  7.22 us
  transfers between devices with their start and end apart: 9, of which 5 were waited for; matrix products, arithmetic and copies ran while one was open for 20% of the time, Pallas kernels for 0%

commit v1 on v0

--- a/solution.py
+++ b/solution.py
@@ -7,6 +7,38 @@
 def silu_parts(pre_gate):
     sigma = jax.nn.sigmoid(pre_gate)
     return (pre_gate * sigma, sigma * (1.0 + pre_gate * (1.0 - sigma)))
+
+
+def swap(value, bit):
+    count = lax.axis_size("dp")
+    return lax.ppermute(value, "dp", [(i, i ^ bit) for i in range(count)])
+
+
+def gather_rows(shard):
+    if lax.axis_size("dp") != 4:
+        return lax.all_gather(shard, "dp", axis=0, tiled=True)
+    me = lax.axis_index("dp")
+    far = swap(shard, 2)
+    near, far_near = swap(shard, 1), swap(far, 1)
+    depth = shard.shape[0]
+    full = jnp.zeros((4 * depth, shard.shape[1]), shard.dtype)
+    for bits, part in ((0, shard), (1, near), (2, far), (3, far_near)):
+        full = lax.dynamic_update_slice(full, part, ((me ^ bits) * depth, 0))
+    return full
+
+
+def scatter_rows(total):
+    if lax.axis_size("dp") != 4:
+        return lax.psum_scatter(total, "dp", scatter_dimension=0, tiled=True)
+    me = lax.axis_index("dp")
+    depth = total.shape[0] // 4
+
+    def block(bits):
+        return lax.dynamic_slice(total, ((me ^ bits) * depth, 0), (depth, total.shape[1]))
+
+    far = block(2) + swap(block(3).astype(jnp.bfloat16), 1).astype(jnp.float32)
+    near = block(0) + swap(block(1).astype(jnp.bfloat16), 1).astype(jnp.float32)
+    return near + swap(far.astype(jnp.bfloat16), 2).astype(jnp.float32)
 
 
 def shards(tokens, cotangent, expert_ids, gate_probs, w_gate, w_up, w_down):
@@ -34,14 +66,7 @@
         .astype(jnp.bfloat16)
         .reshape(owners, slot_cap, width)
     )
-    full_gate, full_up, full_down = (
-        lax.all_gather(w_gate, "dp", axis=1, tiled=True),
-        lax.all_gather(w_up, "dp", axis=1, tiled=True),
-        lax.all_gather(w_down, "dp", axis=1, tiled=True),
-    )
-    gate_full = full_gate[0]
-    up_full = full_up[0]
-    down_full = full_down[0]
+    gate_full, up_full, down_full = gather_rows(w_gate[0]), gather_rows(w_up[0]), gather_rows(w_down[0])
     got_rows, got_cot = (
         lax.all_to_all(send_rows, "expert", split_axis=0, concat_axis=0, tiled=True),
         lax.all_to_all(send_cot, "expert", split_axis=0, concat_axis=0, tiled=True),
@@ -49,7 +74,6 @@
     rows = got_rows.reshape(-1, width)
     pre_gate = jnp.dot(rows, gate_full, preferred_element_type=jnp.float32)
     pre_up = jnp.dot(rows, up_full, preferred_element_type=jnp.float32)
-    pre_gate, pre_up = (pre_gate, pre_up)
     scaled = got_cot.reshape(-1, width)
     act_value, act_slope = silu_parts(pre_gate)
     activ = (act_value * pre_up).astype(jnp.bfloat16)
@@ -72,16 +96,11 @@
     part_gate = jnp.dot(rows.T, grad_pre_gate, preferred_element_type=jnp.float32)
     part_up = jnp.dot(rows.T, grad_pre_up, preferred_element_type=jnp.float32)
     part_down = jnp.dot(activ.T, scaled, preferred_element_type=jnp.float32)
-    sum_gate, sum_up, sum_down = (
-        lax.psum_scatter(part_gate, "dp", scatter_dimension=0, tiled=True),
-        lax.psum_scatter(part_up, "dp", scatter_dimension=0, tiled=True),
-        lax.psum_scatter(part_down, "dp", scatter_dimension=0, tiled=True),
-    )
     return (
         grad_tokens,
-        sum_gate.astype(jnp.bfloat16)[None],
-        sum_up.astype(jnp.bfloat16)[None],
-        sum_down.astype(jnp.bfloat16)[None],
+        scatter_rows(part_gate).astype(jnp.bfloat16)[None],
+        scatter_rows(part_up).astype(jnp.bfloat16)[None],
+        scatter_rows(part_down).astype(jnp.bfloat16)[None],
     )
 
 

time: 345 us -> 257 us (0.74)
  waiting for transfers between devices: 226 us -> 140 us
  between operations: 14.3 us -> 1.14 us
  starting transfers between devices: 15.7 us -> 26.2 us
  local copies, waits for them, and re-layouts: 24.1 us -> 34.4 us
  matrix products: 47.5 us -> 40.3 us
    ppermute x0 -> x18, waiting for transfers between devices: none -> 94.5 us  [swap(): return lax.ppermute(value, 'dp', [(i, i ^ bit) for i in range(count)])]
    reduce_scatter x3 -> x0, waiting for transfers between devices: 82.8 us -> none  [the longest x1 58.4 us: shards(): lax.psum_scatter(part_down, 'dp', scatter_dimension=0, tiled=True)]
    all_to_all x1, waiting for transfers between devices: 53.8 us -> 0.01 us  [shards(): lax.all_to_all(slot_grad.reshape(owners, slot_cap, width), 'expert', spli...]
    all_to_all x1, waiting for transfers between devices: 42.1 us -> 0.01 us  [shards(): lax.all_to_all(send_cot, 'expert', split_axis=0, concat_axis=0, tiled=True)]
    ppermute x0 -> x18, starting transfers between devices: none -> 9.24 us  [swap(): return lax.ppermute(value, 'dp', [(i, i ^ bit) for i in range(count)])]
    dynamic_update_slice x0 -> x12, local copies, waits for them, and re-layouts: none -> 7.72 us  [gather_rows(): full = lax.dynamic_update_slice(full, part, ((me ^ bits) * depth, 0))]
    broadcast_in_dim x3, other arithmetic: 7.18 us -> 3.61 us  [the longest x1 1.25 us: shards(): scatter_rows(part_down).astype(jnp.bfloat16)[None]]
  transfers between devices with their start and end apart: 9 -> 21, of which waited for: 5 -> 8; matrix products, arithmetic and copies ran while one was open for 20% -> 17% of each run, Pallas kernels for 0% -> 0%
where the time goes in v1:
time: 257 us; the launch traced here: 256 us
  waiting for transfers between devices  140 us (54%)
  matrix products  40.3 us (16%)
  local copies, waits for them, and re-layouts  34.4 us (13%)
  starting transfers between devices  26.2 us (10%)
  other arithmetic  13.7 us (5%)
    ppermute x18, waiting for transfers between devices, swap(): return lax.ppermute(value, 'dp', [(i, i ^ bit) for i in range(count)])  94.5 us
    all_to_all x1, waiting for transfers between devices, shards(): lax.all_to_all(send_rows, 'expert', split_axis=0, concat_axis=0, tiled=True)  45.9 us
    ppermute x18, starting transfers between devices, swap(): return lax.ppermute(value, 'dp', [(i, i ^ bit) for i in range(count)])  9.24 us
    dynamic_update_slice x12, local copies, waits for them, and re-layouts, gather_rows(): full = lax.dynamic_update_slice(full, part, ((me ^ bits) * depth, 0))  7.72 us
    all_to_all x1, starting transfers between devices, shards(): lax.all_to_all(send_rows, 'expert', split_axis=0, concat_axis=0, tiled=True)  7.38 us
    dot_general x1, matrix products, shards(): jnp.dot(rows.T, grad_pre_gate, preferred_element_type=jnp.float32)  7.15 us
    dot_general x1, matrix products, shards(): pre_gate = jnp.dot(rows, gate_full, preferred_element_type=jnp.float32)  6.68 us
    dot_general x1, matrix products, shards(): grad_act = jnp.dot(scaled, down_full.T, preferred_element_type=jnp.float32)  6.36 us
  transfers between devices with their start and end apart: 21, of which 8 were waited for; matrix products, arithmetic and copies ran while one was open for 17% of the time, Pallas kernels for 0%

profile of v1, /device:TPU:0, one launch (start us, length us, event | category | flops | bytes accessed | tf_op | source)
XLA Modules:
  0.0 256.1 jit_solution(5186814180193771381)
XLA Ops:
  0.6 0.7 broadcast_multiply_fusion
  1.4 0.8 copy.12
  2.6 1.1 reduce-window.6
  3.8 0.2 slice_reduce_fusion
  4.2 2.4 scatter_custom_fusion.1
  6.6 2.4 scatter_custom_fusion.2
  9.2 3.4 %gather_fusion.1 = bf16[576,2048]{1,0:T(8,128)(2,1)S(1)} fusion(bf16[128,2048]{1,0:T(8,128)(2,1)S(1)} %copy-done, s32[1024]{0:T(1024)S(1)} %pad_clamp_fusion.1), kind=kCustom, calls=%fused_computation.1 | custom fusion | bytes 4720896 | tf_op jit(solution)/shard_map/gather | solution.py:61
  12.6 1.7 broadcast_select_fusion
  14.3 7.4 %all-to-all-start.1 = ((bf16[8,72,2048]{2,1,0:T(8,128)(2,1)}), bf16[8,72,2048]{2,1,0:T(8,128)(2,1)}, u32[]{:S(2)}, u32[]{:S(2)}) async-start(bf16[8,72,2048]{2,1,0:T(8,128)(2,1)} %broadcast_select_fusion), calls=%async_computation.1 | async-start | bytes 4718592 | tf_op jit(solution)/shard_map/all_to_all | solution.py:71
  21.7 3.4 %gather_fusion = bf16[576,2048]{1,0:T(8,128)(2,1)S(1)} fusion(bf16[128,2048]{1,0:T(8,128)(2,1)S(1)} %copy-done.2, s32[1024]{0:T(1024)S(1)} %pad_clamp_fusion.1), kind=kCustom, calls=%fused_computation | custom fusion | bytes 4720896 | tf_op jit(solution)/shard_map/gather | solution.py:65
  25.3 2.4 scatter_custom_fusion
  27.8 1.9 fusion
  29.7 45.9 %all-to-all-done.1 = bf16[8,72,2048]{2,1,0:T(8,128)(2,1)} async-done(((bf16[8,72,2048]{2,1,0:T(8,128)(2,1)}), bf16[8,72,2048]{2,1,0:T(8,128)(2,1)}, u32[]{:S(2)}, u32[]{:S(2)}) %all-to-all-start.1) | async-done | bytes 2359328 | tf_op jit(solution)/shard_map/all_to_all | solution.py:71
  75.6 3.8 %all-to-all-start = ((bf16[8,72,2048]{2,1,0:T(8,128)(2,1)}), bf16[8,72,2048]{2,1,0:T(8,128)(2,1)S(1)}, u32[]{:S(2)}, u32[]{:S(2)}) async-start(bf16[8,72,2048]{2,1,0:T(8,128)(2,1)} %fusion), calls=%async_computation | async-start | bytes 4718592 | tf_op jit(solution)/shard_map/all_to_all | solution.py:72
  79.5 1.6 collective-permute-start.7
  81.3 0.5 collective-permute-start.4
  81.8 1.5 collective-permute-start.1
  83.3 0.4 broadcast_in_dim.48
  83.7 1.3 constant_dynamic-update-slice_fusion.11
  85.0 0.2 broadcast.87.clone
  85.3 0.8 copy-done.12
  86.1 0.2 broadcast.87.clone.1
  86.5 13.8 %collective-permute-done.7 = bf16[512,768]{1,0:T(8,128)(2,1)} collective-permute-done((bf16[512,768]{1,0:T(8,128)(2,1)}, bf16[512,768]{1,0:T(8,128)(2,1)}, u32[]{:S(2)}, u32[]{:S(2)}) %collective-permute-start.7) | collective-permute-done | bytes 786464 | tf_op jit(solution)/shard_map/ppermute | solution.py:14
  100.2 16.8 %collective-permute-done.4 = bf16[512,768]{1,0:T(8,128)(2,1)} collective-permute-done((bf16[512,768]{1,0:T(8,128)(2,1)}, bf16[512,768]{1,0:T(8,128)(2,1)}, u32[]{:S(2)}, u32[]{:S(2)}) %collective-permute-start.4) | collective-permute-done | bytes 786464 | tf_op jit(solution)/shard_map/ppermute | solution.py:14
  117.1 16.4 %collective-permute-done.1 = bf16[192,2048]{1,0:T(8,128)(2,1)} collective-permute-done((bf16[192,2048]{1,0:T(8,128)(2,1)}, bf16[192,2048]{1,0:T(8,128)(2,1)}, u32[]{:S(2)}, u32[]{:S(2)}) %collective-permute-start.1) | collective-permute-done | bytes 786464 | tf_op jit(solution)/shard_map/ppermute | solution.py:14
  133.5 1.2 constant_dynamic-update-slice_fusion.2
  134.7 1.2 constant_dynamic-update-slice_fusion.1
  135.9 1.2 constant_dynamic-update-slice_fusion.6
  137.1 1.2 constant_dynamic-update-slice_fusion.5
  138.4 1.2 constant_dynamic-update-slice_fusion.9
  139.9 6.7 %fusion.20 = f32[576,768]{1,0:T(8,128)} fusion(bf16[576,2048]{1,0:T(8,128)(2,1)} %bitcast.8, bf16[2048,768]{1,0:T(8,128)(2,1)S(1)} %constant_dynamic-update-slice_fusion), kind=kOutput, calls=%fused_computation.69 | convolution fusion | flops 1811939328 | bytes 7274496 | tf_op jit(solution)/shard_map/dot_general | solution.py:75
  146.6 4.9 %fusion.19 = f32[576,768]{1,0:T(8,128)} fusion(bf16[576,2048]{1,0:T(8,128)(2,1)} %bitcast.8, bf16[2048,768]{1,0:T(8,128)(2,1)S(1)} %constant_dynamic-update-slice_fusion.4), kind=kOutput, calls=%fused_computation.68 | convolution fusion | flops 1811939328 | bytes 7274496 | tf_op jit(solution)/shard_map/dot_general | solution.py:76
  151.5 6.4 %multiply_convert_fusion.2 = (bf16[576,768]{1,0:T(8,128)(2,1)S(1)}, bf16[576,768]{1,0:T(8,128)(2,1)S(1)}) fusion(f32[576,768]{1,0:T(8,128)} %fusion.20, f32[576,768]{1,0:T(8,128)} %fusion.19, bf16[576,2048]{1,0:T(8,128)(2,1)S(1)} %bitcast.47, bf16[768,2048]{1,0:T(8,128)(2,1)} %copy-done.3), kind=kOutput, calls=%fused_computation.12 | convolution fusion | flops 1817690112 | bytes 10813440 | tf_op jit(solution)/shard_map/dot_general | solution.py:80
  157.9 2.0 fusion.21
  160.0 7.2 %fusion.22 = f32[2048,768]{1,0:T(8,128)} fusion(bf16[576,2048]{1,0:T(8,128)(2,1)} %bitcast.8, bf16[576,768]{1,0:T(8,128)(2,1)S(1)} %get-tuple-element.10), kind=kOutput, calls=%fused_computation.71 | convolution fusion | flops 1811939328 | bytes 9535488 | tf_op jit(solution)/shard_map/dot_general | solution.py:96
  167.1 3.8 %add_convert_fusion = bf16[576,2048]{1,0:T(8,128)(2,1)} fusion(f32[576,2048]{1,0:T(8,128)S(1)} %fusion.21, bf16[576,768]{1,0:T(8,128)(2,1)S(1)} %get-tuple-element.10, bf16[2048,768]{1,0:T(8,128)(2,1)S(1)} %copy-done.5), kind=kOutput, calls=%fused_computation.8 | convolution fusion | flops 1814298624 | bytes 11108352 | tf_op jit(solution)/shard_map/dot_general | solution.py:83
  170.9 5.7 %all-to-all-start.2 = ((bf16[8,72,2048]{2,1,0:T(8,128)(2,1)}), bf16[8,72,2048]{2,1,0:T(8,128)(2,1)S(1)}, u32[]{:S(2)}, u32[]{:S(2)}) async-start(bf16[8,72,2048]{2,1,0:T(8,128)(2,1)} %bitcast.49), calls=%async_computation.2 | async-start | bytes 4718592 | tf_op jit(solution)/shard_map/all_to_all | solution.py:87
  176.6 2.2 dynamic-slice_convert_fusion.5
  178.8 0.3 collective-permute-start.10
  179.2 4.9 %fusion.2 = f32[768,2048]{1,0:T(8,128)S(1)} fusion(bf16[576,2048]{1,0:T(8,128)(2,1)S(1)} %bitcast.48, f32[576,768]{1,0:T(8,128)} %fusion.19, f32[576,768]{1,0:T(8,128)} %fusion.20), kind=kOutput, calls=%fused_computation.27 | convolution fusion | flops 1814593536 | bytes 12189696 | tf_op jit(solution)/shard_map/dot_general | solution.py:98
  184.2 4.5 %fusion.23 = f32[2048,768]{1,0:T(8,128)S(1)} fusion(bf16[576,2048]{1,0:T(8,128)(2,1)} %bitcast.8, bf16[576,768]{1,0:T(8,128)(2,1)S(1)} %copy-done.15), kind=kOutput, calls=%fused_computation.72 | convolution fusion | flops 1811939328 | bytes 9535488 | tf_op jit(solution)/shard_map/dot_general | solution.py:97
  188.7 0.2 dynamic-slice_convert_fusion.3
  188.9 0.3 collective-permute-start.13
  189.2 0.2 dynamic-slice_convert_fusion.1
  189.4 0.3 collective-permute-start.16
  189.7 0.2 collective-permute-start.9
  190.0 0.3 collective-permute-start.12
  190.3 0.2 collective-permute-start.15
  190.5 0.2 add_convert_fusion.6
  190.7 0.5 collective-permute-done.13
  191.2 1.5 collective-permute-start.11
  192.8 0.2 add_convert_fusion.4
  192.9 0.9 collective-permute-start.14
  193.9 0.2 add_convert_fusion.2
  194.1 1.2 collective-permute-start.17
  195.3 16.3 %collective-permute-done.11 = bf16[512,768]{1,0:T(8,128)(2,1)S(1)} collective-permute-done((bf16[512,768]{1,0:T(8,128)(2,1)S(1)}, bf16[512,768]{1,0:T(8,128)(2,1)S(1)}, u32[]{:S(2)}, u32[]{:S(2)}) %collective-permute-start.11) | collective-permute-done | bytes 786464 | tf_op jit(solution)/shard_map/ppermute | solution.py:14
  211.6 1.2 fusion.3
  212.8 15.7 %collective-permute-done.14 = bf16[512,768]{1,0:T(8,128)(2,1)S(1)} collective-permute-done((bf16[512,768]{1,0:T(8,128)(2,1)S(1)}, bf16[512,768]{1,0:T(8,128)(2,1)S(1)}, u32[]{:S(2)}, u32[]{:S(2)}) %collective-permute-start.14) | collective-permute-done | bytes 786464 | tf_op jit(solution)/shard_map/ppermute | solution.py:14
  228.5 1.2 fusion.4
  229.7 15.0 %collective-permute-done.17 = bf16[192,2048]{1,0:T(8,128)(2,1)S(1)} collective-permute-done((bf16[192,2048]{1,0:T(8,128)(2,1)S(1)}, bf16[192,2048]{1,0:T(8,128)(2,1)S(1)}, u32[]{:S(2)}, u32[]{:S(2)}) %collective-permute-start.17) | collective-permute-done | bytes 786464 | tf_op jit(solution)/shard_map/ppermute | solution.py:14
  244.6 1.2 fusion.5
  245.9 3.3 %gather_fusion.2 = bf16[512,2048]{1,0:T(8,128)(2,1)} fusion(bf16[576,2048]{1,0:T(8,128)(2,1)S(1)} %bitcast.42, s32[1024]{0:T(1024)S(1)} %pad_clamp_fusion), kind=kCustom, calls=%fused_computation.2 | custom fusion | bytes 4196352 | tf_op jit(solution)/shard_map/gather | solution.py:94
  249.1 3.1 %gather.17 = bf16[128,4,2048]{2,1,0:T(4,128)(2,1)S(1)} reshape(bf16[512,2048]{1,0:T(8,128)(2,1)} %gather_fusion.2) | data formatting | bytes 4194304 | tf_op jit(solution)/shard_map/gather | solution.py:94
  252.2 3.9 %reduce_sum.25 = bf16[128,2048]{1,0:T(8,128)(2,1)} reduce(bf16[128,4,2048]{2,1,0:T(4,128)(2,1)S(1)} %gather.17, bf16[]{:T(256)} %constant.27.clone.1), dimensions={1}, to_apply=%region_6.7 | reduce | flops 786432 | bytes 2621442 | tf_op jit(solution)/shard_map/reduce_sum | solution.py:95
  (79 shorter events, 1.9 us)
Async XLA Ops:
  0.6 8.6 %copy-start = (bf16[128,2048]{1,0:T(8,128)(2,1)S(1)}, bf16[128,2048]{1,0:T(8,128)(2,1)}, u32[]{:S(2)}) copy-start(bf16[128,2048]{1,0:T(8,128)(2,1)} %param.7) | copy-start | bytes 1572868
  14.3 7.4 %copy-start.2 = (bf16[128,2048]{1,0:T(8,128)(2,1)S(1)}, bf16[128,2048]{1,0:T(8,128)(2,1)}, u32[]{:S(2)}) copy-start(bf16[128,2048]{1,0:T(8,128)(2,1)} %param.8) | copy-start | bytes 1572868
  14.3 61.3 %all-to-all-start.1 = ((bf16[8,72,2048]{2,1,0:T(8,128)(2,1)}), bf16[8,72,2048]{2,1,0:T(8,128)(2,1)}, u32[]{:S(2)}, u32[]{:S(2)}) async-start(bf16[8,72,2048]{2,1,0:T(8,128)(2,1)} %broadcast_select_fusion), calls=%async_computation.1 | async-start | bytes 4718592 | tf_op jit(solution)/shard_map/all_to_all | solution.py:71
  21.7 3.4 %copy-start.13 = (f32[128,4]{0,1:T(4,128)S(1)}, f32[128,4]{0,1:T(4,128)}, u32[]{:S(2)}) copy-start(f32[128,4]{0,1:T(4,128)} %param.10) | copy-start | bytes 6148
  75.6 75.9 %all-to-all-start = ((bf16[8,72,2048]{2,1,0:T(8,128)(2,1)}), bf16[8,72,2048]{2,1,0:T(8,128)(2,1)S(1)}, u32[]{:S(2)}, u32[]{:S(2)}) async-start(bf16[8,72,2048]{2,1,0:T(8,128)(2,1)} %fusion), calls=%async_computation | async-start | bytes 4718592 | tf_op jit(solution)/shard_map/all_to_all | solution.py:72
  79.4 5.9 %collective-permute-start.6 = (bf16[512,768]{1,0:T(8,128)(2,1)}, bf16[512,768]{1,0:T(8,128)(2,1)}, u32[]{:S(2)}, u32[]{:S(2)}) collective-permute-start(bf16[512,768]{1,0:T(8,128)(2,1)} %bitcast.50), channel_id=1, source_target_pairs={{0,1},{1,0},{2,3},{3,2},{4,5},{5,4},{6,7},{7,6},{8,9},{9,8},{10,11... | collective-permute-start | bytes 2359304 | tf_op jit(solution)/shard_map/ppermute | solution.py:14
  79.5 20.7 %collective-permute-start.7 = (bf16[512,768]{1,0:T(8,128)(2,1)}, bf16[512,768]{1,0:T(8,128)(2,1)}, u32[]{:S(2)}, u32[]{:S(2)}) collective-permute-start(bf16[512,768]{1,0:T(8,128)(2,1)} %bitcast.51), channel_id=1, source_target_pairs={{0,2},{1,3},{2,0},{3,1},{4,6},{5,7},{6,4},{7,5},{8,10},{9,11},{10,... | collective-permute-start | bytes 2359304 | tf_op jit(solution)/shard_map/ppermute | solution.py:14
  81.1 54.8 %collective-permute-start.3 = (bf16[512,768]{1,0:T(8,128)(2,1)}, bf16[512,768]{1,0:T(8,128)(2,1)}, u32[]{:S(2)}, u32[]{:S(2)}) collective-permute-start(bf16[512,768]{1,0:T(8,128)(2,1)} %bitcast.52), channel_id=1, source_target_pairs={{0,1},{1,0},{2,3},{3,2},{4,5},{5,4},{6,7},{7,6},{8,9},{9,8},{10,11... | collective-permute-start | bytes 2359304 | tf_op jit(solution)/shard_map/ppermute | solution.py:14
  81.3 35.8 %collective-permute-start.4 = (bf16[512,768]{1,0:T(8,128)(2,1)}, bf16[512,768]{1,0:T(8,128)(2,1)}, u32[]{:S(2)}, u32[]{:S(2)}) collective-permute-start(bf16[512,768]{1,0:T(8,128)(2,1)} %bitcast.53), channel_id=1, source_target_pairs={{0,2},{1,3},{2,0},{3,1},{4,6},{5,7},{6,4},{7,5},{8,10},{9,11},{10,... | collective-permute-start | bytes 2359304 | tf_op jit(solution)/shard_map/ppermute | solution.py:14
  81.8 51.7 %collective-permute-start.1 = (bf16[192,2048]{1,0:T(8,128)(2,1)}, bf16[192,2048]{1,0:T(8,128)(2,1)}, u32[]{:S(2)}, u32[]{:S(2)}) collective-permute-start(bf16[192,2048]{1,0:T(8,128)(2,1)} %bitcast.54), channel_id=1, source_target_pairs={{0,2},{1,3},{2,0},{3,1},{4,6},{5,7},{6,4},{7,5},{8,10},{9,11},{10,... | collective-permute-start | bytes 2359304 | tf_op jit(solution)/shard_map/ppermute | solution.py:14
  83.7 1.5 copy-start.10
  85.0 1.1 copy-start.12
  85.2 1.2 copy-start.11
  86.1 52.2 %collective-permute-start = (bf16[192,2048]{1,0:T(8,128)(2,1)S(1)}, bf16[192,2048]{1,0:T(8,128)(2,1)S(1)}, u32[]{:S(2)}, u32[]{:S(2)}) collective-permute-start(bf16[192,2048]{1,0:T(8,128)(2,1)S(1)} %bitcast.55), channel_id=1, source_target_pairs={{0,1},{1,0},{2,3},{3,2},{4,5},{5,4},{6,7},{7,6},{8,9},{9,8},{10,11... | collective-permute-start | bytes 2359304 | tf_op jit(solution)/shard_map/ppermute | solution.py:14
  100.2 39.4 %collective-permute-start.8 = (bf16[512,768]{1,0:T(8,128)(2,1)}, bf16[512,768]{1,0:T(8,128)(2,1)S(1)}, u32[]{:S(2)}, u32[]{:S(2)}) collective-permute-start(bf16[512,768]{1,0:T(8,128)(2,1)} %collective-permute-done.7), channel_id=1, source_target_pairs={{0,1},{1,0},{2,3},{3,2},{4,5},{5,4},{6,7},{7,6},{8,9},{9,8},{10,11... | collective-permute-start | bytes 2359304 | tf_op jit(solution)/shard_map/ppermute | solution.py:14
  117.1 22.6 %collective-permute-start.5 = (bf16[512,768]{1,0:T(8,128)(2,1)}, bf16[512,768]{1,0:T(8,128)(2,1)S(1)}, u32[]{:S(2)}, u32[]{:S(2)}) collective-permute-start(bf16[512,768]{1,0:T(8,128)(2,1)} %collective-permute-done.4), channel_id=1, source_target_pairs={{0,1},{1,0},{2,3},{3,2},{4,5},{5,4},{6,7},{7,6},{8,9},{9,8},{10,11... | collective-permute-start | bytes 2359304 | tf_op jit(solution)/shard_map/ppermute | solution.py:14
  133.5 6.3 %collective-permute-start.2 = (bf16[192,2048]{1,0:T(8,128)(2,1)}, bf16[192,2048]{1,0:T(8,128)(2,1)S(1)}, u32[]{:S(2)}, u32[]{:S(2)}) collective-permute-start(bf16[192,2048]{1,0:T(8,128)(2,1)} %collective-permute-done.1), channel_id=1, source_target_pairs={{0,1},{1,0},{2,3},{3,2},{4,5},{5,4},{6,7},{7,6},{8,9},{9,8},{10,11... | collective-permute-start | bytes 2359304 | tf_op jit(solution)/shard_map/ppermute | solution.py:14
  139.7 6.9 %copy-start.4 = (bf16[2048,768]{1,0:T(8,128)(2,1)}, bf16[2048,768]{1,0:T(8,128)(2,1)S(1)}, u32[]{:S(2)}) copy-start(bf16[2048,768]{1,0:T(8,128)(2,1)S(1)} %constant_dynamic-update-slice_fusion) | copy-start | bytes 9437188
  139.8 6.8 %copy-start.6 = (bf16[2048,768]{1,0:T(8,128)(2,1)}, bf16[2048,768]{1,0:T(8,128)(2,1)S(1)}, u32[]{:S(2)}) copy-start(bf16[2048,768]{1,0:T(8,128)(2,1)S(1)} %constant_dynamic-update-slice_fusion.4) | copy-start | bytes 9437188
  139.9 6.7 %copy-start.3 = (bf16[768,2048]{1,0:T(8,128)(2,1)}, bf16[768,2048]{1,0:T(8,128)(2,1)S(1)}, u32[]{:S(2)}) copy-start(bf16[768,2048]{1,0:T(8,128)(2,1)S(1)} %constant_dynamic-update-slice_fusion.8) | copy-start | bytes 9437188
  151.5 6.4 %copy-start.8 = (bf16[8,72,2048]{2,1,0:T(8,128)(2,1)}, bf16[8,72,2048]{2,1,0:T(8,128)(2,1)S(1)}, u32[]{:S(2)}) copy-start(bf16[8,72,2048]{2,1,0:T(8,128)(2,1)S(1)} %all-to-all-done) | copy-start | bytes 7077892
  151.5 6.4 %copy-start.7 = (bf16[2048,768]{1,0:T(8,128)(2,1)S(1)}, bf16[2048,768]{1,0:T(8,128)(2,1)}, u32[]{:S(2)}) copy-start(bf16[2048,768]{1,0:T(8,128)(2,1)} %copy-done.6) | copy-start | bytes 9437188
  157.9 2.1 copy-start.14
  160.0 7.2 %copy-start.5 = (bf16[2048,768]{1,0:T(8,128)(2,1)S(1)}, bf16[2048,768]{1,0:T(8,128)(2,1)}, u32[]{:S(2)}) copy-start(bf16[2048,768]{1,0:T(8,128)(2,1)} %copy-done.4) | copy-start | bytes 9437188
  170.9 75.0 %all-to-all-start.2 = ((bf16[8,72,2048]{2,1,0:T(8,128)(2,1)}), bf16[8,72,2048]{2,1,0:T(8,128)(2,1)S(1)}, u32[]{:S(2)}, u32[]{:S(2)}) async-start(bf16[8,72,2048]{2,1,0:T(8,128)(2,1)} %bitcast.49), calls=%async_computation.2 | async-start | bytes 4718592 | tf_op jit(solution)/shard_map/all_to_all | solution.py:87
  176.6 2.6 %copy-start.9 = (bf16[8,72,2048]{2,1,0:T(8,128)(2,1)S(1)}, bf16[8,72,2048]{2,1,0:T(8,128)(2,1)}, u32[]{:S(2)}) copy-start(bf16[8,72,2048]{2,1,0:T(8,128)(2,1)} %copy-done.8) | copy-start | bytes 7077892
  178.8 5.3 %copy-start.15 = (bf16[576,768]{1,0:T(8,128)(2,1)S(1)}, bf16[576,768]{1,0:T(8,128)(2,1)}, u32[]{:S(2)}) copy-start(bf16[576,768]{1,0:T(8,128)(2,1)} %copy-done.14) | copy-start | bytes 2654212
  178.8 11.4 %collective-permute-start.10 = (bf16[512,768]{1,0:T(8,128)(2,1)S(1)}, bf16[512,768]{1,0:T(8,128)(2,1)S(1)}, u32[]{:S(2)}, u32[]{:S(2)}) collective-permute-start(bf16[512,768]{1,0:T(8,128)(2,1)S(1)} %get-tuple-element.9), channel_id=1, source_target_pairs={{0,1},{1,0},{2,3},{3,2},{4,5},{5,4},{6,7},{7,6},{8,9},{9,8},{10,11... | collective-permute-start | bytes 2359304 | tf_op jit(solution)/shard_map/ppermute | solution.py:14
  179.2 11.3 %slice-start = ((s8[6291456]{0:T(1024)(128)(4,1)}), s8[4194304]{0:T(1024)(128)(4,1)S(1)}, s32[]{:S(2)}) async-start(s8[6291456]{0:T(1024)(128)(4,1)} %bitcast.45), calls=%async_computation.3 | async-start | bytes 8388608
  184.2 6.3 %slice-start.1 = ((s8[6291456]{0:T(1024)(128)(4,1)}), s8[2097152]{0:T(1024)(128)(4,1)S(1)}, s32[]{:S(2)}) async-start(s8[6291456]{0:T(1024)(128)(4,1)} %bitcast.45), calls=%async_computation.4 | async-start | bytes 4194304
  188.9 2.4 collective-permute-start.13
  189.4 3.5 %collective-permute-start.16 = (bf16[192,2048]{1,0:T(8,128)(2,1)S(1)}, bf16[192,2048]{1,0:T(8,128)(2,1)S(1)}, u32[]{:S(2)}, u32[]{:S(2)}) collective-permute-start(bf16[192,2048]{1,0:T(8,128)(2,1)S(1)} %get-tuple-element.5), channel_id=1, source_target_pairs={{0,1},{1,0},{2,3},{3,2},{4,5},{5,4},{6,7},{7,6},{8,9},{9,8},{10,11... | collective-permute-start | bytes 2359304 | tf_op jit(solution)/shard_map/ppermute | solution.py:14
  189.7 4.4 %collective-permute-start.9 = (bf16[512,768]{1,0:T(8,128)(2,1)S(1)}, bf16[512,768]{1,0:T(8,128)(2,1)S(1)}, u32[]{:S(2)}, u32[]{:S(2)}) collective-permute-start(bf16[512,768]{1,0:T(8,128)(2,1)S(1)} %get-tuple-element.8), channel_id=1, source_target_pairs={{0,1},{1,0},{2,3},{3,2},{4,5},{5,4},{6,7},{7,6},{8,9},{9,8},{10,11... | collective-permute-start | bytes 2359304 | tf_op jit(solution)/shard_map/ppermute | solution.py:14
  190.0 22.8 %collective-permute-start.12 = (bf16[512,768]{1,0:T(8,128)(2,1)S(1)}, bf16[512,768]{1,0:T(8,128)(2,1)S(1)}, u32[]{:S(2)}, u32[]{:S(2)}) collective-permute-start(bf16[512,768]{1,0:T(8,128)(2,1)S(1)} %get-tuple-element.6), channel_id=1, source_target_pairs={{0,1},{1,0},{2,3},{3,2},{4,5},{5,4},{6,7},{7,6},{8,9},{9,8},{10,11... | collective-permute-start | bytes 2359304 | tf_op jit(solution)/shard_map/ppermute | solution.py:14
  190.3 39.4 %collective-permute-start.15 = (bf16[192,2048]{1,0:T(8,128)(2,1)S(1)}, bf16[192,2048]{1,0:T(8,128)(2,1)S(1)}, u32[]{:S(2)}, u32[]{:S(2)}) collective-permute-start(bf16[192,2048]{1,0:T(8,128)(2,1)S(1)} %get-tuple-element.4), channel_id=1, source_target_pairs={{0,1},{1,0},{2,3},{3,2},{4,5},{5,4},{6,7},{7,6},{8,9},{9,8},{10,11... | collective-permute-start | bytes 2359304 | tf_op jit(solution)/shard_map/ppermute | solution.py:14
  191.2 20.4 %collective-permute-start.11 = (bf16[512,768]{1,0:T(8,128)(2,1)S(1)}, bf16[512,768]{1,0:T(8,128)(2,1)S(1)}, u32[]{:S(2)}, u32[]{:S(2)}) collective-permute-start(bf16[512,768]{1,0:T(8,128)(2,1)S(1)} %add_convert_fusion.6), channel_id=1, source_target_pairs={{0,2},{1,3},{2,0},{3,1},{4,6},{5,7},{6,4},{7,5},{8,10},{9,11},{10,... | collective-permute-start | bytes 2359304 | tf_op jit(solution)/shard_map/ppermute | solution.py:14
  192.9 35.5 %collective-permute-start.14 = (bf16[512,768]{1,0:T(8,128)(2,1)S(1)}, bf16[512,768]{1,0:T(8,128)(2,1)S(1)}, u32[]{:S(2)}, u32[]{:S(2)}) collective-permute-start(bf16[512,768]{1,0:T(8,128)(2,1)S(1)} %add_convert_fusion.4), channel_id=1, source_target_pairs={{0,2},{1,3},{2,0},{3,1},{4,6},{5,7},{6,4},{7,5},{8,10},{9,11},{10,... | collective-permute-start | bytes 2359304 | tf_op jit(solution)/shard_map/ppermute | solution.py:14
  194.1 50.5 %collective-permute-start.17 = (bf16[192,2048]{1,0:T(8,128)(2,1)S(1)}, bf16[192,2048]{1,0:T(8,128)(2,1)S(1)}, u32[]{:S(2)}, u32[]{:S(2)}) collective-permute-start(bf16[192,2048]{1,0:T(8,128)(2,1)S(1)} %add_convert_fusion.2), channel_id=1, source_target_pairs={{0,2},{1,3},{2,0},{3,1},{4,6},{5,7},{6,4},{7,5},{8,10},{9,11},{10,... | collective-permute-start | bytes 2359304 | tf_op jit(solution)/shard_map/ppermute | solution.py:14
  249.1 6.9 %copy-start.1 = (bf16[128,2048]{1,0:T(8,128)(2,1)S(1)}, bf16[128,2048]{1,0:T(8,128)(2,1)}, u32[]{:S(2)}) copy-start(bf16[128,2048]{1,0:T(8,128)(2,1)} %param.7) | copy-start | bytes 1572868

commit v2 on v1

--- a/solution.py
+++ b/solution.py
@@ -1,7 +1,13 @@
+import functools
+
 import jax
 import jax.numpy as jnp
 from jax import lax
+from jax.experimental import pallas as pl
+from jax.experimental.pallas import tpu as pltpu
 from jax.sharding import PartitionSpec as P
+
+MIB = 1024 * 1024
 
 
 def silu_parts(pre_gate):
@@ -14,17 +20,21 @@
     return lax.ppermute(value, "dp", [(i, i ^ bit) for i in range(count)])
 
 
+def in_order(*parts):
+    me = lax.axis_index("dp")
+    depth = parts[0].shape[0]
+    full = jnp.zeros((4 * depth, parts[0].shape[1]), parts[0].dtype)
+    for bits, part in enumerate(parts):
+        full = lax.dynamic_update_slice(full, part, ((me ^ bits) * depth, 0))
+    return full
+
+
 def gather_rows(shard):
     if lax.axis_size("dp") != 4:
         return lax.all_gather(shard, "dp", axis=0, tiled=True)
-    me = lax.axis_index("dp")
     far = swap(shard, 2)
     near, far_near = swap(shard, 1), swap(far, 1)
-    depth = shard.shape[0]
-    full = jnp.zeros((4 * depth, shard.shape[1]), shard.dtype)
-    for bits, part in ((0, shard), (1, near), (2, far), (3, far_near)):
-        full = lax.dynamic_update_slice(full, part, ((me ^ bits) * depth, 0))
-    return full
+    return in_order(shard, near, far, far_near)
 
 
 def scatter_rows(total):
@@ -104,6 +114,541 @@
     )
 
 
+def after(value, *others):
+    return lax.optimization_barrier((value, *others))[0]
+
+
+def params(mib=20):
+    return pltpu.CompilerParams(vmem_limit_bytes=mib * MIB)
+
+
+def specs(count):
+    return [pl.BlockSpec(memory_space=pltpu.SMEM)] + [pl.BlockSpec(memory_space=pltpu.VMEM)] * count
+
+
+def anywhere(count):
+    return [pl.BlockSpec(memory_space=pl.ANY)] * count
+
+
+def cost(micros):
+    return pl.CostEstimate(flops=int(micros * 1e9), bytes_accessed=0, transcendentals=0)
+
+
+def one_hots(cap, probs):
+    count = probs.shape[1]
+    chosen = (probs > 0.0).astype(jnp.float32)
+    before = lax.broadcasted_iota(jnp.int32, (count, count), 0) < lax.broadcasted_iota(
+        jnp.int32, (count, count), 1
+    )
+    ranks = jnp.dot(
+        jnp.broadcast_to(chosen, (8, count)).astype(jnp.bfloat16),
+        before.astype(jnp.float32).astype(jnp.bfloat16),
+        preferred_element_type=jnp.float32,
+    )[0:1]
+    places = lax.broadcasted_iota(jnp.int32, (cap, count), 0).astype(jnp.float32)
+    return jnp.where(places == ranks, 1.0, 0.0) * chosen
+
+
+def prep_kernel(table_ref, tokens_ref, cots_ref, out_ref):
+    count, width = tokens_ref.shape
+    out_ref[0:count, :] = tokens_ref[...]
+    out_ref[count : 2 * count, :] = cots_ref[...]
+    rest = table_ref[...]
+    terms = []
+    for _ in range(3):
+        term = rest.astype(jnp.bfloat16).astype(jnp.float32)
+        rest = rest - term
+        terms.append(term)
+    owners, cols = table_ref.shape
+    wide = jnp.concatenate(terms + [jnp.zeros((owners, width - 3 * cols), jnp.float32)], axis=1)
+    wide = jnp.concatenate([wide, jnp.zeros((16 - owners, width), jnp.float32)], axis=0)
+    out_ref[2 * count :, :] = wide.astype(jnp.bfloat16)
+
+
+def prep(table, tokens, cots):
+    count, width = tokens.shape
+    return pl.pallas_call(
+        prep_kernel,
+        out_shape=jax.ShapeDtypeStruct((2 * count + 16, width), jnp.bfloat16),
+        in_specs=specs(3)[1:],
+        out_specs=pl.BlockSpec(memory_space=pltpu.VMEM),
+        compiler_params=params(),
+        cost_estimate=cost(2),
+        name="prep",
+    )(table, tokens, cots)
+
+
+def pick_kernel(cap, batch, n_sources, me_ref, *refs):
+    me = me_ref[0]
+    z = me // 2
+    sources = refs[:n_sources]
+    own_ref, other_ref, pair_ref, chunk, sem = refs[n_sources:]
+    width = own_ref.shape[1]
+    count = pair_ref.shape[1]
+    if batch == 0:
+        pltpu.make_async_copy(sources[0], chunk, sem).start()
+    else:
+        levels = {1: (0, 0, 1, 1), 2: (0, 0, 1, 1), 3: (2, 1, 0, 3)}[batch]
+        for level, at in enumerate(levels):
+
+            @pl.when(z == level)
+            def _(at=at):
+                pltpu.make_async_copy(sources[at], chunk, sem).start()
+
+    pltpu.make_async_copy(sources[0], chunk, sem).wait()
+    info = chunk[pl.ds(2 * count, 16), pl.ds(0, 3 * count)].astype(jnp.float32)
+    table = info[:, :count] + info[:, count : 2 * count] + info[:, 2 * count :]
+    places = lax.broadcasted_iota(jnp.int32, table.shape, 0)
+    own = jnp.sum(jnp.where(places == me, table, 0.0), axis=0, keepdims=True)
+    other = jnp.sum(jnp.where(places == (me ^ 1), table, 0.0), axis=0, keepdims=True)
+    places = lax.broadcasted_iota(jnp.int32, pair_ref.shape, 0)
+    pair_ref[...] = jnp.where(places == 0, own, jnp.where(places == 1, other, 0.0))
+    hot_own, hot_other = one_hots(cap, own), one_hots(cap, other)
+    weight = jnp.concatenate(
+        [
+            jnp.sum(hot_own * own, axis=1, keepdims=True),
+            jnp.sum(hot_other * other, axis=1, keepdims=True),
+        ],
+        axis=0,
+    )
+    hot = jnp.concatenate([hot_own, hot_other], axis=0).astype(jnp.bfloat16)
+    step = width // 4
+    for start in range(0, width, step):
+        cols = pl.ds(start, step)
+        rows = jnp.dot(hot, chunk[pl.ds(0, count), cols], preferred_element_type=jnp.float32)
+        cots = jnp.dot(hot, chunk[pl.ds(count, count), cols], preferred_element_type=jnp.float32)
+        cots = cots * weight
+        own_ref[:, cols] = jnp.concatenate([rows[:cap], cots[:cap]], axis=0).astype(jnp.bfloat16)
+        other_ref[:, cols] = jnp.concatenate([rows[cap:], cots[cap:]], axis=0).astype(jnp.bfloat16)
+
+
+def pick(cap, batch, me, sources):
+    height, width = sources[0].shape
+    out = jax.ShapeDtypeStruct((2 * cap, width), jnp.bfloat16)
+    return pl.pallas_call(
+        functools.partial(pick_kernel, cap, batch, len(sources)),
+        out_shape=(out, out, jax.ShapeDtypeStruct((8, (height - 16) // 2), jnp.float32)),
+        in_specs=specs(0) + anywhere(len(sources)),
+        out_specs=(pl.BlockSpec(memory_space=pltpu.VMEM),) * 3,
+        scratch_shapes=[pltpu.VMEM((height, width), jnp.bfloat16), pltpu.SemaphoreType.DMA],
+        compiler_params=params(16),
+        cost_estimate=cost(0),
+        name=f"pick_{batch}",
+    )(me, *sources)
+
+
+def fetch_weights(dp, parts, fulls, sems):
+    waits = []
+    for k, full in enumerate(fulls):
+        depth = full.shape[0] // 4
+        copies = []
+        for bits in range(4):
+            rows = pl.ds(pl.multiple_of((dp ^ bits) * depth, 16), depth)
+            copy = pltpu.make_async_copy(parts[4 * k + bits], full.at[rows, :], sems.at[4 * k + bits])
+            copy.start()
+            copies.append(copy)
+        waits.append(copies)
+    return waits
+
+
+def wait_all(copies):
+    for copy in copies:
+        copy.wait()
+
+
+def join_packs(cap, own_ref, got_ref):
+    own, got = own_ref[...].astype(jnp.float32), got_ref[...].astype(jnp.float32)
+    return (
+        jnp.concatenate([own[:cap], got[:cap]], axis=0).astype(jnp.bfloat16),
+        jnp.concatenate([own[cap:], got[cap:]], axis=0).astype(jnp.bfloat16),
+    )
+
+
+def dot_t(left, right):
+    return lax.dot_general(left, right, (((1,), (1,)), ((), ())), preferred_element_type=jnp.float32)
+
+
+def t_dot(left, right):
+    return lax.dot_general(left, right, (((0,), (0,)), ((), ())), preferred_element_type=jnp.float32)
+
+
+def layer_kernel(cap, count, dp_ref, *refs):
+    packs, parts = refs[: 2 * count], refs[2 * count : 2 * count + 12]
+    own_slots, back_slots, rows_ref, cots_ref, act_ref, dgate_ref, dup_ref = refs[2 * count + 12 : -4]
+    gate_ref, up_ref, down_ref, sems = refs[-4:]
+    waits = fetch_weights(dp_ref[0], parts, (gate_ref, up_ref, down_ref), sems)
+    for b in range(count):
+        span = pl.ds(2 * cap * b, 2 * cap)
+        rows_ref[span, :], cots_ref[span, :] = join_packs(cap, packs[2 * b], packs[2 * b + 1])
+    wait_all(waits[0])
+    wait_all(waits[1])
+    wait_all(waits[2])
+    width, hidden = gate_ref.shape
+    part = hidden // 3
+    for start in range(0, hidden, part):
+        cols = pl.ds(start, part)
+        gate = jnp.dot(rows_ref[...], gate_ref[:, cols], preferred_element_type=jnp.float32)
+        up = jnp.dot(rows_ref[...], up_ref[:, cols], preferred_element_type=jnp.float32)
+        grad = dot_t(cots_ref[...], down_ref[cols, :])
+        value, slope = silu_parts(gate)
+        act_ref[:, cols] = (value * up).astype(jnp.bfloat16)
+        dgate_ref[:, cols] = (grad * up * slope).astype(jnp.bfloat16)
+        dup_ref[:, cols] = (grad * value).astype(jnp.bfloat16)
+    step = width // 4
+    for start in range(0, width, step):
+        cols = pl.ds(start, step)
+        total = dot_t(dgate_ref[...], gate_ref[cols, :]) + dot_t(dup_ref[...], up_ref[cols, :])
+        for first, ref in enumerate((own_slots, back_slots)):
+            slots = [total[b * cap : (b + 1) * cap] for b in range(first, 2 * count, 2)]
+            ref[:, cols] = jnp.concatenate(slots, axis=0).astype(jnp.bfloat16)
+
+
+def weight_scratch(parts):
+    return [pltpu.VMEM((4 * p.shape[0], p.shape[1]), jnp.bfloat16) for p in parts[0::4]]
+
+
+def layer(cap, dp, packs, parts):
+    count = len(packs) // 2
+    width, hidden = packs[0].shape[1], parts[0].shape[1]
+    rows = 2 * cap * count
+    slot = jax.ShapeDtypeStruct((cap * count, width), jnp.bfloat16)
+    wide = jax.ShapeDtypeStruct((rows, width), jnp.bfloat16)
+    thin = jax.ShapeDtypeStruct((rows, hidden), jnp.bfloat16)
+    got = pl.pallas_call(
+        functools.partial(layer_kernel, cap, count),
+        out_shape=(slot, slot, wide, wide, thin, thin, thin),
+        in_specs=specs(len(packs)) + anywhere(12),
+        out_specs=(pl.BlockSpec(memory_space=pltpu.VMEM),) * 7,
+        scratch_shapes=weight_scratch(parts) + [pltpu.SemaphoreType.DMA((12,))],
+        compiler_params=params(60),
+        cost_estimate=cost(0),
+        name="layer",
+    )(dp, *packs, *parts)
+    return got[:2], got[2:]
+
+
+def last_kernel(cap, dp_ref, own_pack, got_pack, *refs):
+    parts, (act_a, cots_a) = refs[:12], refs[12:14]
+    own_slots, back_slots, rows_ref, dgate_ref, dup_ref, far_ref, own_ref, send_ref = refs[14:22]
+    gate_ref, up_ref, down_ref, act_ref, cots_ref, total_ref, short_ref, sems, more = refs[22:]
+    before = act_a.shape[0]
+    waits = fetch_weights(dp_ref[0], parts, (gate_ref, up_ref, down_ref), sems)
+    held = [
+        pltpu.make_async_copy(act_a, act_ref.at[pl.ds(0, before), :], more.at[0]),
+        pltpu.make_async_copy(cots_a, cots_ref.at[pl.ds(0, before), :], more.at[1]),
+    ]
+    for copy in held:
+        copy.start()
+    span = pl.ds(before, 2 * cap)
+    rows_ref[...], cots_ref[span, :] = join_packs(cap, own_pack, got_pack)
+    wait_all(waits[0])
+    gate = jnp.dot(rows_ref[...], gate_ref[...], preferred_element_type=jnp.float32)
+    wait_all(waits[1])
+    up = jnp.dot(rows_ref[...], up_ref[...], preferred_element_type=jnp.float32)
+    value, slope = silu_parts(gate)
+    act_ref[span, :] = (value * up).astype(jnp.bfloat16)
+    wait_all(waits[2])
+    grad = dot_t(cots_ref[span, :], down_ref[...])
+    dgate_ref[...] = (grad * up * slope).astype(jnp.bfloat16)
+    dup_ref[...] = (grad * value).astype(jnp.bfloat16)
+    wait_all(held)
+    width = cots_ref.shape[1]
+    step = width // 4
+    for start in range(0, width, step):
+        cols = pl.ds(start, step)
+        total_ref[:, cols] = t_dot(act_ref[...], cots_ref[:, cols])
+    depth = far_ref.shape[0]
+
+    def block(bits):
+        return total_ref.at[pl.ds(pl.multiple_of((dp_ref[0] ^ bits) * depth, 16), depth), :]
+
+    short_ref[0] = block(3)[...].astype(jnp.bfloat16)
+    short_ref[1] = block(1)[...].astype(jnp.bfloat16)
+    leaving = [
+        pltpu.make_async_copy(short_ref, send_ref, more.at[2]),
+        pltpu.make_async_copy(block(2), far_ref, more.at[3]),
+        pltpu.make_async_copy(block(0), own_ref, more.at[4]),
+    ]
+    for copy in leaving:
+        copy.start()
+    for start in range(0, width, step):
+        cols = pl.ds(start, step)
+        total = dot_t(dgate_ref[...], gate_ref[cols, :]) + dot_t(dup_ref[...], up_ref[cols, :])
+        own_slots[:, cols] = total[:cap].astype(jnp.bfloat16)
+        back_slots[:, cols] = total[cap:].astype(jnp.bfloat16)
+    wait_all(leaving)
+
+
+def last_layer(cap, dp, packs, parts, act, cots):
+    width, hidden = packs[0].shape[1], parts[0].shape[1]
+    rows = 2 * cap
+    all_rows = act.shape[0] + rows
+    slot = jax.ShapeDtypeStruct((cap, width), jnp.bfloat16)
+    wide = jax.ShapeDtypeStruct((rows, width), jnp.bfloat16)
+    thin = jax.ShapeDtypeStruct((rows, hidden), jnp.bfloat16)
+    block = jax.ShapeDtypeStruct((hidden // 4, width), jnp.float32)
+    send = jax.ShapeDtypeStruct((2, hidden // 4, width), jnp.bfloat16)
+    got = pl.pallas_call(
+        functools.partial(last_kernel, cap),
+        out_shape=(slot, slot, wide, thin, thin, block, block, send),
+        in_specs=specs(2) + anywhere(14),
+        out_specs=(pl.BlockSpec(memory_space=pltpu.VMEM),) * 5 + tuple(anywhere(3)),
+        scratch_shapes=weight_scratch(parts)
+        + [
+            pltpu.VMEM((all_rows, hidden), jnp.bfloat16),
+            pltpu.VMEM((all_rows, width), jnp.bfloat16),
+            pltpu.VMEM((hidden, width), jnp.float32),
+            pltpu.VMEM(send.shape, jnp.bfloat16),
+            pltpu.SemaphoreType.DMA((12,)),
+            pltpu.SemaphoreType.DMA((5,)),
+        ],
+        compiler_params=params(40),
+        cost_estimate=cost(0),
+        name="last_layer",
+    )(dp, *packs, *parts, act, cots)
+    return got[:2], got[2:5], got[5:]
+
+
+def outer_kernel(dp_ref, *refs):
+    ins, (far_ref, own_ref, send_ref) = refs[:6], refs[6:9]
+    rows_ref, grads_ref, total_ref, short_ref, sems, more = refs[9:]
+    copies, start = [], 0
+    hidden = ins[2].shape[1]
+    for k, (rows, dgate, dup) in enumerate((ins[0::2], ins[1::2])):
+        span = pl.ds(start, rows.shape[0])
+        start += rows.shape[0]
+        targets = (
+            rows_ref.at[span, :],
+            grads_ref.at[span, pl.ds(0, hidden)],
+            grads_ref.at[span, pl.ds(hidden, hidden)],
+        )
+        for i, (source, target) in enumerate(zip((rows, dgate, dup), targets)):
+            copy = pltpu.make_async_copy(source, target, sems.at[3 * k + i])
+            copy.start()
+            copies.append(copy)
+    wait_all(copies)
+    depth = far_ref.shape[0]
+    leaving = []
+    for i, bits in enumerate((3, 1, 2, 0)):
+        cols = pl.ds(pl.multiple_of((dp_ref[0] ^ bits) * depth, 128), depth)
+        left = rows_ref[:, cols]
+        for first in (0, hidden):
+            part = t_dot(left, grads_ref[:, pl.ds(first, hidden)])
+            if i < 2:
+                short_ref[i, :, pl.ds(first, hidden)] = part.astype(jnp.bfloat16)
+            else:
+                total_ref[i - 2, :, pl.ds(first, hidden)] = part
+        if i < 2:
+            copy = pltpu.make_async_copy(short_ref.at[i], send_ref.at[i], more.at[i])
+        else:
+            copy = pltpu.make_async_copy(total_ref.at[i - 2], (far_ref, own_ref)[i - 2], more.at[i])
+        copy.start()
+        leaving.append(copy)
+    wait_all(leaving)
+
+
+def outer(dp, rows, dgates, dups):
+    depth, hidden = rows[0].shape[1] // 4, dgates[0].shape[1]
+    all_rows = sum(r.shape[0] for r in rows)
+    block = jax.ShapeDtypeStruct((depth, 2 * hidden), jnp.float32)
+    send = jax.ShapeDtypeStruct((2, depth, 2 * hidden), jnp.bfloat16)
+    return pl.pallas_call(
+        outer_kernel,
+        out_shape=(block, block, send),
+        in_specs=specs(0) + anywhere(6),
+        out_specs=tuple(anywhere(3)),
+        scratch_shapes=[
+            pltpu.VMEM((all_rows, rows[0].shape[1]), jnp.bfloat16),
+            pltpu.VMEM((all_rows, 2 * hidden), jnp.bfloat16),
+            pltpu.VMEM((2, depth, 2 * hidden), jnp.float32),
+            pltpu.VMEM(send.shape, jnp.bfloat16),
+            pltpu.SemaphoreType.DMA((6,)),
+            pltpu.SemaphoreType.DMA((4,)),
+        ],
+        compiler_params=params(28),
+        cost_estimate=cost(0),
+        name="outer",
+    )(dp, rows[0], rows[1], dgates[0], dgates[1], dups[0], dups[1])
+
+
+def spread_kernel(cap, count, *refs):
+    pairs, (own_ref, back_ref), outs = refs[:count], refs[count : count + 2], refs[count + 2 :]
+    width = own_ref.shape[1]
+    hots = [
+        [one_hots(cap, pair[row : row + 1, :]).astype(jnp.bfloat16) for row in (0, 1)] for pair in pairs
+    ]
+    step = width // 4
+    for start in range(0, width, step):
+        cols = pl.ds(start, step)
+        slots = [ref[:, cols].astype(jnp.float32) for ref in (own_ref, back_ref)]
+        for b in range(count):
+            total = sum(
+                lax.dot_general(
+                    hot,
+                    part[b * cap : (b + 1) * cap].astype(jnp.bfloat16),
+                    (((0,), (0,)), ((), ())),
+                    preferred_element_type=jnp.float32,
+                )
+                for hot, part in zip(hots[b], slots)
+            )
+            outs[b][:, cols] = total.astype(outs[b].dtype)
+
+
+def spread(cap, pairs, own, back, kinds):
+    tokens, width = pairs[0].shape[1], own.shape[1]
+    out = [jax.ShapeDtypeStruct((tokens, width), kind) for kind in kinds]
+    return pl.pallas_call(
+        functools.partial(spread_kernel, cap, len(pairs)),
+        out_shape=out,
+        in_specs=specs(len(pairs) + 2)[1:],
+        out_specs=[pl.BlockSpec(memory_space=pltpu.VMEM)] * len(out),
+        compiler_params=params(),
+        cost_estimate=cost(0),
+        name=f"spread_{len(pairs)}",
+    )(*pairs, own, back)
+
+
+def pass_kernel(in_ref, out_ref):
+    out_ref[...] = in_ref[...]
+
+
+def pause(value):
+    return pl.pallas_call(
+        pass_kernel,
+        out_shape=jax.ShapeDtypeStruct(value.shape, value.dtype),
+        in_specs=specs(1)[1:],
+        out_specs=pl.BlockSpec(memory_space=pltpu.VMEM),
+        compiler_params=params(),
+        cost_estimate=cost(30),
+        name="pause",
+    )(value)
+
+
+def merge_kernel(far_ref, got_ref, out_ref):
+    out_ref[...] = (far_ref[...] + got_ref[0].astype(jnp.float32)).astype(jnp.bfloat16)
+
+
+def merge(far, got):
+    rows, cols = far.shape
+    part = rows // 4
+    return pl.pallas_call(
+        merge_kernel,
+        out_shape=jax.ShapeDtypeStruct(far.shape, jnp.bfloat16),
+        grid=(4,),
+        in_specs=[
+            pl.BlockSpec((part, cols), lambda i: (i, 0)),
+            pl.BlockSpec((1, part, cols), lambda i: (0, i, 0)),
+        ],
+        out_specs=pl.BlockSpec((part, cols), lambda i: (i, 0)),
+        compiler_params=params(),
+        cost_estimate=cost(0),
+        name="merge",
+    )(far, got)
+
+
+def finish_kernel(own_ref, got_ref, far_ref, *outs):
+    total = own_ref[...] + got_ref[0].astype(jnp.float32) + far_ref[...].astype(jnp.float32)
+    cols = outs[0].shape[1]
+    for i, ref in enumerate(outs):
+        ref[...] = total[:, i * cols : (i + 1) * cols].astype(jnp.bfloat16)
+
+
+def finish(own, got, far, count):
+    rows, cols = own.shape
+    part = rows // 4
+    out = jax.ShapeDtypeStruct((rows, cols // count), jnp.bfloat16)
+    return pl.pallas_call(
+        finish_kernel,
+        out_shape=(out,) * count,
+        grid=(4,),
+        in_specs=[
+            pl.BlockSpec((part, cols), lambda i: (i, 0)),
+            pl.BlockSpec((1, part, cols), lambda i: (1, i, 0)),
+            pl.BlockSpec((part, cols), lambda i: (i, 0)),
+        ],
+        out_specs=(pl.BlockSpec((part, cols // count), lambda i: (i, 0)),) * count,
+        compiler_params=params(),
+        cost_estimate=cost(1),
+        name=f"finish_{count}",
+    )(own, got, far)
+
+
+def grid_shards(tokens, cotangent, expert_ids, gate_probs, w_gate, w_up, w_down):
+    tok_rows, top_count = expert_ids.shape
+    owners = lax.axis_size("expert")
+    cap = (tok_rows * top_count * 9 + 8 * owners - 1) // (8 * owners)
+    me = lax.axis_index("expert").astype(jnp.int32).reshape(1)
+    dp = lax.axis_index("dp").astype(jnp.int32).reshape(1)
+    z = lax.axis_index("expert") // 2
+
+    def along(value, pairs):
+        return lax.ppermute(value, "expert", [(2 * a + x, 2 * b + x) for a, b in pairs for x in (0, 1)])
+
+    def across(value):
+        return lax.ppermute(value, "expert", [(e, e ^ 1) for e in range(owners)])
+
+    upward, downward = [(0, 1), (1, 2), (2, 3)], [(1, 0), (2, 1), (3, 2)]
+    experts = jnp.arange(owners, dtype=jnp.int32)
+    table = jnp.sum(
+        jnp.where(expert_ids.T[None] == experts[:, None, None], gate_probs.T[None], 0.0), axis=1
+    )
+    chunk = prep(table, tokens, cotangent)
+    picked = [pick(cap, 0, me, [chunk])]
+    up_1, down_1 = along(chunk, upward), along(chunk, downward)
+    weights = [w[0] for w in (w_gate, w_up, w_down)]
+    near = [swap(w, 1) for w in weights]
+    up_2 = along(after(up_1, picked[0][2], *near), upward[1:])
+    down_2 = along(after(down_1, picked[0][2], *near), downward[:2])
+    crossed = [across(picked[0][1])]
+    far = [swap(w, 2) for w in weights[:2]]
+    picked.append(pick(cap, 1, after(me, crossed[0]), [down_1, up_1]))
+    far.append(swap(after(weights[2], picked[1][2]), 2))
+    far_near = [swap(w, 1) for w in far]
+    up_3 = along(after(up_2, *far_near[:2]), upward[2:])
+    down_3 = along(after(down_2, *far_near[:2]), downward[:1])
+    crossed.append(across(picked[1][1]))
+    picked.append(pick(cap, 2, after(me, crossed[1]), [down_2, up_2]))
+    crossed.append(across(picked[2][1]))
+    picked.append(pick(cap, 3, after(me, crossed[2]), [down_1, up_1, down_3, up_3]))
+    crossed.append(across(after(picked[3][1], far_near[2])))
+    pairs = [p[2] for p in picked]
+    packs = list(zip((p[0] for p in picked), crossed))
+    parts = [part for group in zip(weights, near, far, far_near) for part in group]
+    slots_a, (rows_a, cots_a, act_a, dgate_a, dup_a) = layer(
+        cap, dp, [p for pack in packs[:3] for p in pack], parts
+    )
+    slots_b, (rows_b, dgate_b, dup_b), down_sums = last_layer(
+        cap, dp, [after(p, slots_a[0]) for p in packs[3]], parts, act_a, cots_a
+    )
+    back_a, back_b = across(slots_a[1]), across(slots_b[1])
+    pairs[0] = pause(after(pairs[0], back_a))
+    far_sum, own_sum, send = down_sums
+    got = swap(send, 1)
+    far_down = merge(after(far_sum, pairs[0]), got)
+    (sum_down,) = finish(own_sum, got, swap(far_down, 2), 1)
+    far_sum, own_sum, send = outer(dp, (rows_a, rows_b), (dgate_a, dgate_b), (dup_a, dup_b))
+    got = swap(send, 1)
+    far_both = merge(after(far_sum, pairs[0]), got)
+    sum_gate, sum_up = finish(own_sum, got, swap(far_both, 2), 2)
+    here, nigh, mid = spread(
+        cap,
+        [after(p, far_both) for p in pairs[:3]],
+        slots_a[0],
+        back_a,
+        (jnp.float32, jnp.bfloat16, jnp.bfloat16),
+    )
+    (last,) = spread(cap, [after(pairs[3], far_both)], slots_b[0], back_b, (jnp.bfloat16,))
+
+    parts = [
+        along(mid, [(a, (a + 2) % 4) for a in range(4)]),
+        along(jnp.where(z >= 2, last, nigh), [(a, (a + 1) % 4) for a in range(4)]),
+        along(jnp.where(z <= 1, last, nigh), [(a, (a + 3) % 4) for a in range(4)]),
+    ]
+    here = after(here, sum_down, sum_gate)
+    grad_tokens = (here + sum(part.astype(jnp.float32) for part in parts)).astype(jnp.bfloat16)
+    return grad_tokens, sum_gate[None], sum_up[None], sum_down[None]
+
+
 def solution(mesh):
     placed = (
         P(("expert", "dp"), None),
@@ -114,8 +659,9 @@
         P("expert", "dp", None),
         P("expert", "dp", None),
     )
+    small = mesh.shape["expert"] == 8 and mesh.shape["dp"] == 4
     return jax.shard_map(
-        shards,
+        grid_shards if small else shards,
         mesh=mesh,
         in_specs=placed,
         out_specs=(

time: 257 us -> 209 us (0.81)
  Pallas kernels: 0 us -> 52.9 us
  matrix products: 40.3 us -> 0 us
  waiting for transfers between devices: 140 us -> 106 us
  local copies, waits for them, and re-layouts: 34.4 us -> 14.7 us
  other arithmetic: 13.7 us -> 1.85 us
  starting transfers between devices: 26.2 us -> 32 us
    pallas_call x0 -> x15, Pallas kernels: none -> 52.9 us  [the longest x1 14.9 us: layer(): pl.pallas_call(functools.partial(layer_kernel, cap, count), out_shape=(sl...]
    ppermute x0 -> x15, waiting for transfers between devices: none -> 46.6 us  [the longest x9 25.8 us: along(): lax.ppermute(value, 'expert', [(2 * a + x, 2 * b + x) for a, b in pairs f...]
    all_to_all x3 -> x0, waiting for transfers between devices: 45.9 us -> none  [the longest x1 45.9 us: shards(): lax.all_to_all(send_rows, 'expert', split_axis=0, concat_axis=0, tiled=True)]
    dot_general x8 -> x0, matrix products: 40.3 us -> none  [the longest x1 7.15 us: shards(): jnp.dot(rows.T, grad_pre_gate, preferred_element_type=jnp.float32)]
    ppermute x18 -> x13, waiting for transfers between devices: 94.5 us -> 58.9 us  [swap(): return lax.ppermute(value, 'dp', [(i, i ^ bit) for i in range(count)])]
    ppermute x0 -> x15, starting transfers between devices: none -> 25 us  [the longest x9 17.2 us: along(): lax.ppermute(value, 'expert', [(2 * a + x, 2 * b + x) for a, b in pairs f...]
    all_to_all x3 -> x0, starting transfers between devices: 16.9 us -> none  [the longest x1 7.38 us: shards(): lax.all_to_all(send_rows, 'expert', split_axis=0, concat_axis=0, tiled=True)]
    gather x4 -> x0, local copies, waits for them, and re-layouts: 13.1 us -> none  [the longest x2 6.3 us: shards(): returned[slots].astype(jnp.float32).reshape(tok_rows, top_count, width)]
  transfers between devices with their start and end apart: 21 -> 28, of which waited for: 8 -> 11; matrix products, arithmetic and copies ran while one was open for 17% -> 0% of each run, Pallas kernels for 0% -> 25%
where the time goes in v2:
time: 209 us; the launch traced here: 208 us
  waiting for transfers between devices  106 us (51%)
  Pallas kernels  52.9 us (25%)
  starting transfers between devices  32 us (15%)
  local copies, waits for them, and re-layouts  14.7 us (7%)
    ppermute x13, waiting for transfers between devices, swap(): return lax.ppermute(value, 'dp', [(i, i ^ bit) for i in range(count)])  58.9 us
    ppermute x9, waiting for transfers between devices, along(): lax.ppermute(value, 'expert', [(2 * a + x, 2 * b + x) for a, b in pairs f...  25.8 us
    ppermute x6, waiting for transfers between devices, across(): return lax.ppermute(value, 'expert', [(e, e ^ 1) for e in range(owners)])  20.9 us
    ppermute x9, starting transfers between devices, along(): lax.ppermute(value, 'expert', [(2 * a + x, 2 * b + x) for a, b in pairs f...  17.2 us
    pallas_call x1, Pallas kernels, layer(): pl.pallas_call(functools.partial(layer_kernel, cap, count), out_shape=(sl...  14.9 us
    unnamed x72, local copies, waits for them, and re-layouts  14.7 us
    pallas_call x1, Pallas kernels, last_layer(): pl.pallas_call(functools.partial(last_kernel, cap), out_shape=(slot, slot...  11.9 us
    ppermute x6, starting transfers between devices, across(): return lax.ppermute(value, 'expert', [(e, e ^ 1) for e in range(owners)])  7.78 us
  transfers between devices with their start and end apart: 28, of which 11 were waited for; matrix products, arithmetic and copies ran while one was open for 0% of the time, Pallas kernels for 25%

profile of v2, /device:TPU:0, one launch (start us, length us, event | category | flops | bytes accessed | tf_op | source)
XLA Modules:
  0.0 208.1 jit_solution(15600559282907661354)
XLA Ops:
  0.6 0.5 collective-permute-start.4
  1.2 0.7 select_reduce_fusion.table_ref
  1.9 1.0 copy-done.33
  3.0 1.0 copy-done.34
  4.0 1.1 prep.1.refs_0_
  5.1 1.3 collective-permute-start.1
  6.4 5.6 %collective-permute-start.2 = (bf16[272,2048]{1,0:T(8,128)(2,1)}, bf16[272,2048]{1,0:T(8,128)(2,1)S(1)}, u32[]{:S(2)}, u32[]{:S(2)}) collective-permute-start(bf16[272,2048]{1,0:T(8,128)(2,1)} %prep.1.refs_0_), channel_id=1, source_target_pairs={{0,8},{4,12},{8,16},{12,20},{16,24},{20,28},{1,9},{5,13},{9,17},{1... | collective-permute-start | bytes 3342344 | tf_op jit(solution)/shard_map/ppermute | solution.py:585
  12.1 2.0 collective-permute-start.10
  14.1 0.9 copy-done.4
  15.0 0.8 collective-permute-start.12
  15.8 1.8 pick_0.1
  17.7 17.3 %collective-permute-done.1.refs_0_ = bf16[272,2048]{1,0:T(8,128)(2,1)S(1)} collective-permute-done((bf16[272,2048]{1,0:T(8,128)(2,1)}, bf16[272,2048]{1,0:T(8,128)(2,1)S(1)}, u32[]{:S(2)}, u32[]{:S(2)}) %collective-permute-start.1) | collective-permute-done | bytes 1114144 | tf_op jit(solution)/shard_map/ppermute | solution.py:585
  35.0 1.3 collective-permute-start.7
  36.3 0.7 collective-permute-start.8
  37.0 1.7 collective-permute-start
  38.8 10.5 %collective-permute-done.12.refs_12_.refs_6_ = bf16[512,768]{1,0:T(8,128)(2,1)} collective-permute-done((bf16[512,768]{1,0:T(8,128)(2,1)}, bf16[512,768]{1,0:T(8,128)(2,1)}, u32[]{:S(2)}, u32[]{:S(2)}) %collective-permute-start.12) | collective-permute-done | bytes 786464 | tf_op jit(solution)/shard_map/ppermute | solution.py:20
  49.3 2.8 %collective-permute-done.refs_1_ = bf16[144,2048]{1,0:T(8,128)(2,1)} collective-permute-done((bf16[144,2048]{1,0:T(8,128)(2,1)S(1)}, bf16[144,2048]{1,0:T(8,128)(2,1)}, u32[]{:S(2)}, u32[]{:S(2)}) %collective-permute-start) | collective-permute-done | bytes 589856 | tf_op jit(solution)/shard_map/ppermute | solution.py:588
  52.1 0.8 pick_1.1
  52.9 0.8 copy-done.27
  53.7 1.4 collective-permute-start.14
  55.0 1.5 collective-permute-start.3
  56.5 6.5 %collective-permute-done.7.refs_0_ = bf16[272,2048]{1,0:T(8,128)(2,1)S(1)} collective-permute-done((bf16[272,2048]{1,0:T(8,128)(2,1)S(1)}, bf16[272,2048]{1,0:T(8,128)(2,1)S(1)}, u32[]{:S(2)}, u32[]{:S(2)}) %collective-permute-start.7) | collective-permute-done | bytes 1114144 | tf_op jit(solution)/shard_map/ppermute | solution.py:585
  63.0 1.3 collective-permute-start.17
  64.3 0.7 collective-permute-start.18
  65.1 7.0 %collective-permute-done.14.refs_16_.refs_10_ = bf16[192,2048]{1,0:T(8,128)(2,1)S(1)} collective-permute-done((bf16[192,2048]{1,0:T(8,128)(2,1)}, bf16[192,2048]{1,0:T(8,128)(2,1)S(1)}, u32[]{:S(2)}, u32[]{:S(2)}) %collective-permute-start.14) | collective-permute-done | bytes 786464 | tf_op jit(solution)/shard_map/ppermute | solution.py:20
  72.1 0.8 pick_2.1
  72.9 0.8 copy-done.30
  73.7 1.0 collective-permute-start.9
  74.7 14.7 %collective-permute-done.9.refs_5_ = bf16[144,2048]{1,0:T(8,128)(2,1)S(1)} collective-permute-done((bf16[144,2048]{1,0:T(8,128)(2,1)S(1)}, bf16[144,2048]{1,0:T(8,128)(2,1)S(1)}, u32[]{:S(2)}, u32[]{:S(2)}) %collective-permute-start.9) | collective-permute-done | bytes 589856 | tf_op jit(solution)/shard_map/ppermute | solution.py:588
  89.4 0.8 collective-permute-done.17.refs_2_
  90.2 1.6 pick_3.1
  91.9 0.8 copy-done.28
  92.7 0.9 copy-done.12
  93.6 1.0 collective-permute-start.19
  94.6 14.9 %layer.1 = (bf16[216,2048]{1,0:T(8,128)(2,1)}, bf16[216,2048]{1,0:T(8,128)(2,1)}, bf16[432,2048]{1,0:T(8,128)(2,1)}, bf16[432,2048]{1,0:T(8,128)(2,1)}, bf16[432...) custom-call(s32[1]{0:T(128)} %bitcast.3.dp_ref, bf16[144,2048]{1,0:T(8,128)(2,1)} %copy-done.26, ...), custom_call_target="tpu_custom_call" | custom-call | tf_op jit(solution)/shard_map/layer/pallas_call | solution.py:317
  109.5 1.1 collective-permute-start.16
  110.7 1.1 copy-done.11
  111.8 1.1 copy-done.13
  113.0 1.1 copy-done.25
  114.0 1.1 copy-done.29
  115.1 11.9 %last_layer.1 = (bf16[72,2048]{1,0:T(8,128)(2,1)S(1)}, bf16[72,2048]{1,0:T(8,128)(2,1)}, bf16[144,2048]{1,0:T(8,128)(2,1)S(1)}, bf16[144,768]{1,0:T(8,128)(2,1)S...) custom-call(s32[1]{0:T(128)} %bitcast.3.dp_ref, ...), custom_call_target="tpu_custom_call" | custom-call | tf_op jit(solution)/shard_map/last_layer/pallas_call | solution.py:391
  127.1 1.1 copy-done.18
  128.2 7.1 %outer.1 = (f32[512,1536]{1,0:T(8,128)S(1)}, f32[512,1536]{1,0:T(8,128)S(1)}, bf16[2,512,1536]{2,1,0:T(8,128)(2,1)S(1)}) custom-call(s32[1]{0:T(128)} %bitcast.3.dp_ref, bf16[432,2048]{1,0:T(8,128)(2,1)S(1)} %copy-done.16, bf16[144,2048]{1,0:T(8,128)(2,1)S(1)} %get-tuple-element.85.refs_1_, bf16[432,768]{1,0:T(8,128)(2,1)S(1)} %copy-done.23, ...), custom_call_target="tpu_custom_call" | custom-call | tf_op jit(solution)/shard_map/outer/pallas_call | solution.py:455
  135.5 0.5 collective-permute-start.21
  136.0 1.1 copy-done.14
  137.1 0.3 copy-done.21
  137.3 6.0 %collective-permute-done.20.got_ref = bf16[2,512,1536]{2,1,0:T(8,128)(2,1)S(1)} collective-permute-done((bf16[2,512,1536]{2,1,0:T(8,128)(2,1)S(1)}, bf16[2,512,1536]{2,1,0:T(8,128)(2,1)S(1)}, u32[]{:S(2)}, u32[]{:S(2)}) %collective-permute-start.20) | collective-permute-done | bytes 3145760 | tf_op jit(solution)/shard_map/ppermute | solution.py:20
  143.4 1.8 merge.2
  145.2 1.0 collective-permute-start.23
  146.2 1.5 collective-permute-start.25
  147.7 1.4 copy-done.19
  149.1 2.2 %merge.3 = bf16[192,2048]{1,0:T(8,128)(2,1)S(1)} custom-call(f32[192,2048]{1,0:T(8,128)S(1)} %copy-done.19, bf16[2,192,2048]{2,1,0:T(8,128)(2,1)} %collective-permute-done.21.got_ref), custom_call_target="tpu_custom_call" | custom-call | tf_op jit(solution)/shard_map/merge/pallas_call | solution.py:534
  151.3 0.6 collective-permute-start.22
  151.9 3.3 %collective-permute-done.25.refs_2_ = bf16[72,2048]{1,0:T(8,128)(2,1)S(1)} collective-permute-done((bf16[72,2048]{1,0:T(8,128)(2,1)}, bf16[72,2048]{1,0:T(8,128)(2,1)S(1)}, u32[]{:S(2)}, u32[]{:S(2)}) %collective-permute-start.25) | collective-permute-done | bytes 294944 | tf_op jit(solution)/shard_map/ppermute | solution.py:588
  155.2 0.6 spread_1.1
  155.8 1.1 spread_3.1
  157.0 3.7 %collective-permute-start.26 = (bf16[128,2048]{1,0:T(8,128)(2,1)S(1)}, bf16[128,2048]{1,0:T(8,128)(2,1)S(1)}, u32[]{:S(2)}, u32[]{:S(2)}) collective-permute-start(bf16[128,2048]{1,0:T(8,128)(2,1)S(1)} %get-tuple-element.112), channel_id=1, source_target_pairs={{0,8},{4,12},{8,16},{12,20},{16,24},{20,28},{24,0},{28,4},{1,9},{5... | collective-permute-start | bytes 1572872 | tf_op jit(solution)/shard_map/ppermute | solution.py:585
  160.7 1.5 collective-permute-start.27
  162.3 1.1 collective-permute-start.24
  163.3 35.4 %collective-permute-done.22.far_ref = bf16[192,2048]{1,0:T(8,128)(2,1)S(1)} collective-permute-done((bf16[192,2048]{1,0:T(8,128)(2,1)S(1)}, bf16[192,2048]{1,0:T(8,128)(2,1)S(1)}, u32[]{:S(2)}, u32[]{:S(2)}) %collective-permute-start.22) | collective-permute-done | bytes 786464 | tf_op jit(solution)/shard_map/ppermute | solution.py:20
  198.7 3.6 %finish_1.1 = bf16[192,2048]{1,0:T(8,128)(2,1)} custom-call(f32[192,2048]{1,0:T(8,128)S(1)} %copy-done.17, bf16[2,192,2048]{2,1,0:T(8,128)(2,1)} %collective-permute-done.21.got_ref, bf16[192,2048]{1,0:T(8,128)(2,1)S(1)} %collective-permute-done.22.far_ref), custom_call_target="tpu_custom_call" | custom-call | flops 1000000000 | tf_op jit(solution)/shard_map/finish_1/pallas_call | solution.py:560
  202.2 3.6 %finish_2.1 = (bf16[512,768]{1,0:T(8,128)(2,1)}, bf16[512,768]{1,0:T(8,128)(2,1)}) custom-call(f32[512,1536]{1,0:T(8,128)S(1)} %copy-done.15, bf16[2,512,1536]{2,1,0:T(8,128)(2,1)S(1)} %collective-permute-done.20.got_ref, bf16[512,1536]{1,0:T(8,128)(2,1)} %collective-permute-done.23.far_ref), custom_call_target="tpu_custom_call" | custom-call | flops 1000000000 | tf_op jit(solution)/shard_map/finish_2/pallas_call | solution.py:560
  205.9 1.2 collective-permute-done.24
  207.1 1.1 add_convert_fusion
  (82 shorter events, 0.5 us)
Async XLA Ops:
  0.6 11.4 %collective-permute-start.4 = (bf16[512,768]{1,0:T(8,128)(2,1)}, bf16[512,768]{1,0:T(8,128)(2,1)S(1)}, u32[]{:S(2)}, u32[]{:S(2)}) collective-permute-start(bf16[512,768]{1,0:T(8,128)(2,1)} %bitcast.10), channel_id=1, source_target_pairs={{0,1},{1,0},{2,3},{3,2},{4,5},{5,4},{6,7},{7,6},{8,9},{9,8},{10,11... | collective-permute-start | bytes 2359304 | tf_op jit(solution)/shard_map/ppermute | solution.py:20
  1.1 13.0 %collective-permute-start.5 = (bf16[512,768]{1,0:T(8,128)(2,1)}, bf16[512,768]{1,0:T(8,128)(2,1)S(1)}, u32[]{:S(2)}, u32[]{:S(2)}) collective-permute-start(bf16[512,768]{1,0:T(8,128)(2,1)} %bitcast.5.refs_10_.refs_4_), channel_id=1, source_target_pairs={{0,1},{1,0},{2,3},{3,2},{4,5},{5,4},{6,7},{7,6},{8,9},{9,8},{10,11... | collective-permute-start | bytes 2359304 | tf_op jit(solution)/shard_map/ppermute | solution.py:20
  1.9 1.0 copy-start.33
  3.0 1.0 copy-start.34
  4.0 8.1 %copy-start = (bf16[1,512,768]{2,1,0:T(8,128)(2,1)S(1)}, bf16[1,512,768]{2,1,0:T(8,128)(2,1)}, u32[]{:S(2)}) copy-start(bf16[1,512,768]{2,1,0:T(8,128)(2,1)} %param.11) | copy-start | bytes 2359300
  5.1 29.9 %collective-permute-start.1 = (bf16[272,2048]{1,0:T(8,128)(2,1)}, bf16[272,2048]{1,0:T(8,128)(2,1)S(1)}, u32[]{:S(2)}, u32[]{:S(2)}) collective-permute-start(bf16[272,2048]{1,0:T(8,128)(2,1)} %prep.1.refs_0_), channel_id=1, source_target_pairs={{8,0},{12,4},{16,8},{20,12},{24,16},{28,20},{9,1},{13,5},{17,9},{2... | collective-permute-start | bytes 3342344 | tf_op jit(solution)/shard_map/ppermute | solution.py:585
  6.4 29.9 %collective-permute-start.2 = (bf16[272,2048]{1,0:T(8,128)(2,1)}, bf16[272,2048]{1,0:T(8,128)(2,1)S(1)}, u32[]{:S(2)}, u32[]{:S(2)}) collective-permute-start(bf16[272,2048]{1,0:T(8,128)(2,1)} %prep.1.refs_0_), channel_id=1, source_target_pairs={{0,8},{4,12},{8,16},{12,20},{16,24},{20,28},{1,9},{5,13},{9,17},{1... | collective-permute-start | bytes 3342344 | tf_op jit(solution)/shard_map/ppermute | solution.py:585
  12.0 5.7 %collective-permute-start.6 = (bf16[192,2048]{1,0:T(8,128)(2,1)}, bf16[192,2048]{1,0:T(8,128)(2,1)}, u32[]{:S(2)}, u32[]{:S(2)}) collective-permute-start(bf16[192,2048]{1,0:T(8,128)(2,1)} %bitcast.6.refs_14_.refs_8_), channel_id=1, source_target_pairs={{0,1},{1,0},{2,3},{3,2},{4,5},{5,4},{6,7},{7,6},{8,9},{9,8},{10,11... | collective-permute-start | bytes 2359304 | tf_op jit(solution)/shard_map/ppermute | solution.py:20
  12.1 2.0 copy-start.2
  12.1 26.7 %collective-permute-start.10 = (bf16[512,768]{1,0:T(8,128)(2,1)S(1)}, bf16[512,768]{1,0:T(8,128)(2,1)}, u32[]{:S(2)}, u32[]{:S(2)}) collective-permute-start(bf16[512,768]{1,0:T(8,128)(2,1)S(1)} %bitcast.12), channel_id=1, source_target_pairs={{0,2},{1,3},{2,0},{3,1},{4,6},{5,7},{6,4},{7,5},{8,10},{9,11},{10,... | collective-permute-start | bytes 2359304 | tf_op jit(solution)/shard_map/ppermute | solution.py:20
  14.1 0.9 copy-start.4
  15.0 34.2 %collective-permute-start.12 = (bf16[512,768]{1,0:T(8,128)(2,1)}, bf16[512,768]{1,0:T(8,128)(2,1)}, u32[]{:S(2)}, u32[]{:S(2)}) collective-permute-start(bf16[512,768]{1,0:T(8,128)(2,1)} %bitcast.5.refs_10_.refs_4_), channel_id=1, source_target_pairs={{0,2},{1,3},{2,0},{3,1},{4,6},{5,7},{6,4},{7,5},{8,10},{9,11},{10,... | collective-permute-start | bytes 2359304 | tf_op jit(solution)/shard_map/ppermute | solution.py:20
  17.7 38.9 %copy-start.26 = (bf16[144,2048]{1,0:T(8,128)(2,1)}, bf16[144,2048]{1,0:T(8,128)(2,1)S(1)}, u32[]{:S(2)}) copy-start(bf16[144,2048]{1,0:T(8,128)(2,1)S(1)} %get-tuple-element.59.refs_0_) | copy-start | bytes 1769476
  35.0 28.0 %collective-permute-start.7 = (bf16[272,2048]{1,0:T(8,128)(2,1)S(1)}, bf16[272,2048]{1,0:T(8,128)(2,1)S(1)}, u32[]{:S(2)}, u32[]{:S(2)}) collective-permute-start(bf16[272,2048]{1,0:T(8,128)(2,1)S(1)} %collective-permute-done.1.refs_0_), channel_id=1, source_target_pairs={{8,0},{12,4},{16,8},{20,12},{9,1},{13,5},{17,9},{21,13},{10,2},{14... | collective-permute-start | bytes 3342344 | tf_op jit(solution)/shard_map/ppermute | solution.py:585
  36.3 28.0 %collective-permute-start.8 = (bf16[272,2048]{1,0:T(8,128)(2,1)S(1)}, bf16[272,2048]{1,0:T(8,128)(2,1)S(1)}, u32[]{:S(2)}, u32[]{:S(2)}) collective-permute-start(bf16[272,2048]{1,0:T(8,128)(2,1)S(1)} %collective-permute-done.2.refs_1_), channel_id=1, source_target_pairs={{8,16},{12,20},{16,24},{20,28},{9,17},{13,21},{17,25},{21,29},{10,... | collective-permute-start | bytes 3342344 | tf_op jit(solution)/shard_map/ppermute | solution.py:585
  37.0 15.1 %collective-permute-start = (bf16[144,2048]{1,0:T(8,128)(2,1)S(1)}, bf16[144,2048]{1,0:T(8,128)(2,1)}, u32[]{:S(2)}, u32[]{:S(2)}) collective-permute-start(bf16[144,2048]{1,0:T(8,128)(2,1)S(1)} %get-tuple-element.60), channel_id=1, source_target_pairs={{0,4},{4,0},{8,12},{12,8},{16,20},{20,16},{24,28},{28,24},{1,5},{5... | collective-permute-start | bytes 1769480 | tf_op jit(solution)/shard_map/ppermute | solution.py:588
  38.8 16.3 %collective-permute-start.11 = (bf16[512,768]{1,0:T(8,128)(2,1)}, bf16[512,768]{1,0:T(8,128)(2,1)S(1)}, u32[]{:S(2)}, u32[]{:S(2)}) collective-permute-start(bf16[512,768]{1,0:T(8,128)(2,1)} %collective-permute-done.10.refs_8_.refs_2_), channel_id=1, source_target_pairs={{0,1},{1,0},{2,3},{3,2},{4,5},{5,4},{6,7},{7,6},{8,9},{9,8},{10,11... | collective-permute-start | bytes 2359304 | tf_op jit(solution)/shard_map/ppermute | solution.py:20
  49.3 7.3 %collective-permute-start.13 = (bf16[512,768]{1,0:T(8,128)(2,1)}, bf16[512,768]{1,0:T(8,128)(2,1)S(1)}, u32[]{:S(2)}, u32[]{:S(2)}) collective-permute-start(bf16[512,768]{1,0:T(8,128)(2,1)} %collective-permute-done.12.refs_12_.refs_6_), channel_id=1, source_target_pairs={{0,1},{1,0},{2,3},{3,2},{4,5},{5,4},{6,7},{7,6},{8,9},{9,8},{10,11... | collective-permute-start | bytes 2359304 | tf_op jit(solution)/shard_map/ppermute | solution.py:20
  52.9 0.8 copy-start.27
  53.7 18.4 %collective-permute-start.14 = (bf16[192,2048]{1,0:T(8,128)(2,1)}, bf16[192,2048]{1,0:T(8,128)(2,1)S(1)}, u32[]{:S(2)}, u32[]{:S(2)}) collective-permute-start(bf16[192,2048]{1,0:T(8,128)(2,1)} %bitcast.6.refs_14_.refs_8_), channel_id=1, source_target_pairs={{0,2},{1,3},{2,0},{3,1},{4,6},{5,7},{6,4},{7,5},{8,10},{9,11},{10,... | collective-permute-start | bytes 2359304 | tf_op jit(solution)/shard_map/ppermute | solution.py:20
  55.0 36.8 %copy-start.6 = (bf16[512,768]{1,0:T(8,128)(2,1)}, bf16[512,768]{1,0:T(8,128)(2,1)S(1)}, u32[]{:S(2)}) copy-start(bf16[512,768]{1,0:T(8,128)(2,1)S(1)} %collective-permute-done.11.refs_9_.refs_3_) | copy-start | bytes 2359300
  55.0 17.1 %collective-permute-start.3 = (bf16[144,2048]{1,0:T(8,128)(2,1)S(1)}, bf16[144,2048]{1,0:T(8,128)(2,1)}, u32[]{:S(2)}, u32[]{:S(2)}) collective-permute-start(bf16[144,2048]{1,0:T(8,128)(2,1)S(1)} %get-tuple-element.63), channel_id=1, source_target_pairs={{0,4},{4,0},{8,12},{12,8},{16,20},{20,16},{24,28},{28,24},{1,5},{5... | collective-permute-start | bytes 1769480 | tf_op jit(solution)/shard_map/ppermute | solution.py:588
  56.5 7.8 %copy-start.8 = (bf16[512,768]{1,0:T(8,128)(2,1)}, bf16[512,768]{1,0:T(8,128)(2,1)S(1)}, u32[]{:S(2)}) copy-start(bf16[512,768]{1,0:T(8,128)(2,1)S(1)} %collective-permute-done.13.refs_13_.refs_7_) | copy-start | bytes 2359300
  63.0 27.2 %collective-permute-start.17 = (bf16[272,2048]{1,0:T(8,128)(2,1)S(1)}, bf16[272,2048]{1,0:T(8,128)(2,1)S(1)}, u32[]{:S(2)}, u32[]{:S(2)}) collective-permute-start(bf16[272,2048]{1,0:T(8,128)(2,1)S(1)} %collective-permute-done.7.refs_0_), channel_id=1, source_target_pairs={{8,0},{12,4},{9,1},{13,5},{10,2},{14,6},{11,3},{15,7}} | collective-permute-start | bytes 3342344 | tf_op jit(solution)/shard_map/ppermute | solution.py:585
  64.3 25.9 %collective-permute-start.18 = (bf16[272,2048]{1,0:T(8,128)(2,1)S(1)}, bf16[272,2048]{1,0:T(8,128)(2,1)S(1)}, u32[]{:S(2)}, u32[]{:S(2)}) collective-permute-start(bf16[272,2048]{1,0:T(8,128)(2,1)S(1)} %collective-permute-done.8.refs_1_), channel_id=1, source_target_pairs={{16,24},{20,28},{17,25},{21,29},{18,26},{22,30},{19,27},{23,31}} | collective-permute-start | bytes 3342344 | tf_op jit(solution)/shard_map/ppermute | solution.py:585
  72.1 19.7 %copy-start.10 = (bf16[192,2048]{1,0:T(8,128)(2,1)}, bf16[192,2048]{1,0:T(8,128)(2,1)S(1)}, u32[]{:S(2)}) copy-start(bf16[192,2048]{1,0:T(8,128)(2,1)S(1)} %collective-permute-done.14.refs_16_.refs_10_) | copy-start | bytes 2359300
  72.1 20.6 %collective-permute-start.15 = (bf16[192,2048]{1,0:T(8,128)(2,1)S(1)}, bf16[192,2048]{1,0:T(8,128)(2,1)S(1)}, u32[]{:S(2)}, u32[]{:S(2)}) collective-permute-start(bf16[192,2048]{1,0:T(8,128)(2,1)S(1)} %collective-permute-done.14.refs_16_.refs_10_), channel_id=1, source_target_pairs={{0,1},{1,0},{2,3},{3,2},{4,5},{5,4},{6,7},{7,6},{8,9},{9,8},{10,11... | collective-permute-start | bytes 2359304 | tf_op jit(solution)/shard_map/ppermute | solution.py:20
  72.9 0.8 copy-start.30
  73.7 15.7 %collective-permute-start.9 = (bf16[144,2048]{1,0:T(8,128)(2,1)S(1)}, bf16[144,2048]{1,0:T(8,128)(2,1)S(1)}, u32[]{:S(2)}, u32[]{:S(2)}) collective-permute-start(bf16[144,2048]{1,0:T(8,128)(2,1)S(1)} %get-tuple-element.68), channel_id=1, source_target_pairs={{0,4},{4,0},{8,12},{12,8},{16,20},{20,16},{24,28},{28,24},{1,5},{5... | collective-permute-start | bytes 1769480 | tf_op jit(solution)/shard_map/ppermute | solution.py:588
  89.4 2.4 %copy-start.35 = (bf16[144,2048]{1,0:T(8,128)(2,1)}, bf16[144,2048]{1,0:T(8,128)(2,1)S(1)}, u32[]{:S(2)}) copy-start(bf16[144,2048]{1,0:T(8,128)(2,1)S(1)} %collective-permute-done.9.refs_5_) | copy-start | bytes 1769476
  91.8 0.8 copy-start.28
  92.7 0.9 copy-start.12
  93.6 17.0 %collective-permute-start.19 = (bf16[144,2048]{1,0:T(8,128)(2,1)}, bf16[144,2048]{1,0:T(8,128)(2,1)}, u32[]{:S(2)}, u32[]{:S(2)}) collective-permute-start(bf16[144,2048]{1,0:T(8,128)(2,1)} %get-tuple-element.81), channel_id=1, source_target_pairs={{0,4},{4,0},{8,12},{12,8},{16,20},{20,16},{24,28},{28,24},{1,5},{5... | collective-permute-start | bytes 1769480 | tf_op jit(solution)/shard_map/ppermute | solution.py:588
  94.6 16.1 %copy-start.1 = (bf16[1,512,768]{2,1,0:T(8,128)(2,1)S(1)}, bf16[1,512,768]{2,1,0:T(8,128)(2,1)}, u32[]{:S(2)}) copy-start(bf16[1,512,768]{2,1,0:T(8,128)(2,1)} %param.11) | copy-start | bytes 2359300
  94.6 16.1 %copy-start.3 = (bf16[512,768]{1,0:T(8,128)(2,1)S(1)}, bf16[512,768]{1,0:T(8,128)(2,1)}, u32[]{:S(2)}) copy-start(bf16[512,768]{1,0:T(8,128)(2,1)} %copy-done.2) | copy-start | bytes 2359300
  94.6 16.1 %copy-start.5 = (bf16[512,768]{1,0:T(8,128)(2,1)S(1)}, bf16[512,768]{1,0:T(8,128)(2,1)}, u32[]{:S(2)}) copy-start(bf16[512,768]{1,0:T(8,128)(2,1)} %copy-done.4) | copy-start | bytes 2359300
  94.6 16.1 %copy-start.7 = (bf16[512,768]{1,0:T(8,128)(2,1)S(1)}, bf16[512,768]{1,0:T(8,128)(2,1)}, u32[]{:S(2)}) copy-start(bf16[512,768]{1,0:T(8,128)(2,1)} %copy-done.6) | copy-start | bytes 2359300
  94.6 16.1 %copy-start.9 = (bf16[512,768]{1,0:T(8,128)(2,1)S(1)}, bf16[512,768]{1,0:T(8,128)(2,1)}, u32[]{:S(2)}) copy-start(bf16[512,768]{1,0:T(8,128)(2,1)} %copy-done.8) | copy-start | bytes 2359300
  109.5 25.9 %collective-permute-start.16 = (bf16[216,2048]{1,0:T(8,128)(2,1)}, bf16[216,2048]{1,0:T(8,128)(2,1)S(1)}, u32[]{:S(2)}, u32[]{:S(2)}) collective-permute-start(bf16[216,2048]{1,0:T(8,128)(2,1)} %get-tuple-element.71), channel_id=1, source_target_pairs={{0,4},{4,0},{8,12},{12,8},{16,20},{20,16},{24,28},{28,24},{1,5},{5... | collective-permute-start | bytes 2654216 | tf_op jit(solution)/shard_map/ppermute | solution.py:588
  110.7 1.1 copy-start.11
  111.8 1.1 copy-start.13
  113.0 1.1 copy-start.25
  114.0 1.1 copy-start.29
  115.1 13.1 %copy-start.16 = (bf16[432,2048]{1,0:T(8,128)(2,1)S(1)}, bf16[432,2048]{1,0:T(8,128)(2,1)}, u32[]{:S(2)}) copy-start(bf16[432,2048]{1,0:T(8,128)(2,1)} %get-tuple-element.73.refs_0_) | copy-start | bytes 5308420
  115.1 13.1 %copy-start.23 = (bf16[432,768]{1,0:T(8,128)(2,1)S(1)}, bf16[432,768]{1,0:T(8,128)(2,1)}, u32[]{:S(2)}) copy-start(bf16[432,768]{1,0:T(8,128)(2,1)} %get-tuple-element.86.refs_2_) | copy-start | bytes 1990660
  115.1 13.1 %copy-start.24 = (bf16[432,768]{1,0:T(8,128)(2,1)S(1)}, bf16[432,768]{1,0:T(8,128)(2,1)}, u32[]{:S(2)}) copy-start(bf16[432,768]{1,0:T(8,128)(2,1)} %get-tuple-element.88.refs_4_) | copy-start | bytes 1990660
  127.1 1.2 copy-start.18
  128.2 7.2 %copy-start.31 = (bf16[72,2048]{1,0:T(8,128)(2,1)}, bf16[72,2048]{1,0:T(8,128)(2,1)S(1)}, u32[]{:S(2)}) copy-start(bf16[72,2048]{1,0:T(8,128)(2,1)S(1)} %get-tuple-element.108.refs_1_) | copy-start | bytes 884740
  135.4 1.7 copy-start.14
  135.4 8.0 %collective-permute-start.20 = (bf16[2,512,1536]{2,1,0:T(8,128)(2,1)S(1)}, bf16[2,512,1536]{2,1,0:T(8,128)(2,1)S(1)}, u32[]{:S(2)}, u32[]{:S(2)}) collective-permute-start(bf16[2,512,1536]{2,1,0:T(8,128)(2,1)S(1)} %get-tuple-element.92), channel_id=1, source_target_pairs={{0,1},{1,0},{2,3},{3,2},{4,5},{5,4},{6,7},{7,6},{8,9},{9,8},{10,11... | collective-permute-start | bytes 9437192 | tf_op jit(solution)/shard_map/ppermute | solution.py:20
  135.5 1.9 copy-start.21
  135.5 12.2 %collective-permute-start.21 = (bf16[2,192,2048]{2,1,0:T(8,128)(2,1)}, bf16[2,192,2048]{2,1,0:T(8,128)(2,1)}, u32[]{:S(2)}, u32[]{:S(2)}) collective-permute-start(bf16[2,192,2048]{2,1,0:T(8,128)(2,1)} %get-tuple-element.99), channel_id=1, source_target_pairs={{0,1},{1,0},{2,3},{3,2},{4,5},{5,4},{6,7},{7,6},{8,9},{9,8},{10,11... | collective-permute-start | bytes 4718600 | tf_op jit(solution)/shard_map/ppermute | solution.py:20
  145.2 57.1 %collective-permute-start.23 = (bf16[512,1536]{1,0:T(8,128)(2,1)}, bf16[512,1536]{1,0:T(8,128)(2,1)}, u32[]{:S(2)}, u32[]{:S(2)}) collective-permute-start(bf16[512,1536]{1,0:T(8,128)(2,1)} %merge.2), channel_id=1, source_target_pairs={{0,2},{1,3},{2,0},{3,1},{4,6},{5,7},{6,4},{7,5},{8,10},{9,11},{10,... | collective-permute-start | bytes 4718600 | tf_op jit(solution)/shard_map/ppermute | solution.py:20
  146.2 9.0 %collective-permute-start.25 = (bf16[72,2048]{1,0:T(8,128)(2,1)}, bf16[72,2048]{1,0:T(8,128)(2,1)S(1)}, u32[]{:S(2)}, u32[]{:S(2)}) collective-permute-start(bf16[72,2048]{1,0:T(8,128)(2,1)} %get-tuple-element.109), channel_id=1, source_target_pairs={{0,4},{4,0},{8,12},{12,8},{16,20},{20,16},{24,28},{28,24},{1,5},{5... | collective-permute-start | bytes 884744 | tf_op jit(solution)/shard_map/ppermute | solution.py:588
  147.7 1.4 copy-start.19
  149.1 6.1 %copy-start.32 = (bf16[72,2048]{1,0:T(8,128)(2,1)S(1)}, bf16[72,2048]{1,0:T(8,128)(2,1)}, u32[]{:S(2)}) copy-start(bf16[72,2048]{1,0:T(8,128)(2,1)} %copy-done.31) | copy-start | bytes 884740
  149.1 6.7 %copy-start.20 = (bf16[216,2048]{1,0:T(8,128)(2,1)S(1)}, bf16[216,2048]{1,0:T(8,128)(2,1)}, u32[]{:S(2)}) copy-start(bf16[216,2048]{1,0:T(8,128)(2,1)} %get-tuple-element.78.refs_3_) | copy-start | bytes 2654212
  149.1 6.7 %copy-start.22 = (bf16[216,2048]{1,0:T(8,128)(2,1)S(1)}, bf16[216,2048]{1,0:T(8,128)(2,1)}, u32[]{:S(2)}) copy-start(bf16[216,2048]{1,0:T(8,128)(2,1)} %copy-done.21) | copy-start | bytes 2654212
  151.3 47.4 %collective-permute-start.22 = (bf16[192,2048]{1,0:T(8,128)(2,1)S(1)}, bf16[192,2048]{1,0:T(8,128)(2,1)S(1)}, u32[]{:S(2)}, u32[]{:S(2)}) collective-permute-start(bf16[192,2048]{1,0:T(8,128)(2,1)S(1)} %merge.3), channel_id=1, source_target_pairs={{0,2},{1,3},{2,0},{3,1},{4,6},{5,7},{6,4},{7,5},{8,10},{9,11},{10,... | collective-permute-start | bytes 2359304 | tf_op jit(solution)/shard_map/ppermute | solution.py:20
  155.8 42.9 %copy-start.17 = (f32[192,2048]{1,0:T(8,128)S(1)}, f32[192,2048]{1,0:T(8,128)}, u32[]{:S(2)}) copy-start(f32[192,2048]{1,0:T(8,128)} %get-tuple-element.98.own_ref) | copy-start | bytes 4718596
  157.0 48.9 %collective-permute-start.26 = (bf16[128,2048]{1,0:T(8,128)(2,1)S(1)}, bf16[128,2048]{1,0:T(8,128)(2,1)S(1)}, u32[]{:S(2)}, u32[]{:S(2)}) collective-permute-start(bf16[128,2048]{1,0:T(8,128)(2,1)S(1)} %get-tuple-element.112), channel_id=1, source_target_pairs={{0,8},{4,12},{8,16},{12,20},{16,24},{20,28},{24,0},{28,4},{1,9},{5... | collective-permute-start | bytes 1572872 | tf_op jit(solution)/shard_map/ppermute | solution.py:585
  160.7 45.2 %collective-permute-start.27 = (bf16[128,2048]{1,0:T(8,128)(2,1)S(1)}, bf16[128,2048]{1,0:T(8,128)(2,1)S(1)}, u32[]{:S(2)}, u32[]{:S(2)}) collective-permute-start(bf16[128,2048]{1,0:T(8,128)(2,1)S(1)} %get-tuple-element.113), channel_id=1, source_target_pairs={{0,24},{4,28},{8,0},{12,4},{16,8},{20,12},{24,16},{28,20},{1,25},{... | collective-permute-start | bytes 1572872 | tf_op jit(solution)/shard_map/ppermute | solution.py:585
  162.3 44.8 %collective-permute-start.24 = (bf16[128,2048]{1,0:T(8,128)(2,1)S(1)}, bf16[128,2048]{1,0:T(8,128)(2,1)S(1)}, u32[]{:S(2)}, u32[]{:S(2)}) collective-permute-start(bf16[128,2048]{1,0:T(8,128)(2,1)S(1)} %get-tuple-element.105), channel_id=1, source_target_pairs={{0,16},{4,20},{8,24},{12,28},{16,0},{20,4},{24,8},{28,12},{1,17},{... | collective-permute-start | bytes 1572872 | tf_op jit(solution)/shard_map/ppermute | solution.py:585
  198.7 3.6 %copy-start.15 = (f32[512,1536]{1,0:T(8,128)S(1)}, f32[512,1536]{1,0:T(8,128)}, u32[]{:S(2)}) copy-start(f32[512,1536]{1,0:T(8,128)} %copy-done.14) | copy-start | bytes 9437188

commit v3 on v2

--- a/solution.py
+++ b/solution.py
@@ -149,20 +149,27 @@
     return jnp.where(places == ranks, 1.0, 0.0) * chosen
 
 
+def in_terms(table, width):
+    rows, cols = table.shape
+    terms = []
+    for _ in range(3):
+        term = table.astype(jnp.bfloat16).astype(jnp.float32)
+        table = table - term
+        terms.append(term)
+    wide = jnp.concatenate(terms + [jnp.zeros((rows, width - 3 * cols), jnp.float32)], axis=1)
+    return jnp.concatenate([wide, jnp.zeros((16 - rows, width), jnp.float32)], axis=0).astype(jnp.bfloat16)
+
+
+def from_terms(terms, cols):
+    terms = terms.astype(jnp.float32)
+    return terms[0:8, :cols] + terms[0:8, cols : 2 * cols] + terms[0:8, 2 * cols : 3 * cols]
+
+
 def prep_kernel(table_ref, tokens_ref, cots_ref, out_ref):
     count, width = tokens_ref.shape
     out_ref[0:count, :] = tokens_ref[...]
     out_ref[count : 2 * count, :] = cots_ref[...]
-    rest = table_ref[...]
-    terms = []
-    for _ in range(3):
-        term = rest.astype(jnp.bfloat16).astype(jnp.float32)
-        rest = rest - term
-        terms.append(term)
-    owners, cols = table_ref.shape
-    wide = jnp.concatenate(terms + [jnp.zeros((owners, width - 3 * cols), jnp.float32)], axis=1)
-    wide = jnp.concatenate([wide, jnp.zeros((16 - owners, width), jnp.float32)], axis=0)
-    out_ref[2 * count :, :] = wide.astype(jnp.bfloat16)
+    out_ref[2 * count :, :] = in_terms(table_ref[...], width)
 
 
 def prep(table, tokens, cots):
@@ -172,23 +179,42 @@
         out_shape=jax.ShapeDtypeStruct((2 * count + 16, width), jnp.bfloat16),
         in_specs=specs(3)[1:],
         out_specs=pl.BlockSpec(memory_space=pltpu.VMEM),
-        compiler_params=params(),
+        compiler_params=params(60),
         cost_estimate=cost(2),
         name="prep",
     )(table, tokens, cots)
+
+
+def stack_kernel(first_ref, second_ref, out_ref):
+    count = first_ref.shape[0]
+    out_ref[0:count, :] = first_ref[...]
+    out_ref[count:, :] = second_ref[...]
+
+
+def stack(first, second):
+    return pl.pallas_call(
+        stack_kernel,
+        out_shape=jax.ShapeDtypeStruct((2 * first.shape[0], first.shape[1]), first.dtype),
+        in_specs=specs(2)[1:],
+        out_specs=pl.BlockSpec(memory_space=pltpu.VMEM),
+        compiler_params=params(60),
+        cost_estimate=cost(0),
+        name="stack",
+    )(first, second)
 
 
 def pick_kernel(cap, batch, n_sources, me_ref, *refs):
     me = me_ref[0]
     z = me // 2
     sources = refs[:n_sources]
-    own_ref, other_ref, pair_ref, chunk, sem = refs[n_sources:]
+    outs, (chunk, sem) = refs[n_sources:-2], refs[-2:]
+    own_ref, other_ref, pair_ref = outs
     width = own_ref.shape[1]
     count = pair_ref.shape[1]
-    if batch == 0:
+    if n_sources == 1:
         pltpu.make_async_copy(sources[0], chunk, sem).start()
     else:
-        levels = {1: (0, 0, 1, 1), 2: (0, 0, 1, 1), 3: (2, 1, 0, 3)}[batch]
+        levels = (0, 1, 0, 1) if batch == 3 else (0, 0, 1, 1)
         for level, at in enumerate(levels):
 
             @pl.when(z == level)
@@ -196,13 +222,15 @@
                 pltpu.make_async_copy(sources[at], chunk, sem).start()
 
     pltpu.make_async_copy(sources[0], chunk, sem).wait()
-    info = chunk[pl.ds(2 * count, 16), pl.ds(0, 3 * count)].astype(jnp.float32)
-    table = info[:, :count] + info[:, count : 2 * count] + info[:, 2 * count :]
+    table = from_terms(chunk[pl.ds(2 * count, 16), pl.ds(0, 3 * count)], count)
+    expert = me ^ 6 if batch == 4 else me
     places = lax.broadcasted_iota(jnp.int32, table.shape, 0)
-    own = jnp.sum(jnp.where(places == me, table, 0.0), axis=0, keepdims=True)
-    other = jnp.sum(jnp.where(places == (me ^ 1), table, 0.0), axis=0, keepdims=True)
+    own = jnp.sum(jnp.where(places == expert, table, 0.0), axis=0, keepdims=True)
+    other = jnp.sum(jnp.where(places == (expert ^ 1), table, 0.0), axis=0, keepdims=True)
     places = lax.broadcasted_iota(jnp.int32, pair_ref.shape, 0)
     pair_ref[...] = jnp.where(places == 0, own, jnp.where(places == 1, other, 0.0))
+    if batch == 4:
+        own_ref[pl.ds(2 * cap, 16), :] = in_terms(pair_ref[...], width)
     hot_own, hot_other = one_hots(cap, own), one_hots(cap, other)
     weight = jnp.concatenate(
         [
@@ -218,33 +246,37 @@
         rows = jnp.dot(hot, chunk[pl.ds(0, count), cols], preferred_element_type=jnp.float32)
         cots = jnp.dot(hot, chunk[pl.ds(count, count), cols], preferred_element_type=jnp.float32)
         cots = cots * weight
-        own_ref[:, cols] = jnp.concatenate([rows[:cap], cots[:cap]], axis=0).astype(jnp.bfloat16)
+        packed = jnp.concatenate([rows[:cap], cots[:cap]], axis=0)
+        own_ref[pl.ds(0, 2 * cap), cols] = packed.astype(jnp.bfloat16)
         other_ref[:, cols] = jnp.concatenate([rows[cap:], cots[cap:]], axis=0).astype(jnp.bfloat16)
 
 
 def pick(cap, batch, me, sources):
     height, width = sources[0].shape
     out = jax.ShapeDtypeStruct((2 * cap, width), jnp.bfloat16)
+    pair = jax.ShapeDtypeStruct((8, (height - 16) // 2), jnp.float32)
+    own = jax.ShapeDtypeStruct((2 * cap + 16, width), jnp.bfloat16) if batch == 4 else out
     return pl.pallas_call(
         functools.partial(pick_kernel, cap, batch, len(sources)),
-        out_shape=(out, out, jax.ShapeDtypeStruct((8, (height - 16) // 2), jnp.float32)),
+        out_shape=(own, out, pair),
         in_specs=specs(0) + anywhere(len(sources)),
         out_specs=(pl.BlockSpec(memory_space=pltpu.VMEM),) * 3,
         scratch_shapes=[pltpu.VMEM((height, width), jnp.bfloat16), pltpu.SemaphoreType.DMA],
-        compiler_params=params(16),
-        cost_estimate=cost(0),
+        compiler_params=params(20),
+        cost_estimate=cost(4 if batch == 1 else 0),
         name=f"pick_{batch}",
     )(me, *sources)
 
 
-def fetch_weights(dp, parts, fulls, sems):
+def fetch_pair(dp, parts, fulls, sems):
     waits = []
     for k, full in enumerate(fulls):
         depth = full.shape[0] // 4
         copies = []
         for bits in range(4):
             rows = pl.ds(pl.multiple_of((dp ^ bits) * depth, 16), depth)
-            copy = pltpu.make_async_copy(parts[4 * k + bits], full.at[rows, :], sems.at[4 * k + bits])
+            source = parts[bits].at[pl.ds(k * depth, depth), :]
+            copy = pltpu.make_async_copy(source, full.at[rows, :], sems.at[4 * k + bits])
             copy.start()
             copies.append(copy)
         waits.append(copies)
@@ -256,8 +288,8 @@
         copy.wait()
 
 
-def join_packs(cap, own_ref, got_ref):
-    own, got = own_ref[...].astype(jnp.float32), got_ref[...].astype(jnp.float32)
+def join_packs(cap, own, got):
+    own, got = own.astype(jnp.float32), got.astype(jnp.float32)
     return (
         jnp.concatenate([own[:cap], got[:cap]], axis=0).astype(jnp.bfloat16),
         jnp.concatenate([own[cap:], got[cap:]], axis=0).astype(jnp.bfloat16),
@@ -273,27 +305,40 @@
 
 
 def layer_kernel(cap, count, dp_ref, *refs):
-    packs, parts = refs[: 2 * count], refs[2 * count : 2 * count + 12]
-    own_slots, back_slots, rows_ref, cots_ref, act_ref, dgate_ref, dup_ref = refs[2 * count + 12 : -4]
-    gate_ref, up_ref, down_ref, sems = refs[-4:]
-    waits = fetch_weights(dp_ref[0], parts, (gate_ref, up_ref, down_ref), sems)
+    packs, parts = refs[: 2 * count], refs[2 * count : 2 * count + 8]
+    own_slots, back_slots, *outs = refs[2 * count + 8 : 2 * count + 15]
+    gate_ref, up_ref, down_ref, sems, *held, more, pack_ref, pack_sems = refs[2 * count + 15 :]
+    rows_ref, cots_ref, act_ref, dgate_ref, dup_ref = held
+    arriving = [
+        pltpu.make_async_copy(pack, pack_ref.at[i], pack_sems.at[i]) for i, pack in enumerate(packs)
+    ]
+    for copy in arriving:
+        copy.start()
+    leaving = [
+        pltpu.make_async_copy(ref, out, more.at[i]) for i, (ref, out) in enumerate(zip(held, outs))
+    ]
+    waits = fetch_pair(dp_ref[0], parts[:4], (gate_ref, up_ref), sems)
+    waits += fetch_pair(dp_ref[0], parts[4:], (down_ref,), sems.at[pl.ds(8, 4)])
+    wait_all(arriving)
     for b in range(count):
         span = pl.ds(2 * cap * b, 2 * cap)
-        rows_ref[span, :], cots_ref[span, :] = join_packs(cap, packs[2 * b], packs[2 * b + 1])
+        rows_ref[span, :], cots_ref[span, :] = join_packs(cap, pack_ref[2 * b], pack_ref[2 * b + 1])
+    leaving[0].start()
+    leaving[1].start()
     wait_all(waits[0])
+    gate = jnp.dot(rows_ref[...], gate_ref[...], preferred_element_type=jnp.float32)
     wait_all(waits[1])
+    up = jnp.dot(rows_ref[...], up_ref[...], preferred_element_type=jnp.float32)
+    value, slope = silu_parts(gate)
+    act_ref[...] = (value * up).astype(jnp.bfloat16)
+    leaving[2].start()
     wait_all(waits[2])
-    width, hidden = gate_ref.shape
-    part = hidden // 3
-    for start in range(0, hidden, part):
-        cols = pl.ds(start, part)
-        gate = jnp.dot(rows_ref[...], gate_ref[:, cols], preferred_element_type=jnp.float32)
-        up = jnp.dot(rows_ref[...], up_ref[:, cols], preferred_element_type=jnp.float32)
-        grad = dot_t(cots_ref[...], down_ref[cols, :])
-        value, slope = silu_parts(gate)
-        act_ref[:, cols] = (value * up).astype(jnp.bfloat16)
-        dgate_ref[:, cols] = (grad * up * slope).astype(jnp.bfloat16)
-        dup_ref[:, cols] = (grad * value).astype(jnp.bfloat16)
+    grad = dot_t(cots_ref[...], down_ref[...])
+    dgate_ref[...] = (grad * up * slope).astype(jnp.bfloat16)
+    dup_ref[...] = (grad * value).astype(jnp.bfloat16)
+    leaving[3].start()
+    leaving[4].start()
+    width = gate_ref.shape[0]
     step = width // 4
     for start in range(0, width, step):
         cols = pl.ds(start, step)
@@ -301,10 +346,13 @@
         for first, ref in enumerate((own_slots, back_slots)):
             slots = [total[b * cap : (b + 1) * cap] for b in range(first, 2 * count, 2)]
             ref[:, cols] = jnp.concatenate(slots, axis=0).astype(jnp.bfloat16)
+    wait_all(leaving)
 
 
 def weight_scratch(parts):
-    return [pltpu.VMEM((4 * p.shape[0], p.shape[1]), jnp.bfloat16) for p in parts[0::4]]
+    depth, hidden = parts[0].shape
+    half, width = parts[4].shape
+    return [pltpu.VMEM((2 * depth, hidden), jnp.bfloat16)] * 2 + [pltpu.VMEM((4 * half, width), jnp.bfloat16)]
 
 
 def layer(cap, dp, packs, parts):
@@ -317,9 +365,16 @@
     got = pl.pallas_call(
         functools.partial(layer_kernel, cap, count),
         out_shape=(slot, slot, wide, wide, thin, thin, thin),
-        in_specs=specs(len(packs)) + anywhere(12),
-        out_specs=(pl.BlockSpec(memory_space=pltpu.VMEM),) * 7,
-        scratch_shapes=weight_scratch(parts) + [pltpu.SemaphoreType.DMA((12,))],
+        in_specs=specs(0) + anywhere(len(packs) + 8),
+        out_specs=(pl.BlockSpec(memory_space=pltpu.VMEM),) * 2 + tuple(anywhere(5)),
+        scratch_shapes=weight_scratch(parts)
+        + [pltpu.SemaphoreType.DMA((12,))]
+        + [pltpu.VMEM(v.shape, v.dtype) for v in (wide, wide, thin, thin, thin)]
+        + [
+            pltpu.SemaphoreType.DMA((5,)),
+            pltpu.VMEM((len(packs), *packs[0].shape), jnp.bfloat16),
+            pltpu.SemaphoreType.DMA((len(packs),)),
+        ],
         compiler_params=params(60),
         cost_estimate=cost(0),
         name="layer",
@@ -327,21 +382,63 @@
     return got[:2], got[2:]
 
 
-def last_kernel(cap, dp_ref, own_pack, got_pack, *refs):
-    parts, (act_a, cots_a) = refs[:12], refs[12:14]
-    own_slots, back_slots, rows_ref, dgate_ref, dup_ref, far_ref, own_ref, send_ref = refs[14:22]
-    gate_ref, up_ref, down_ref, act_ref, cots_ref, total_ref, short_ref, sems, more = refs[22:]
+def last_kernel(cap, dp_ref, pair_ref, own_pack, got_pack, far_own, far_got, *refs):
+    parts, (act_a, cots_a) = refs[:8], refs[8:10]
+    own_slots, back_slots, rows_ref, dgate_ref, dup_ref, far_ref, own_ref, send_ref = refs[10:18]
+    pair_out = refs[18]
+    gate_ref, up_ref, down_ref, act_ref, cots_ref, total_ref, short_ref, sems, more = refs[19:28]
+    own_ref_3, got_ref_3, pack_sems = refs[28:]
     before = act_a.shape[0]
-    waits = fetch_weights(dp_ref[0], parts, (gate_ref, up_ref, down_ref), sems)
+    middle = (dp_ref[1] == 1) | (dp_ref[1] == 2)
+    near_packs = [
+        pltpu.make_async_copy(own_pack, own_ref_3.at[pl.ds(0, 2 * cap), :], pack_sems.at[0]),
+        pltpu.make_async_copy(got_pack, got_ref_3, pack_sems.at[1]),
+    ]
+    far_packs = [
+        pltpu.make_async_copy(far_own, own_ref_3, pack_sems.at[0]),
+        pltpu.make_async_copy(far_got, got_ref_3, pack_sems.at[1]),
+    ]
+
+    @pl.when(middle)
+    def _():
+        for copy in near_packs:
+            copy.start()
+
+    @pl.when(jnp.logical_not(middle))
+    def _():
+        for copy in far_packs:
+            copy.start()
+
+    waits = fetch_pair(dp_ref[0], parts[:4], (gate_ref, up_ref), sems)
     held = [
         pltpu.make_async_copy(act_a, act_ref.at[pl.ds(0, before), :], more.at[0]),
         pltpu.make_async_copy(cots_a, cots_ref.at[pl.ds(0, before), :], more.at[1]),
     ]
+    span = pl.ds(before, 2 * cap)
+
+    @pl.when(middle)
+    def _():
+        wait_all(near_packs)
+
+    @pl.when(jnp.logical_not(middle))
+    def _():
+        wait_all(far_packs)
+
+    rows_ref[...], cots_ref[span, :] = join_packs(
+        cap,
+        own_ref_3[pl.ds(0, 2 * cap), :],
+        got_ref_3[...],
+    )
+    cols = pair_ref.shape[1]
+    pair_out[...] = jnp.where(
+        middle,
+        pair_ref[...],
+        from_terms(own_ref_3[pl.ds(2 * cap, 16), pl.ds(0, 3 * cols)], cols),
+    )
+    wait_all(waits[0])
+    waits += fetch_pair(dp_ref[0], parts[4:], (down_ref,), sems.at[pl.ds(8, 4)])
     for copy in held:
         copy.start()
-    span = pl.ds(before, 2 * cap)
-    rows_ref[...], cots_ref[span, :] = join_packs(cap, own_pack, got_pack)
-    wait_all(waits[0])
     gate = jnp.dot(rows_ref[...], gate_ref[...], preferred_element_type=jnp.float32)
     wait_all(waits[1])
     up = jnp.dot(rows_ref[...], up_ref[...], preferred_element_type=jnp.float32)
@@ -353,10 +450,11 @@
     dup_ref[...] = (grad * value).astype(jnp.bfloat16)
     wait_all(held)
     width = cots_ref.shape[1]
+    step = act_ref.shape[1] // 3
+    for start in range(0, act_ref.shape[1], step):
+        cols = pl.ds(start, step)
+        total_ref[cols, :] = t_dot(act_ref[:, cols], cots_ref[...])
     step = width // 4
-    for start in range(0, width, step):
-        cols = pl.ds(start, step)
-        total_ref[:, cols] = t_dot(act_ref[...], cots_ref[:, cols])
     depth = far_ref.shape[0]
 
     def block(bits):
@@ -379,7 +477,7 @@
     wait_all(leaving)
 
 
-def last_layer(cap, dp, packs, parts, act, cots):
+def last_layer(cap, dp, pair, packs, parts, act, cots):
     width, hidden = packs[0].shape[1], parts[0].shape[1]
     rows = 2 * cap
     all_rows = act.shape[0] + rows
@@ -388,11 +486,14 @@
     thin = jax.ShapeDtypeStruct((rows, hidden), jnp.bfloat16)
     block = jax.ShapeDtypeStruct((hidden // 4, width), jnp.float32)
     send = jax.ShapeDtypeStruct((2, hidden // 4, width), jnp.bfloat16)
+    pair_out = jax.ShapeDtypeStruct(pair.shape, pair.dtype)
     got = pl.pallas_call(
         functools.partial(last_kernel, cap),
-        out_shape=(slot, slot, wide, thin, thin, block, block, send),
-        in_specs=specs(2) + anywhere(14),
-        out_specs=(pl.BlockSpec(memory_space=pltpu.VMEM),) * 5 + tuple(anywhere(3)),
+        out_shape=(slot, slot, wide, thin, thin, block, block, send, pair_out),
+        in_specs=specs(1) + anywhere(12) + anywhere(2),
+        out_specs=(pl.BlockSpec(memory_space=pltpu.VMEM),) * 5
+        + tuple(anywhere(3))
+        + (pl.BlockSpec(memory_space=pltpu.VMEM),),
         scratch_shapes=weight_scratch(parts)
         + [
             pltpu.VMEM((all_rows, hidden), jnp.bfloat16),
@@ -401,12 +502,15 @@
             pltpu.VMEM(send.shape, jnp.bfloat16),
             pltpu.SemaphoreType.DMA((12,)),
             pltpu.SemaphoreType.DMA((5,)),
+            pltpu.VMEM(packs[2].shape, jnp.bfloat16),
+            pltpu.VMEM(packs[3].shape, jnp.bfloat16),
+            pltpu.SemaphoreType.DMA((2,)),
         ],
-        compiler_params=params(40),
+        compiler_params=params(48),
         cost_estimate=cost(0),
         name="last_layer",
-    )(dp, *packs, *parts, act, cots)
-    return got[:2], got[2:5], got[5:]
+    )(dp, pair, *packs, *parts, act, cots)
+    return got[:2], got[2:5], got[5:8], got[8]
 
 
 def outer_kernel(dp_ref, *refs):
@@ -432,12 +536,11 @@
     for i, bits in enumerate((3, 1, 2, 0)):
         cols = pl.ds(pl.multiple_of((dp_ref[0] ^ bits) * depth, 128), depth)
         left = rows_ref[:, cols]
-        for first in (0, hidden):
-            part = t_dot(left, grads_ref[:, pl.ds(first, hidden)])
-            if i < 2:
-                short_ref[i, :, pl.ds(first, hidden)] = part.astype(jnp.bfloat16)
-            else:
-                total_ref[i - 2, :, pl.ds(first, hidden)] = part
+        part = t_dot(left, grads_ref[...])
+        if i < 2:
+            short_ref[i] = part.astype(jnp.bfloat16)
+        else:
+            total_ref[i - 2] = part
         if i < 2:
             copy = pltpu.make_async_copy(short_ref.at[i], send_ref.at[i], more.at[i])
         else:
@@ -512,14 +615,14 @@
     out_ref[...] = in_ref[...]
 
 
-def pause(value):
+def pause(value, micros):
     return pl.pallas_call(
         pass_kernel,
         out_shape=jax.ShapeDtypeStruct(value.shape, value.dtype),
         in_specs=specs(1)[1:],
         out_specs=pl.BlockSpec(memory_space=pltpu.VMEM),
         compiler_params=params(),
-        cost_estimate=cost(30),
+        cost_estimate=cost(micros),
         name="pause",
     )(value)
 
@@ -530,11 +633,11 @@
 
 def merge(far, got):
     rows, cols = far.shape
-    part = rows // 4
+    part = rows // 2
     return pl.pallas_call(
         merge_kernel,
         out_shape=jax.ShapeDtypeStruct(far.shape, jnp.bfloat16),
-        grid=(4,),
+        grid=(2,),
         in_specs=[
             pl.BlockSpec((part, cols), lambda i: (i, 0)),
             pl.BlockSpec((1, part, cols), lambda i: (0, i, 0)),
@@ -555,12 +658,12 @@
 
 def finish(own, got, far, count):
     rows, cols = own.shape
-    part = rows // 4
+    part = rows // 2
     out = jax.ShapeDtypeStruct((rows, cols // count), jnp.bfloat16)
     return pl.pallas_call(
         finish_kernel,
         out_shape=(out,) * count,
-        grid=(4,),
+        grid=(2,),
         in_specs=[
             pl.BlockSpec((part, cols), lambda i: (i, 0)),
             pl.BlockSpec((1, part, cols), lambda i: (1, i, 0)),
@@ -568,7 +671,7 @@
         ],
         out_specs=(pl.BlockSpec((part, cols // count), lambda i: (i, 0)),) * count,
         compiler_params=params(),
-        cost_estimate=cost(1),
+        cost_estimate=cost(4 if count == 1 else 0),
         name=f"finish_{count}",
     )(own, got, far)
 
@@ -592,53 +695,61 @@
     table = jnp.sum(
         jnp.where(expert_ids.T[None] == experts[:, None, None], gate_probs.T[None], 0.0), axis=1
     )
+    ends = [(0, 3), (3, 0)]
     chunk = prep(table, tokens, cotangent)
-    picked = [pick(cap, 0, me, [chunk])]
+    weights = [stack(w_gate[0], w_up[0]), w_down[0]]
+    near = [swap(w, 1) for w in weights]
     up_1, down_1 = along(chunk, upward), along(chunk, downward)
-    weights = [w[0] for w in (w_gate, w_up, w_down)]
-    near = [swap(w, 1) for w in weights]
-    up_2 = along(after(up_1, picked[0][2], *near), upward[1:])
-    down_2 = along(after(down_1, picked[0][2], *near), downward[:2])
+    picked = [pick(cap, 0, after(me, *near), [chunk])]
+    own_4, other_4, _ = pick(cap, 4, after(me, *near), [chunk])
     crossed = [across(picked[0][1])]
-    far = [swap(w, 2) for w in weights[:2]]
-    picked.append(pick(cap, 1, after(me, crossed[0]), [down_1, up_1]))
-    far.append(swap(after(weights[2], picked[1][2]), 2))
-    far_near = [swap(w, 1) for w in far]
-    up_3 = along(after(up_2, *far_near[:2]), upward[2:])
-    down_3 = along(after(down_2, *far_near[:2]), downward[:1])
-    crossed.append(across(picked[1][1]))
+    crossed_4 = lax.ppermute(other_4, "expert", [(e, e ^ 1) for e in (0, 1, 6, 7)])
+    far = [swap(weights[0], 2)]
+    picked.append(pick(cap, 1, me, [down_1, up_1]))
+    first = [picked[1][2]]
+    down_2 = along(after(down_1, *first), downward[:2])
+    up_2 = along(after(up_1, *first), upward[1:])
+    own_3, other_3, pair_3 = pick(cap, 3, me, [down_1, up_1])
+    crossed.append(across(after(picked[1][1], crossed[0], crossed_4)))
+    far.append(swap(weights[1], 2))
     picked.append(pick(cap, 2, after(me, crossed[1]), [down_2, up_2]))
+    far_near = [swap(after(w, picked[2][2]), 1) for w in far]
     crossed.append(across(picked[2][1]))
-    picked.append(pick(cap, 3, after(me, crossed[2]), [down_1, up_1, down_3, up_3]))
-    crossed.append(across(after(picked[3][1], far_near[2])))
+    crossed_3 = lax.ppermute(
+        after(other_3, picked[2][2]), "expert", [(e, e ^ 1) for e in (2, 3, 4, 5)]
+    )
+    far_own, far_got = (along(after(v, down_2, up_2), ends) for v in (own_4, crossed_4))
     pairs = [p[2] for p in picked]
-    packs = list(zip((p[0] for p in picked), crossed))
     parts = [part for group in zip(weights, near, far, far_near) for part in group]
-    slots_a, (rows_a, cots_a, act_a, dgate_a, dup_a) = layer(
-        cap, dp, [p for pack in packs[:3] for p in pack], parts
-    )
-    slots_b, (rows_b, dgate_b, dup_b), down_sums = last_layer(
-        cap, dp, [after(p, slots_a[0]) for p in packs[3]], parts, act_a, cots_a
-    )
+    packs = [v for p, c in zip(picked, crossed) for v in (p[0], c)]
+    slots_a, (rows_a, cots_a, act_a, dgate_a, dup_a) = layer(cap, dp, packs, parts)
+    packs = [own_3, crossed_3, far_own, far_got]
+    slots_b, (rows_b, dgate_b, dup_b), down_sums, pair_b = last_layer(
+        cap,
+        jnp.concatenate([dp, z.astype(jnp.int32).reshape(1)]),
+        pair_3,
+        [after(p, slots_a[0]) for p in packs],
+        parts,
+        act_a,
+        cots_a,
+    )
+    pairs.append(pair_b)
     back_a, back_b = across(slots_a[1]), across(slots_b[1])
-    pairs[0] = pause(after(pairs[0], back_a))
+    both_sums = outer(dp, (rows_a, rows_b), (dgate_a, dgate_b), (dup_a, dup_b))
+    pairs[0] = pause(after(pairs[0], back_a, both_sums[2]), 8)
     far_sum, own_sum, send = down_sums
     got = swap(send, 1)
     far_down = merge(after(far_sum, pairs[0]), got)
     (sum_down,) = finish(own_sum, got, swap(far_down, 2), 1)
-    far_sum, own_sum, send = outer(dp, (rows_a, rows_b), (dgate_a, dgate_b), (dup_a, dup_b))
+    far_sum, own_sum, send = both_sums
     got = swap(send, 1)
-    far_both = merge(after(far_sum, pairs[0]), got)
-    sum_gate, sum_up = finish(own_sum, got, swap(far_both, 2), 2)
     here, nigh, mid = spread(
-        cap,
-        [after(p, far_both) for p in pairs[:3]],
-        slots_a[0],
-        back_a,
-        (jnp.float32, jnp.bfloat16, jnp.bfloat16),
-    )
-    (last,) = spread(cap, [after(pairs[3], far_both)], slots_b[0], back_b, (jnp.bfloat16,))
-
+        cap, pairs[:3], slots_a[0], back_a, (jnp.float32, jnp.bfloat16, jnp.bfloat16)
+    )
+    pairs[3] = pause(after(pairs[3], back_b, far_down, mid), 30)
+    far_both = merge(after(far_sum, pairs[3]), got)
+    sum_gate, sum_up = finish(after(own_sum, sum_down), got, swap(far_both, 2), 2)
+    (last,) = spread(cap, pairs[3:], slots_b[0], back_b, (jnp.bfloat16,))
     parts = [
         along(mid, [(a, (a + 2) % 4) for a in range(4)]),
         along(jnp.where(z >= 2, last, nigh), [(a, (a + 1) % 4) for a in range(4)]),

time: 209 us -> 197 us (0.943)
  waiting for transfers between devices: 106 us -> 88.4 us
  starting transfers between devices: 32 us -> 39.6 us
  local copies, waits for them, and re-layouts: 14.7 us -> 9.88 us
    ppermute x13 -> x10, waiting for transfers between devices: 58.9 us -> 42.1 us  [swap(): return lax.ppermute(value, 'dp', [(i, i ^ bit) for i in range(count)])]
    ppermute x9, starting transfers between devices: 17.2 us -> 23.4 us  [along(): lax.ppermute(value, 'expert', [(2 * a + x, 2 * b + x) for a, b in pairs f...]
    unnamed x72 -> x60, local copies, waits for them, and re-layouts: 14.7 us -> 9.88 us
    ppermute x0 -> x2, starting transfers between devices: none -> 4.09 us  [the longest x1 3.4 us: grid_shards(): lax.ppermute(other_4, 'expert', [(e, e ^ 1) for e in (0, 1, 6, 7)])]
    pallas_call x1, Pallas kernels: 11.9 us -> 14.4 us  [last_layer(): pl.pallas_call(functools.partial(last_kernel, cap), out_shape=(slot, slot...]
    ppermute x6 -> x5, starting transfers between devices: 7.78 us -> 5.8 us  [across(): return lax.ppermute(value, 'expert', [(e, e ^ 1) for e in range(owners)])]
    ppermute x6 -> x5, waiting for transfers between devices: 20.9 us -> 21.7 us  [across(): return lax.ppermute(value, 'expert', [(e, e ^ 1) for e in range(owners)])]
    ppermute x13 -> x10, starting transfers between devices: 7 us -> 6.34 us  [swap(): return lax.ppermute(value, 'dp', [(i, i ^ bit) for i in range(count)])]
  transfers between devices with their start and end apart: 28 -> 26, of which waited for: 11 -> 9; matrix products, arithmetic and copies ran while one was open for 0% -> 1% of each run, Pallas kernels for 25% -> 26%
where the time goes in v3:
time: 197 us
  waiting for transfers between devices  88.4 us (45%)
  Pallas kernels  54.6 us (28%)
  starting transfers between devices  39.6 us (20%)
  local copies, waits for them, and re-layouts  9.88 us (5%)
  other arithmetic  3.16 us (2%)
    ppermute x10, waiting for transfers between devices, swap(): return lax.ppermute(value, 'dp', [(i, i ^ bit) for i in range(count)])  42.1 us
    ppermute x9, waiting for transfers between devices, along(): lax.ppermute(value, 'expert', [(2 * a + x, 2 * b + x) for a, b in pairs f...  24.5 us
    ppermute x9, starting transfers between devices, along(): lax.ppermute(value, 'expert', [(2 * a + x, 2 * b + x) for a, b in pairs f...  23.4 us
    ppermute x5, waiting for transfers between devices, across(): return lax.ppermute(value, 'expert', [(e, e ^ 1) for e in range(owners)])  21.7 us
    pallas_call x1, Pallas kernels, layer(): pl.pallas_call(functools.partial(layer_kernel, cap, count), out_shape=(sl...  14.6 us
    pallas_call x1, Pallas kernels, last_layer(): pl.pallas_call(functools.partial(last_kernel, cap), out_shape=(slot, slot...  14.4 us
    unnamed x60, local copies, waits for them, and re-layouts  9.88 us
    pallas_call x1, Pallas kernels, outer(): pl.pallas_call(outer_kernel, out_shape=(block, block, send), in_specs=spe...  7.13 us
  transfers between devices with their start and end apart: 26, of which 9 were waited for; matrix products, arithmetic and copies ran while one was open for 1% of the time, Pallas kernels for 26%

profile of v3, /device:TPU:0, one launch (start us, length us, event | category | flops | bytes accessed | tf_op | source)
XLA Modules:
  0.0 196.7 jit_solution(11958497848118793810)
XLA Ops:
  0.7 2.7 %stack.1.refs_6_.refs_0_ = bf16[1024,768]{1,0:T(8,128)(2,1)} custom-call(bf16[512,768]{1,0:T(8,128)(2,1)} %bitcast.15, bf16[512,768]{1,0:T(8,128)(2,1)} %bitcast.16), custom_call_target="tpu_custom_call" | custom-call | tf_op jit(solution)/shard_map/stack/pallas_call | solution.py:195
  3.3 0.5 collective-permute-start
  3.8 0.6 select_reduce_fusion.table_ref
  4.4 2.4 %prep.1.refs_0_ = bf16[272,2048]{1,0:T(8,128)(2,1)} custom-call(f32[8,128]{1,0:T(8,128)} %select_reduce_fusion.table_ref, bf16[128,2048]{1,0:T(8,128)(2,1)} %tokens_ref.1, bf16[128,2048]{1,0:T(8,128)(2,1)} %cots_ref.1), custom_call_target="tpu_custom_call" | custom-call | flops 2000000000 | tf_op jit(solution)/shard_map/prep/pallas_call | solution.py:177
  6.7 4.5 %collective-permute-start.4 = (bf16[272,2048]{1,0:T(8,128)(2,1)}, bf16[272,2048]{1,0:T(8,128)(2,1)S(1)}, u32[]{:S(2)}, u32[]{:S(2)}) collective-permute-start(bf16[272,2048]{1,0:T(8,128)(2,1)} %prep.1.refs_0_), channel_id=1, source_target_pairs={{0,8},{4,12},{8,16},{12,20},{16,24},{20,28},{1,9},{5,13},{9,17},{1... | collective-permute-start | bytes 3342344 | tf_op jit(solution)/shard_map/ppermute | solution.py:688
  11.3 1.3 collective-permute-start.3
  12.6 0.3 collective-permute-start.1
  12.9 1.5 collective-permute-start.10
  14.4 0.7 collective-permute-done.1.refs_11_.refs_5_
  15.1 1.2 copy-done
  16.3 0.7 pick_0.1
  17.1 0.8 copy-done.15
  17.9 1.6 pick_4.1
  19.5 3.4 %collective-permute-start.5 = (bf16[144,2048]{1,0:T(8,128)(2,1)S(1)}, bf16[144,2048]{1,0:T(8,128)(2,1)}, u32[]{:S(2)}, u32[]{:S(2)}) collective-permute-start(bf16[144,2048]{1,0:T(8,128)(2,1)S(1)} %get-tuple-element.68), channel_id=1, source_target_pairs={{0,4},{4,0},{24,28},{28,24},{1,5},{5,1},{25,29},{29,25},{2,6},{6,2... | collective-permute-start | bytes 1769480 | tf_op jit(solution)/shard_map/ppermute | solution.py:706
  22.9 0.6 collective-permute-start.2
  23.5 12.5 %collective-permute-done.4.refs_1_ = bf16[272,2048]{1,0:T(8,128)(2,1)S(1)} collective-permute-done((bf16[272,2048]{1,0:T(8,128)(2,1)}, bf16[272,2048]{1,0:T(8,128)(2,1)S(1)}, u32[]{:S(2)}, u32[]{:S(2)}) %collective-permute-start.4) | collective-permute-done | bytes 1114144 | tf_op jit(solution)/shard_map/ppermute | solution.py:688
  36.0 4.1 %collective-permute-done.3.refs_0_ = bf16[272,2048]{1,0:T(8,128)(2,1)S(1)} collective-permute-done((bf16[272,2048]{1,0:T(8,128)(2,1)}, bf16[272,2048]{1,0:T(8,128)(2,1)S(1)}, u32[]{:S(2)}, u32[]{:S(2)}) %collective-permute-start.3) | collective-permute-done | bytes 1114144 | tf_op jit(solution)/shard_map/ppermute | solution.py:688
  40.1 0.8 pick_1.1
  40.9 0.8 copy-done.16
  41.7 1.3 collective-permute-start.7
  42.9 0.7 collective-permute-start.8
  43.7 5.8 %collective-permute-done.2.refs_1_ = bf16[144,2048]{1,0:T(8,128)(2,1)S(1)} collective-permute-done((bf16[144,2048]{1,0:T(8,128)(2,1)S(1)}, bf16[144,2048]{1,0:T(8,128)(2,1)S(1)}, u32[]{:S(2)}, u32[]{:S(2)}) %collective-permute-start.2) | collective-permute-done | bytes 589856 | tf_op jit(solution)/shard_map/ppermute | solution.py:691
  49.5 1.5 collective-permute-start.6
  51.0 1.5 collective-permute-start.12
  52.5 11.7 %collective-permute-done.6.refs_3_ = bf16[144,2048]{1,0:T(8,128)(2,1)S(1)} collective-permute-done((bf16[144,2048]{1,0:T(8,128)(2,1)S(1)}, bf16[144,2048]{1,0:T(8,128)(2,1)S(1)}, u32[]{:S(2)}, u32[]{:S(2)}) %collective-permute-start.6) | collective-permute-done | bytes 589856 | tf_op jit(solution)/shard_map/ppermute | solution.py:691
  64.2 5.3 %collective-permute-done.7.refs_0_ = bf16[272,2048]{1,0:T(8,128)(2,1)S(1)} collective-permute-done((bf16[272,2048]{1,0:T(8,128)(2,1)S(1)}, bf16[272,2048]{1,0:T(8,128)(2,1)S(1)}, u32[]{:S(2)}, u32[]{:S(2)}) %collective-permute-start.7) | collective-permute-done | bytes 1114144 | tf_op jit(solution)/shard_map/ppermute | solution.py:688
  69.5 0.8 pick_2.1
  70.4 1.6 collective-permute-start.9
  72.0 0.2 collective-permute-start.13
  72.1 6.3 %collective-permute-start.16 = (bf16[160,2048]{1,0:T(8,128)(2,1)}, bf16[160,2048]{1,0:T(8,128)(2,1)}, u32[]{:S(2)}, u32[]{:S(2)}) collective-permute-start(bf16[160,2048]{1,0:T(8,128)(2,1)} %get-tuple-element.89), channel_id=1, source_target_pairs={{0,24},{4,28},{24,0},{28,4},{1,25},{5,29},{25,1},{29,5},{2,26},{6,... | collective-permute-start | bytes 1966088 | tf_op jit(solution)/shard_map/ppermute | solution.py:688
  78.4 1.9 collective-permute-start.17
  80.3 0.8 pick_3.1
  81.1 0.8 copy-done.17
  81.9 4.2 %collective-permute-done.9.refs_5_ = bf16[144,2048]{1,0:T(8,128)(2,1)S(1)} collective-permute-done((bf16[144,2048]{1,0:T(8,128)(2,1)S(1)}, bf16[144,2048]{1,0:T(8,128)(2,1)S(1)}, u32[]{:S(2)}, u32[]{:S(2)}) %collective-permute-start.9) | collective-permute-done | bytes 589856 | tf_op jit(solution)/shard_map/ppermute | solution.py:691
  86.1 0.8 copy-done.27
  87.0 0.7 collective-permute-start.15
  87.7 14.6 %layer.1 = (bf16[216,2048]{1,0:T(8,128)(2,1)}, bf16[216,2048]{1,0:T(8,128)(2,1)}, bf16[432,2048]{1,0:T(8,128)(2,1)}, bf16[432,2048]{1,0:T(8,128)(2,1)}, bf16[432...) custom-call(s32[1]{0:T(128)} %bitcast.6.dp_ref, bf16[144,2048]{1,0:T(8,128)(2,1)} %copy-done.15, ...), custom_call_target="tpu_custom_call" | custom-call | tf_op jit(solution)/shard_map/layer/pallas_call | solution.py:365
  102.3 1.6 collective-permute-start.14
  104.0 2.6 %collective-permute-done.17.far_got = bf16[144,2048]{1,0:T(8,128)(2,1)} collective-permute-done((bf16[144,2048]{1,0:T(8,128)(2,1)}, bf16[144,2048]{1,0:T(8,128)(2,1)}, u32[]{:S(2)}, u32[]{:S(2)}) %collective-permute-start.17) | collective-permute-done | bytes 589856 | tf_op jit(solution)/shard_map/ppermute | solution.py:688
  106.6 1.1 copy-done.14
  107.7 14.4 %last_layer.1 = (bf16[72,2048]{1,0:T(8,128)(2,1)S(1)}, bf16[72,2048]{1,0:T(8,128)(2,1)}, bf16[144,2048]{1,0:T(8,128)(2,1)S(1)}, bf16[144,768]{1,0:T(8,128)(2,1)S...) custom-call(s32[2]{0:T(128)S(1)} %pad_add_fusion.dp_ref, ...), custom_call_target="tpu_custom_call" | custom-call | tf_op jit(solution)/shard_map/last_layer/pallas_call | solution.py:490
  122.2 0.6 collective-permute-start.21
  122.8 7.1 %outer.1 = (f32[512,1536]{1,0:T(8,128)S(1)}, f32[512,1536]{1,0:T(8,128)S(1)}, bf16[2,512,1536]{2,1,0:T(8,128)(2,1)S(1)}) custom-call(s32[1]{0:T(128)} %bitcast.6.dp_ref, bf16[432,2048]{1,0:T(8,128)(2,1)S(1)} %copy-done.5, bf16[144,2048]{1,0:T(8,128)(2,1)S(1)} %get-tuple-element.95.refs_1_, bf16[432,768]{1,0:T(8,128)(2,1)S(1)} %copy-done.12, ...), custom_call_target="tpu_custom_call" | custom-call | tf_op jit(solution)/shard_map/outer/pallas_call | solution.py:558
  129.9 0.2 collective-permute-start.20
  130.2 1.4 copy-done.3
  131.6 0.5 copy-done.11
  132.0 1.1 spread_3.1
  133.2 1.1 merge.2
  134.4 0.5 copy-done.9
  134.9 0.2 copy-done.20
  135.3 0.6 copy-done.21
  135.8 1.3 merge.3
  137.1 1.5 collective-permute-start.22
  138.6 0.5 collective-permute-start.19
  139.1 3.5 %collective-permute-start.23 = (bf16[128,2048]{1,0:T(8,128)(2,1)}, bf16[128,2048]{1,0:T(8,128)(2,1)S(1)}, u32[]{:S(2)}, u32[]{:S(2)}) collective-permute-start(bf16[128,2048]{1,0:T(8,128)(2,1)} %copy-done.24), channel_id=1, source_target_pairs={{0,16},{4,20},{8,24},{12,28},{16,0},{20,4},{24,8},{28,12},{1,17},{... | collective-permute-start | bytes 1572872 | tf_op jit(solution)/shard_map/ppermute | solution.py:688
  142.6 1.0 copy-done.22
  143.6 0.6 spread_1.1
  144.2 1.4 broadcast_select_fusion.1
  145.6 0.7 collective-permute-start.24
  146.3 3.2 %collective-permute-start.25 = (bf16[128,2048]{1,0:T(8,128)(2,1)S(1)}, bf16[128,2048]{1,0:T(8,128)(2,1)S(1)}, u32[]{:S(2)}, u32[]{:S(2)}) collective-permute-start(bf16[128,2048]{1,0:T(8,128)(2,1)S(1)} %get-tuple-element.121), channel_id=1, source_target_pairs={{0,24},{4,28},{8,0},{12,4},{16,8},{20,12},{24,16},{28,20},{1,25},{... | collective-permute-start | bytes 1572872 | tf_op jit(solution)/shard_map/ppermute | solution.py:688
  149.5 41.4 %collective-permute-done.19.far_ref = bf16[192,2048]{1,0:T(8,128)(2,1)} collective-permute-done((bf16[192,2048]{1,0:T(8,128)(2,1)}, bf16[192,2048]{1,0:T(8,128)(2,1)}, u32[]{:S(2)}, u32[]{:S(2)}) %collective-permute-start.19) | collective-permute-done | bytes 786464 | tf_op jit(solution)/shard_map/ppermute | solution.py:20
  190.9 2.2 %finish_1.1 = bf16[192,2048]{1,0:T(8,128)(2,1)} custom-call(f32[192,2048]{1,0:T(8,128)S(1)} %copy-done.23, bf16[2,192,2048]{2,1,0:T(8,128)(2,1)S(1)} %copy-done.7, bf16[192,2048]{1,0:T(8,128)(2,1)} %collective-permute-done.19.far_ref), custom_call_target="tpu_custom_call" | custom-call | flops 4000000000 | tf_op jit(solution)/shard_map/finish_1/pallas_call | solution.py:663
  193.1 2.5 %finish_2.1 = (bf16[512,768]{1,0:T(8,128)(2,1)}, bf16[512,768]{1,0:T(8,128)(2,1)}) custom-call(f32[512,1536]{1,0:T(8,128)S(1)} %copy-done.4, bf16[2,512,1536]{2,1,0:T(8,128)(2,1)S(1)} %collective-permute-done.20.got_ref, bf16[512,1536]{1,0:T(8,128)(2,1)} %collective-permute-done.22.far_ref), custom_call_target="tpu_custom_call" | custom-call | tf_op jit(solution)/shard_map/finish_2/pallas_call | solution.py:663
  195.6 1.1 add_convert_fusion
  (70 shorter events, 0.5 us)
Async XLA Ops:
  0.6 3.1 %copy-start.28 = (f32[128,4]{0,1:T(4,128)S(1)}, f32[128,4]{0,1:T(4,128)}, u32[]{:S(2)}) copy-start(f32[128,4]{0,1:T(4,128)} %param.10) | copy-start | bytes 6148
  0.6 3.1 %copy-start.29 = (s32[128,4]{0,1:T(4,128)S(1)}, s32[128,4]{0,1:T(4,128)}, u32[]{:S(2)}) copy-start(s32[128,4]{0,1:T(4,128)} %param.9) | copy-start | bytes 6148
  3.3 11.8 %collective-permute-start = (bf16[1024,768]{1,0:T(8,128)(2,1)}, bf16[1024,768]{1,0:T(8,128)(2,1)}, u32[]{:S(2)}, u32[]{:S(2)}) collective-permute-start(bf16[1024,768]{1,0:T(8,128)(2,1)} %stack.1.refs_6_.refs_0_), channel_id=1, source_target_pairs={{0,1},{1,0},{2,3},{3,2},{4,5},{5,4},{6,7},{7,6},{8,9},{9,8},{10,11... | collective-permute-start | bytes 4718600 | tf_op jit(solution)/shard_map/ppermute | solution.py:20
  4.4 8.2 %copy-start.1 = (bf16[1,192,2048]{2,1,0:T(8,128)(2,1)S(1)}, bf16[1,192,2048]{2,1,0:T(8,128)(2,1)}, u32[]{:S(2)}) copy-start(bf16[1,192,2048]{2,1,0:T(8,128)(2,1)} %param.13) | copy-start | bytes 2359300
  6.7 29.3 %collective-permute-start.4 = (bf16[272,2048]{1,0:T(8,128)(2,1)}, bf16[272,2048]{1,0:T(8,128)(2,1)S(1)}, u32[]{:S(2)}, u32[]{:S(2)}) collective-permute-start(bf16[272,2048]{1,0:T(8,128)(2,1)} %prep.1.refs_0_), channel_id=1, source_target_pairs={{0,8},{4,12},{8,16},{12,20},{16,24},{20,28},{1,9},{5,13},{9,17},{1... | collective-permute-start | bytes 3342344 | tf_op jit(solution)/shard_map/ppermute | solution.py:688
  11.3 28.8 %collective-permute-start.3 = (bf16[272,2048]{1,0:T(8,128)(2,1)}, bf16[272,2048]{1,0:T(8,128)(2,1)S(1)}, u32[]{:S(2)}, u32[]{:S(2)}) collective-permute-start(bf16[272,2048]{1,0:T(8,128)(2,1)} %prep.1.refs_0_), channel_id=1, source_target_pairs={{8,0},{12,4},{16,8},{20,12},{24,16},{28,20},{9,1},{13,5},{17,9},{2... | collective-permute-start | bytes 3342344 | tf_op jit(solution)/shard_map/ppermute | solution.py:688
  12.6 2.5 %collective-permute-start.1 = (bf16[192,2048]{1,0:T(8,128)(2,1)S(1)}, bf16[192,2048]{1,0:T(8,128)(2,1)}, u32[]{:S(2)}, u32[]{:S(2)}) collective-permute-start(bf16[192,2048]{1,0:T(8,128)(2,1)S(1)} %bitcast.12), channel_id=1, source_target_pairs={{0,1},{1,0},{2,3},{3,2},{4,5},{5,4},{6,7},{7,6},{8,9},{9,8},{10,11... | collective-permute-start | bytes 2359304 | tf_op jit(solution)/shard_map/ppermute | solution.py:20
  12.9 57.4 %collective-permute-start.10 = (bf16[1024,768]{1,0:T(8,128)(2,1)}, bf16[1024,768]{1,0:T(8,128)(2,1)}, u32[]{:S(2)}, u32[]{:S(2)}) collective-permute-start(bf16[1024,768]{1,0:T(8,128)(2,1)} %stack.1.refs_6_.refs_0_), channel_id=1, source_target_pairs={{0,2},{1,3},{2,0},{3,1},{4,6},{5,7},{6,4},{7,5},{8,10},{9,11},{10,... | collective-permute-start | bytes 4718600 | tf_op jit(solution)/shard_map/ppermute | solution.py:20
  15.1 1.2 copy-start
  17.1 0.8 copy-start.15
  19.5 24.2 %collective-permute-start.5 = (bf16[144,2048]{1,0:T(8,128)(2,1)S(1)}, bf16[144,2048]{1,0:T(8,128)(2,1)}, u32[]{:S(2)}, u32[]{:S(2)}) collective-permute-start(bf16[144,2048]{1,0:T(8,128)(2,1)S(1)} %get-tuple-element.68), channel_id=1, source_target_pairs={{0,4},{4,0},{24,28},{28,24},{1,5},{5,1},{25,29},{29,25},{2,6},{6,2... | collective-permute-start | bytes 1769480 | tf_op jit(solution)/shard_map/ppermute | solution.py:706
  22.9 26.6 %collective-permute-start.2 = (bf16[144,2048]{1,0:T(8,128)(2,1)S(1)}, bf16[144,2048]{1,0:T(8,128)(2,1)S(1)}, u32[]{:S(2)}, u32[]{:S(2)}) collective-permute-start(bf16[144,2048]{1,0:T(8,128)(2,1)S(1)} %get-tuple-element.65), channel_id=1, source_target_pairs={{0,4},{4,0},{8,12},{12,8},{16,20},{20,16},{24,28},{28,24},{1,5},{5... | collective-permute-start | bytes 1769480 | tf_op jit(solution)/shard_map/ppermute | solution.py:691
  40.9 0.8 copy-start.16
  41.7 27.9 %collective-permute-start.7 = (bf16[272,2048]{1,0:T(8,128)(2,1)S(1)}, bf16[272,2048]{1,0:T(8,128)(2,1)S(1)}, u32[]{:S(2)}, u32[]{:S(2)}) collective-permute-start(bf16[272,2048]{1,0:T(8,128)(2,1)S(1)} %collective-permute-done.3.refs_0_), channel_id=1, source_target_pairs={{8,0},{12,4},{16,8},{20,12},{9,1},{13,5},{17,9},{21,13},{10,2},{14... | collective-permute-start | bytes 3342344 | tf_op jit(solution)/shard_map/ppermute | solution.py:688
  42.9 26.6 %collective-permute-start.8 = (bf16[272,2048]{1,0:T(8,128)(2,1)S(1)}, bf16[272,2048]{1,0:T(8,128)(2,1)S(1)}, u32[]{:S(2)}, u32[]{:S(2)}) collective-permute-start(bf16[272,2048]{1,0:T(8,128)(2,1)S(1)} %collective-permute-done.4.refs_1_), channel_id=1, source_target_pairs={{8,16},{12,20},{16,24},{20,28},{9,17},{13,21},{17,25},{21,29},{10,... | collective-permute-start | bytes 3342344 | tf_op jit(solution)/shard_map/ppermute | solution.py:688
  49.5 31.6 %copy-start.25 = (bf16[144,2048]{1,0:T(8,128)(2,1)}, bf16[144,2048]{1,0:T(8,128)(2,1)S(1)}, u32[]{:S(2)}) copy-start(bf16[144,2048]{1,0:T(8,128)(2,1)S(1)} %collective-permute-done.2.refs_1_) | copy-start | bytes 1769476
  49.5 14.7 %collective-permute-start.6 = (bf16[144,2048]{1,0:T(8,128)(2,1)S(1)}, bf16[144,2048]{1,0:T(8,128)(2,1)S(1)}, u32[]{:S(2)}, u32[]{:S(2)}) collective-permute-start(bf16[144,2048]{1,0:T(8,128)(2,1)S(1)} %get-tuple-element.69), channel_id=1, source_target_pairs={{0,4},{4,0},{8,12},{12,8},{16,20},{20,16},{24,28},{28,24},{1,5},{5... | collective-permute-start | bytes 1769480 | tf_op jit(solution)/shard_map/ppermute | solution.py:691
  51.0 21.0 %collective-permute-start.12 = (bf16[192,2048]{1,0:T(8,128)(2,1)S(1)}, bf16[192,2048]{1,0:T(8,128)(2,1)}, u32[]{:S(2)}, u32[]{:S(2)}) collective-permute-start(bf16[192,2048]{1,0:T(8,128)(2,1)S(1)} %bitcast.13), channel_id=1, source_target_pairs={{0,2},{1,3},{2,0},{3,1},{4,6},{5,7},{6,4},{7,5},{8,10},{9,11},{10,... | collective-permute-start | bytes 2359304 | tf_op jit(solution)/shard_map/ppermute | solution.py:20
  64.2 5.3 %copy-start.26 = (bf16[144,2048]{1,0:T(8,128)(2,1)}, bf16[144,2048]{1,0:T(8,128)(2,1)S(1)}, u32[]{:S(2)}) copy-start(bf16[144,2048]{1,0:T(8,128)(2,1)S(1)} %collective-permute-done.6.refs_3_) | copy-start | bytes 1769476
  70.3 10.8 %copy-start.19 = (bf16[144,2048]{1,0:T(8,128)(2,1)}, bf16[144,2048]{1,0:T(8,128)(2,1)S(1)}, u32[]{:S(2)}) copy-start(bf16[144,2048]{1,0:T(8,128)(2,1)S(1)} %get-tuple-element.74.refs_4_) | copy-start | bytes 1769476
  70.3 17.4 %collective-permute-start.11 = (bf16[1024,768]{1,0:T(8,128)(2,1)}, bf16[1024,768]{1,0:T(8,128)(2,1)}, u32[]{:S(2)}, u32[]{:S(2)}) collective-permute-start(bf16[1024,768]{1,0:T(8,128)(2,1)} %collective-permute-done.10.refs_8_.refs_2_), channel_id=1, source_target_pairs={{0,1},{1,0},{2,3},{3,2},{4,5},{5,4},{6,7},{7,6},{8,9},{9,8},{10,11... | collective-permute-start | bytes 4718600 | tf_op jit(solution)/shard_map/ppermute | solution.py:20
  70.4 15.7 %collective-permute-start.9 = (bf16[144,2048]{1,0:T(8,128)(2,1)S(1)}, bf16[144,2048]{1,0:T(8,128)(2,1)S(1)}, u32[]{:S(2)}, u32[]{:S(2)}) collective-permute-start(bf16[144,2048]{1,0:T(8,128)(2,1)S(1)} %get-tuple-element.75), channel_id=1, source_target_pairs={{0,4},{4,0},{8,12},{12,8},{16,20},{20,16},{24,28},{28,24},{1,5},{5... | collective-permute-start | bytes 1769480 | tf_op jit(solution)/shard_map/ppermute | solution.py:691
  72.0 15.7 %collective-permute-start.13 = (bf16[192,2048]{1,0:T(8,128)(2,1)}, bf16[192,2048]{1,0:T(8,128)(2,1)}, u32[]{:S(2)}, u32[]{:S(2)}) collective-permute-start(bf16[192,2048]{1,0:T(8,128)(2,1)} %collective-permute-done.12.refs_12_.refs_6_), channel_id=1, source_target_pairs={{0,1},{1,0},{2,3},{3,2},{4,5},{5,4},{6,7},{7,6},{8,9},{9,8},{10,11... | collective-permute-start | bytes 2359304 | tf_op jit(solution)/shard_map/ppermute | solution.py:20
  72.1 34.5 %collective-permute-start.16 = (bf16[160,2048]{1,0:T(8,128)(2,1)}, bf16[160,2048]{1,0:T(8,128)(2,1)}, u32[]{:S(2)}, u32[]{:S(2)}) collective-permute-start(bf16[160,2048]{1,0:T(8,128)(2,1)} %get-tuple-element.89), channel_id=1, source_target_pairs={{0,24},{4,28},{24,0},{28,4},{1,25},{5,29},{25,1},{29,5},{2,26},{6,... | collective-permute-start | bytes 1966088 | tf_op jit(solution)/shard_map/ppermute | solution.py:688
  78.4 28.2 %collective-permute-start.17 = (bf16[144,2048]{1,0:T(8,128)(2,1)}, bf16[144,2048]{1,0:T(8,128)(2,1)}, u32[]{:S(2)}, u32[]{:S(2)}) collective-permute-start(bf16[144,2048]{1,0:T(8,128)(2,1)} %collective-permute-done.5), channel_id=1, source_target_pairs={{0,24},{4,28},{24,0},{28,4},{1,25},{5,29},{25,1},{29,5},{2,26},{6,... | collective-permute-start | bytes 1769480 | tf_op jit(solution)/shard_map/ppermute | solution.py:688
  81.1 0.8 copy-start.17
  86.1 0.8 copy-start.27
  87.0 19.6 %collective-permute-start.15 = (bf16[144,2048]{1,0:T(8,128)(2,1)S(1)}, bf16[144,2048]{1,0:T(8,128)(2,1)S(1)}, u32[]{:S(2)}, u32[]{:S(2)}) collective-permute-start(bf16[144,2048]{1,0:T(8,128)(2,1)S(1)} %get-tuple-element.86), channel_id=1, source_target_pairs={{8,12},{12,8},{16,20},{20,16},{9,13},{13,9},{17,21},{21,17},{10,14... | collective-permute-start | bytes 1769480 | tf_op jit(solution)/shard_map/ppermute | solution.py:718
  87.7 18.9 %copy-start.2 = (bf16[1,192,2048]{2,1,0:T(8,128)(2,1)S(1)}, bf16[1,192,2048]{2,1,0:T(8,128)(2,1)}, u32[]{:S(2)}) copy-start(bf16[1,192,2048]{2,1,0:T(8,128)(2,1)} %param.13) | copy-start | bytes 2359300
  87.7 18.9 %copy-start.18 = (bf16[144,2048]{1,0:T(8,128)(2,1)S(1)}, bf16[144,2048]{1,0:T(8,128)(2,1)}, u32[]{:S(2)}) copy-start(bf16[144,2048]{1,0:T(8,128)(2,1)} %copy-done.17) | copy-start | bytes 1769476
  102.3 27.8 %collective-permute-start.14 = (bf16[216,2048]{1,0:T(8,128)(2,1)}, bf16[216,2048]{1,0:T(8,128)(2,1)S(1)}, u32[]{:S(2)}, u32[]{:S(2)}) collective-permute-start(bf16[216,2048]{1,0:T(8,128)(2,1)} %get-tuple-element.79), channel_id=1, source_target_pairs={{0,4},{4,0},{8,12},{12,8},{16,20},{20,16},{24,28},{28,24},{1,5},{5... | collective-permute-start | bytes 2654216 | tf_op jit(solution)/shard_map/ppermute | solution.py:691
  106.6 1.1 copy-start.14
  107.7 15.1 %copy-start.5 = (bf16[432,2048]{1,0:T(8,128)(2,1)S(1)}, bf16[432,2048]{1,0:T(8,128)(2,1)}, u32[]{:S(2)}) copy-start(bf16[432,2048]{1,0:T(8,128)(2,1)} %get-tuple-element.80.refs_0_) | copy-start | bytes 5308420
  107.7 15.1 %copy-start.12 = (bf16[432,768]{1,0:T(8,128)(2,1)S(1)}, bf16[432,768]{1,0:T(8,128)(2,1)}, u32[]{:S(2)}) copy-start(bf16[432,768]{1,0:T(8,128)(2,1)} %get-tuple-element.96.refs_2_) | copy-start | bytes 1990660
  107.7 15.1 %copy-start.13 = (bf16[432,768]{1,0:T(8,128)(2,1)S(1)}, bf16[432,768]{1,0:T(8,128)(2,1)}, u32[]{:S(2)}) copy-start(bf16[432,768]{1,0:T(8,128)(2,1)} %get-tuple-element.98.refs_4_) | copy-start | bytes 1990660
  122.1 11.1 %collective-permute-start.18 = (bf16[2,192,2048]{2,1,0:T(8,128)(2,1)}, bf16[2,192,2048]{2,1,0:T(8,128)(2,1)S(1)}, u32[]{:S(2)}, u32[]{:S(2)}) collective-permute-start(bf16[2,192,2048]{2,1,0:T(8,128)(2,1)} %get-tuple-element.104), channel_id=1, source_target_pairs={{0,1},{1,0},{2,3},{3,2},{4,5},{5,4},{6,7},{7,6},{8,9},{9,8},{10,11... | collective-permute-start | bytes 4718600 | tf_op jit(solution)/shard_map/ppermute | solution.py:20
  122.2 12.9 %collective-permute-start.21 = (bf16[72,2048]{1,0:T(8,128)(2,1)}, bf16[72,2048]{1,0:T(8,128)(2,1)S(1)}, u32[]{:S(2)}, u32[]{:S(2)}) collective-permute-start(bf16[72,2048]{1,0:T(8,128)(2,1)} %get-tuple-element.111), channel_id=1, source_target_pairs={{0,4},{4,0},{8,12},{12,8},{16,20},{20,16},{24,28},{28,24},{1,5},{5... | collective-permute-start | bytes 884744 | tf_op jit(solution)/shard_map/ppermute | solution.py:691
  129.9 1.6 copy-start.3
  129.9 5.9 %collective-permute-start.20 = (bf16[2,512,1536]{2,1,0:T(8,128)(2,1)S(1)}, bf16[2,512,1536]{2,1,0:T(8,128)(2,1)S(1)}, u32[]{:S(2)}, u32[]{:S(2)}) collective-permute-start(bf16[2,512,1536]{2,1,0:T(8,128)(2,1)S(1)} %get-tuple-element.100), channel_id=1, source_target_pairs={{0,1},{1,0},{2,3},{3,2},{4,5},{5,4},{6,7},{7,6},{8,9},{9,8},{10,11... | collective-permute-start | bytes 9437192 | tf_op jit(solution)/shard_map/ppermute | solution.py:20
  130.2 1.8 copy-start.11
  131.6 1.7 copy-start.8
  133.2 1.7 copy-start.9
  133.2 1.9 copy-start.20
  133.2 2.1 %copy-start.24 = (bf16[128,2048]{1,0:T(8,128)(2,1)}, bf16[128,2048]{1,0:T(8,128)(2,1)S(1)}, u32[]{:S(2)}) copy-start(bf16[128,2048]{1,0:T(8,128)(2,1)S(1)} %get-tuple-element.112) | copy-start | bytes 1572868
  133.2 1.9 copy-start.6
  135.1 0.7 copy-start.21
  137.1 56.0 %collective-permute-start.22 = (bf16[512,1536]{1,0:T(8,128)(2,1)}, bf16[512,1536]{1,0:T(8,128)(2,1)}, u32[]{:S(2)}, u32[]{:S(2)}) collective-permute-start(bf16[512,1536]{1,0:T(8,128)(2,1)} %merge.3), channel_id=1, source_target_pairs={{0,2},{1,3},{2,0},{3,1},{4,6},{5,7},{6,4},{7,5},{8,10},{9,11},{10,... | collective-permute-start | bytes 4718600 | tf_op jit(solution)/shard_map/ppermute | solution.py:20
  138.6 52.3 %collective-permute-start.19 = (bf16[192,2048]{1,0:T(8,128)(2,1)}, bf16[192,2048]{1,0:T(8,128)(2,1)}, u32[]{:S(2)}, u32[]{:S(2)}) collective-permute-start(bf16[192,2048]{1,0:T(8,128)(2,1)} %merge.2), channel_id=1, source_target_pairs={{0,2},{1,3},{2,0},{3,1},{4,6},{5,7},{6,4},{7,5},{8,10},{9,11},{10,... | collective-permute-start | bytes 2359304 | tf_op jit(solution)/shard_map/ppermute | solution.py:20
  139.1 56.5 %collective-permute-start.23 = (bf16[128,2048]{1,0:T(8,128)(2,1)}, bf16[128,2048]{1,0:T(8,128)(2,1)S(1)}, u32[]{:S(2)}, u32[]{:S(2)}) collective-permute-start(bf16[128,2048]{1,0:T(8,128)(2,1)} %copy-done.24), channel_id=1, source_target_pairs={{0,16},{4,20},{8,24},{12,28},{16,0},{20,4},{24,8},{28,12},{1,17},{... | collective-permute-start | bytes 1572872 | tf_op jit(solution)/shard_map/ppermute | solution.py:688
  142.6 1.0 copy-start.22
  143.6 47.3 %copy-start.7 = (bf16[2,192,2048]{2,1,0:T(8,128)(2,1)S(1)}, bf16[2,192,2048]{2,1,0:T(8,128)(2,1)}, u32[]{:S(2)}) copy-start(bf16[2,192,2048]{2,1,0:T(8,128)(2,1)} %copy-done.6) | copy-start | bytes 4718596
  143.6 47.3 %copy-start.23 = (f32[192,2048]{1,0:T(8,128)S(1)}, f32[192,2048]{1,0:T(8,128)}, u32[]{:S(2)}) copy-start(f32[192,2048]{1,0:T(8,128)} %get-tuple-element.103.own_ref) | copy-start | bytes 4718596
  145.6 50.0 %collective-permute-start.24 = (bf16[128,2048]{1,0:T(8,128)(2,1)S(1)}, bf16[128,2048]{1,0:T(8,128)(2,1)S(1)}, u32[]{:S(2)}, u32[]{:S(2)}) collective-permute-start(bf16[128,2048]{1,0:T(8,128)(2,1)S(1)} %get-tuple-element.120), channel_id=1, source_target_pairs={{0,8},{4,12},{8,16},{12,20},{16,24},{20,28},{24,0},{28,4},{1,9},{5... | collective-permute-start | bytes 1572872 | tf_op jit(solution)/shard_map/ppermute | solution.py:688
  146.3 49.4 %collective-permute-start.25 = (bf16[128,2048]{1,0:T(8,128)(2,1)S(1)}, bf16[128,2048]{1,0:T(8,128)(2,1)S(1)}, u32[]{:S(2)}, u32[]{:S(2)}) collective-permute-start(bf16[128,2048]{1,0:T(8,128)(2,1)S(1)} %get-tuple-element.121), channel_id=1, source_target_pairs={{0,24},{4,28},{8,0},{12,4},{16,8},{20,12},{24,16},{28,20},{1,25},{... | collective-permute-start | bytes 1572872 | tf_op jit(solution)/shard_map/ppermute | solution.py:688
  190.9 2.2 %copy-start.4 = (f32[512,1536]{1,0:T(8,128)S(1)}, f32[512,1536]{1,0:T(8,128)}, u32[]{:S(2)}) copy-start(f32[512,1536]{1,0:T(8,128)} %copy-done.3) | copy-start | bytes 9437188
  193.1 2.6 %copy-start.10 = (f32[128,2048]{1,0:T(8,128)S(1)}, f32[128,2048]{1,0:T(8,128)}, u32[]{:S(2)}) copy-start(f32[128,2048]{1,0:T(8,128)} %copy-done.9) | copy-start | bytes 3145732

commit v4 on v3

--- a/solution.py
+++ b/solution.py
@@ -214,7 +214,7 @@
     if n_sources == 1:
         pltpu.make_async_copy(sources[0], chunk, sem).start()
     else:
-        levels = (0, 1, 0, 1) if batch == 3 else (0, 0, 1, 1)
+        levels = {1: (1, 1, 0, 0), 2: (0, 0, 1, 1), 3: (0, 1, 0, 1)}[batch]
         for level, at in enumerate(levels):
 
             @pl.when(z == level)
@@ -263,24 +263,34 @@
         out_specs=(pl.BlockSpec(memory_space=pltpu.VMEM),) * 3,
         scratch_shapes=[pltpu.VMEM((height, width), jnp.bfloat16), pltpu.SemaphoreType.DMA],
         compiler_params=params(20),
-        cost_estimate=cost(4 if batch == 1 else 0),
+        cost_estimate=cost(0),
         name=f"pick_{batch}",
     )(me, *sources)
 
 
-def fetch_pair(dp, parts, fulls, sems):
+def fetch_weights(dp, parts, fulls, sems):
+    gate_0, up_0, gate_1, up_1, both_2, both_3, *down = parts
+    depth = gate_0.shape[0]
+    top, bottom = pl.ds(0, depth), pl.ds(depth, depth)
+    sources = [
+        (gate_0, gate_1, both_2.at[top, :], both_3.at[top, :]),
+        (up_0, up_1, both_2.at[bottom, :], both_3.at[bottom, :]),
+        down,
+    ]
     waits = []
-    for k, full in enumerate(fulls):
+    for k, (blocks, full) in enumerate(zip(sources, fulls)):
         depth = full.shape[0] // 4
         copies = []
-        for bits in range(4):
+        for bits, block in enumerate(blocks):
             rows = pl.ds(pl.multiple_of((dp ^ bits) * depth, 16), depth)
-            source = parts[bits].at[pl.ds(k * depth, depth), :]
-            copy = pltpu.make_async_copy(source, full.at[rows, :], sems.at[4 * k + bits])
-            copy.start()
-            copies.append(copy)
+            copies.append(pltpu.make_async_copy(block, full.at[rows, :], sems.at[4 * k + bits]))
         waits.append(copies)
     return waits
+
+
+def start_all(copies):
+    for copy in copies:
+        copy.start()
 
 
 def wait_all(copies):
@@ -305,9 +315,9 @@
 
 
 def layer_kernel(cap, count, dp_ref, *refs):
-    packs, parts = refs[: 2 * count], refs[2 * count : 2 * count + 8]
-    own_slots, back_slots, *outs = refs[2 * count + 8 : 2 * count + 15]
-    gate_ref, up_ref, down_ref, sems, *held, more, pack_ref, pack_sems = refs[2 * count + 15 :]
+    packs, parts = refs[: 2 * count], refs[2 * count : 2 * count + 10]
+    own_slots, back_slots, *outs = refs[2 * count + 10 : 2 * count + 17]
+    gate_ref, up_ref, down_ref, sems, *held, more, pack_ref, pack_sems = refs[2 * count + 17 :]
     rows_ref, cots_ref, act_ref, dgate_ref, dup_ref = held
     arriving = [
         pltpu.make_async_copy(pack, pack_ref.at[i], pack_sems.at[i]) for i, pack in enumerate(packs)
@@ -317,8 +327,9 @@
     leaving = [
         pltpu.make_async_copy(ref, out, more.at[i]) for i, (ref, out) in enumerate(zip(held, outs))
     ]
-    waits = fetch_pair(dp_ref[0], parts[:4], (gate_ref, up_ref), sems)
-    waits += fetch_pair(dp_ref[0], parts[4:], (down_ref,), sems.at[pl.ds(8, 4)])
+    waits = fetch_weights(dp_ref[0], parts, (gate_ref, up_ref, down_ref), sems)
+    for copies in waits:
+        start_all(copies)
     wait_all(arriving)
     for b in range(count):
         span = pl.ds(2 * cap * b, 2 * cap)
@@ -351,8 +362,8 @@
 
 def weight_scratch(parts):
     depth, hidden = parts[0].shape
-    half, width = parts[4].shape
-    return [pltpu.VMEM((2 * depth, hidden), jnp.bfloat16)] * 2 + [pltpu.VMEM((4 * half, width), jnp.bfloat16)]
+    half, width = parts[6].shape
+    return [pltpu.VMEM((4 * depth, hidden), jnp.bfloat16)] * 2 + [pltpu.VMEM((4 * half, width), jnp.bfloat16)]
 
 
 def layer(cap, dp, packs, parts):
@@ -365,7 +376,7 @@
     got = pl.pallas_call(
         functools.partial(layer_kernel, cap, count),
         out_shape=(slot, slot, wide, wide, thin, thin, thin),
-        in_specs=specs(0) + anywhere(len(packs) + 8),
+        in_specs=specs(0) + anywhere(len(packs) + 10),
         out_specs=(pl.BlockSpec(memory_space=pltpu.VMEM),) * 2 + tuple(anywhere(5)),
         scratch_shapes=weight_scratch(parts)
         + [pltpu.SemaphoreType.DMA((12,))]
@@ -383,11 +394,11 @@
 
 
 def last_kernel(cap, dp_ref, pair_ref, own_pack, got_pack, far_own, far_got, *refs):
-    parts, (act_a, cots_a) = refs[:8], refs[8:10]
-    own_slots, back_slots, rows_ref, dgate_ref, dup_ref, far_ref, own_ref, send_ref = refs[10:18]
-    pair_out = refs[18]
-    gate_ref, up_ref, down_ref, act_ref, cots_ref, total_ref, short_ref, sems, more = refs[19:28]
-    own_ref_3, got_ref_3, pack_sems = refs[28:]
+    parts, (act_a, cots_a) = refs[:10], refs[10:12]
+    own_slots, back_slots, rows_ref, dgate_ref, dup_ref, far_ref, own_ref, send_ref = refs[12:20]
+    pair_out = refs[20]
+    gate_ref, up_ref, down_ref, act_ref, cots_ref, total_ref, short_ref, sems, more = refs[21:30]
+    own_ref_3, got_ref_3, pack_sems = refs[30:]
     before = act_a.shape[0]
     middle = (dp_ref[1] == 1) | (dp_ref[1] == 2)
     near_packs = [
@@ -409,7 +420,9 @@
         for copy in far_packs:
             copy.start()
 
-    waits = fetch_pair(dp_ref[0], parts[:4], (gate_ref, up_ref), sems)
+    waits = fetch_weights(dp_ref[0], parts, (gate_ref, up_ref, down_ref), sems)
+    start_all(waits[0])
+    start_all(waits[1])
     held = [
         pltpu.make_async_copy(act_a, act_ref.at[pl.ds(0, before), :], more.at[0]),
         pltpu.make_async_copy(cots_a, cots_ref.at[pl.ds(0, before), :], more.at[1]),
@@ -436,7 +449,7 @@
         from_terms(own_ref_3[pl.ds(2 * cap, 16), pl.ds(0, 3 * cols)], cols),
     )
     wait_all(waits[0])
-    waits += fetch_pair(dp_ref[0], parts[4:], (down_ref,), sems.at[pl.ds(8, 4)])
+    start_all(waits[2])
     for copy in held:
         copy.start()
     gate = jnp.dot(rows_ref[...], gate_ref[...], preferred_element_type=jnp.float32)
@@ -490,7 +503,7 @@
     got = pl.pallas_call(
         functools.partial(last_kernel, cap),
         out_shape=(slot, slot, wide, thin, thin, block, block, send, pair_out),
-        in_specs=specs(1) + anywhere(12) + anywhere(2),
+        in_specs=specs(1) + anywhere(16),
         out_specs=(pl.BlockSpec(memory_space=pltpu.VMEM),) * 5
         + tuple(anywhere(3))
         + (pl.BlockSpec(memory_space=pltpu.VMEM),),
@@ -506,7 +519,7 @@
             pltpu.VMEM(packs[3].shape, jnp.bfloat16),
             pltpu.SemaphoreType.DMA((2,)),
         ],
-        compiler_params=params(48),
+        compiler_params=params(52),
         cost_estimate=cost(0),
         name="last_layer",
     )(dp, pair, *packs, *parts, act, cots)
@@ -671,7 +684,7 @@
         ],
         out_specs=(pl.BlockSpec((part, cols // count), lambda i: (i, 0)),) * count,
         compiler_params=params(),
-        cost_estimate=cost(4 if count == 1 else 0),
+        cost_estimate=cost(6 if count == 1 else 0),
         name=f"finish_{count}",
     )(own, got, far)
 
@@ -697,21 +710,22 @@
     )
     ends = [(0, 3), (3, 0)]
     chunk = prep(table, tokens, cotangent)
-    weights = [stack(w_gate[0], w_up[0]), w_down[0]]
+    weights = [w[0] for w in (w_gate, w_up, w_down)]
     near = [swap(w, 1) for w in weights]
     up_1, down_1 = along(chunk, upward), along(chunk, downward)
     picked = [pick(cap, 0, after(me, *near), [chunk])]
     own_4, other_4, _ = pick(cap, 4, after(me, *near), [chunk])
     crossed = [across(picked[0][1])]
     crossed_4 = lax.ppermute(other_4, "expert", [(e, e ^ 1) for e in (0, 1, 6, 7)])
-    far = [swap(weights[0], 2)]
-    picked.append(pick(cap, 1, me, [down_1, up_1]))
-    first = [picked[1][2]]
+    far = [swap(stack(weights[0], weights[1]), 2)]
+    picked.append(pick(cap, 1, me, [up_1, down_1]))
+    ready = pause(after(picked[0][2], up_1, down_1), 4)
+    first = [ready]
     down_2 = along(after(down_1, *first), downward[:2])
     up_2 = along(after(up_1, *first), upward[1:])
     own_3, other_3, pair_3 = pick(cap, 3, me, [down_1, up_1])
     crossed.append(across(after(picked[1][1], crossed[0], crossed_4)))
-    far.append(swap(weights[1], 2))
+    far.append(swap(weights[2], 2))
     picked.append(pick(cap, 2, after(me, crossed[1]), [down_2, up_2]))
     far_near = [swap(after(w, picked[2][2]), 1) for w in far]
     crossed.append(across(picked[2][1]))
@@ -719,8 +733,8 @@
         after(other_3, picked[2][2]), "expert", [(e, e ^ 1) for e in (2, 3, 4, 5)]
     )
     far_own, far_got = (along(after(v, down_2, up_2), ends) for v in (own_4, crossed_4))
-    pairs = [p[2] for p in picked]
-    parts = [part for group in zip(weights, near, far, far_near) for part in group]
+    pairs = [ready] + [p[2] for p in picked[1:]]
+    parts = [*weights[:2], *near[:2], far[0], far_near[0], weights[2], near[2], far[1], far_near[1]]
     packs = [v for p, c in zip(picked, crossed) for v in (p[0], c)]
     slots_a, (rows_a, cots_a, act_a, dgate_a, dup_a) = layer(cap, dp, packs, parts)
     packs = [own_3, crossed_3, far_own, far_got]

time: 197 us -> 194 us (0.985)
  waiting for transfers between devices: 88.4 us -> 84.8 us
    ppermute x9, waiting for transfers between devices: 24.5 us -> 15.4 us  [along(): lax.ppermute(value, 'expert', [(2 * a + x, 2 * b + x) for a, b in pairs f...]
    ppermute x5, waiting for transfers between devices: 21.7 us -> 25.3 us  [across(): return lax.ppermute(value, 'expert', [(e, e ^ 1) for e in range(owners)])]
    ppermute x10 -> x11, waiting for transfers between devices: 42.1 us -> 44.1 us  [swap(): return lax.ppermute(value, 'dp', [(i, i ^ bit) for i in range(count)])]
    unnamed x60 -> x54, local copies, waits for them, and re-layouts: 9.88 us -> 8.35 us
    ppermute x10 -> x11, starting transfers between devices: 6.34 us -> 6.46 us  [swap(): return lax.ppermute(value, 'dp', [(i, i ^ bit) for i in range(count)])]
  transfers between devices with their start and end apart: 26 -> 27, of which waited for: 9 -> 9; matrix products, arithmetic and copies ran while one was open for 1% -> 1% of each run, Pallas kernels for 26% -> 27%
where the time goes in v4:
time: 194 us
  waiting for transfers between devices  84.8 us (44%)
  Pallas kernels  55.4 us (29%)
  starting transfers between devices  40.4 us (21%)
  local copies, waits for them, and re-layouts  8.35 us (4%)
  other arithmetic  3.87 us (2%)
    ppermute x11, waiting for transfers between devices, swap(): return lax.ppermute(value, 'dp', [(i, i ^ bit) for i in range(count)])  44.1 us
    ppermute x5, waiting for transfers between devices, across(): return lax.ppermute(value, 'expert', [(e, e ^ 1) for e in range(owners)])  25.3 us
    ppermute x9, starting transfers between devices, along(): lax.ppermute(value, 'expert', [(2 * a + x, 2 * b + x) for a, b in pairs f...  22.8 us
    ppermute x9, waiting for transfers between devices, along(): lax.ppermute(value, 'expert', [(2 * a + x, 2 * b + x) for a, b in pairs f...  15.4 us
    pallas_call x1, Pallas kernels, layer(): pl.pallas_call(functools.partial(layer_kernel, cap, count), out_shape=(sl...  14.8 us
    pallas_call x1, Pallas kernels, last_layer(): pl.pallas_call(functools.partial(last_kernel, cap), out_shape=(slot, slot...  14.6 us
    unnamed x54, local copies, waits for them, and re-layouts  8.35 us
    pallas_call x1, Pallas kernels, outer(): pl.pallas_call(outer_kernel, out_shape=(block, block, send), in_specs=spe...  7.35 us
  transfers between devices with their start and end apart: 27, of which 9 were waited for; matrix products, arithmetic and copies ran while one was open for 1% of the time, Pallas kernels for 27%

profile of v4, /device:TPU:0, one launch (start us, length us, event | category | flops | bytes accessed | tf_op | source)
XLA Modules:
  0.0 193.9 jit_solution(4610105822446110649)
XLA Ops:
  0.6 1.3 select_reduce_fusion.table_ref
  1.9 2.3 %prep.1.refs_0_ = bf16[272,2048]{1,0:T(8,128)(2,1)} custom-call(f32[8,128]{1,0:T(8,128)} %select_reduce_fusion.table_ref, bf16[128,2048]{1,0:T(8,128)(2,1)} %tokens_ref.1, bf16[128,2048]{1,0:T(8,128)(2,1)} %cots_ref.1), custom_call_target="tpu_custom_call" | custom-call | flops 2000000000 | tf_op jit(solution)/shard_map/prep/pallas_call | solution.py:177
  4.2 1.3 collective-permute-start.4
  5.5 5.6 %collective-permute-start.3 = (bf16[272,2048]{1,0:T(8,128)(2,1)}, bf16[272,2048]{1,0:T(8,128)(2,1)S(1)}, u32[]{:S(2)}, u32[]{:S(2)}) collective-permute-start(bf16[272,2048]{1,0:T(8,128)(2,1)} %prep.1.refs_0_), channel_id=1, source_target_pairs={{0,8},{4,12},{8,16},{12,20},{16,24},{20,28},{1,9},{5,13},{9,17},{1... | collective-permute-start | bytes 3342344 | tf_op jit(solution)/shard_map/ppermute | solution.py:701
  11.2 0.5 collective-permute-start.1
  11.7 0.1 collective-permute-start.2
  11.8 2.7 %stack.1 = bf16[1024,768]{1,0:T(8,128)(2,1)} custom-call(bf16[512,768]{1,0:T(8,128)(2,1)} %bitcast.1.first_ref.refs_6_.refs_0_, bf16[512,768]{1,0:T(8,128)(2,1)} %bitcast.2.second_ref.refs_7_.refs_1_), custom_call_target="tpu_custom_call" | custom-call | tf_op jit(solution)/shard_map/stack/pallas_call | solution.py:195
  14.6 2.0 %collective-permute-start.11 = (bf16[1024,768]{1,0:T(8,128)(2,1)}, bf16[1024,768]{1,0:T(8,128)(2,1)}, u32[]{:S(2)}, u32[]{:S(2)}) collective-permute-start(bf16[1024,768]{1,0:T(8,128)(2,1)} %stack.1), channel_id=1, source_target_pairs={{0,2},{1,3},{2,0},{3,1},{4,6},{5,7},{6,4},{7,5},{8,10},{9,11},{10,... | collective-permute-start | bytes 4718600 | tf_op jit(solution)/shard_map/ppermute | solution.py:20
  16.5 0.7 pick_0.1
  17.3 1.6 pick_4.1
  18.9 3.4 %collective-permute-start.6 = (bf16[144,2048]{1,0:T(8,128)(2,1)S(1)}, bf16[144,2048]{1,0:T(8,128)(2,1)}, u32[]{:S(2)}, u32[]{:S(2)}) collective-permute-start(bf16[144,2048]{1,0:T(8,128)(2,1)S(1)} %get-tuple-element.70), channel_id=1, source_target_pairs={{0,4},{4,0},{24,28},{28,24},{1,5},{5,1},{25,29},{29,25},{2,6},{6,2... | collective-permute-start | bytes 1769480 | tf_op jit(solution)/shard_map/ppermute | solution.py:719
  22.3 0.6 collective-permute-start.5
  22.9 11.0 %collective-permute-done.4.refs_1_.refs_0_ = bf16[272,2048]{1,0:T(8,128)(2,1)S(1)} collective-permute-done((bf16[272,2048]{1,0:T(8,128)(2,1)}, bf16[272,2048]{1,0:T(8,128)(2,1)S(1)}, u32[]{:S(2)}, u32[]{:S(2)}) %collective-permute-start.4) | collective-permute-done | bytes 1114144 | tf_op jit(solution)/shard_map/ppermute | solution.py:701
  33.9 1.3 collective-permute-done.3.refs_0_.refs_1_
  35.2 1.4 collective-permute-start.8
  36.6 0.7 collective-permute-start.9
  37.4 0.8 pick_1.1
  38.2 10.5 %collective-permute-done.5.refs_1_ = bf16[144,2048]{1,0:T(8,128)(2,1)S(1)} collective-permute-done((bf16[144,2048]{1,0:T(8,128)(2,1)S(1)}, bf16[144,2048]{1,0:T(8,128)(2,1)S(1)}, u32[]{:S(2)}, u32[]{:S(2)}) %collective-permute-start.5) | collective-permute-done | bytes 589856 | tf_op jit(solution)/shard_map/ppermute | solution.py:704
  48.7 1.6 collective-permute-start.7
  50.3 1.5 collective-permute-start.13
  51.8 11.5 %collective-permute-done.7.refs_3_ = bf16[144,2048]{1,0:T(8,128)(2,1)S(1)} collective-permute-done((bf16[144,2048]{1,0:T(8,128)(2,1)S(1)}, bf16[144,2048]{1,0:T(8,128)(2,1)S(1)}, u32[]{:S(2)}, u32[]{:S(2)}) %collective-permute-start.7) | collective-permute-done | bytes 589856 | tf_op jit(solution)/shard_map/ppermute | solution.py:704
  63.3 0.1 collective-permute-done.8.refs_0_
  63.4 0.7 copy-done.24
  64.1 0.8 pick_2.1
  64.9 0.8 copy-done.15
  65.7 1.6 collective-permute-start.10
  67.4 1.6 collective-permute-done.13.refs_14_.refs_8_
  69.0 4.1 %collective-permute-start.17 = (bf16[160,2048]{1,0:T(8,128)(2,1)}, bf16[160,2048]{1,0:T(8,128)(2,1)S(1)}, u32[]{:S(2)}, u32[]{:S(2)}) collective-permute-start(bf16[160,2048]{1,0:T(8,128)(2,1)} %get-tuple-element.90), channel_id=1, source_target_pairs={{0,24},{4,28},{24,0},{28,4},{1,25},{5,29},{25,1},{29,5},{2,26},{6,... | collective-permute-start | bytes 1966088 | tf_op jit(solution)/shard_map/ppermute | solution.py:701
  73.1 3.5 %collective-permute-start.18 = (bf16[144,2048]{1,0:T(8,128)(2,1)}, bf16[144,2048]{1,0:T(8,128)(2,1)}, u32[]{:S(2)}, u32[]{:S(2)}) collective-permute-start(bf16[144,2048]{1,0:T(8,128)(2,1)} %collective-permute-done.6), channel_id=1, source_target_pairs={{0,24},{4,28},{24,0},{28,4},{1,25},{5,29},{25,1},{29,5},{2,26},{6,... | collective-permute-start | bytes 1769480 | tf_op jit(solution)/shard_map/ppermute | solution.py:701
  76.6 0.8 pick_3.1
  77.4 0.8 copy-done.14
  78.2 3.2 %collective-permute-done.10.refs_5_ = bf16[144,2048]{1,0:T(8,128)(2,1)S(1)} collective-permute-done((bf16[144,2048]{1,0:T(8,128)(2,1)S(1)}, bf16[144,2048]{1,0:T(8,128)(2,1)S(1)}, u32[]{:S(2)}, u32[]{:S(2)}) %collective-permute-start.10) | collective-permute-done | bytes 589856 | tf_op jit(solution)/shard_map/ppermute | solution.py:704
  81.5 0.8 copy-done.26
  82.3 0.9 collective-permute-start.16
  83.2 14.8 %layer.1 = (bf16[216,2048]{1,0:T(8,128)(2,1)}, bf16[216,2048]{1,0:T(8,128)(2,1)}, bf16[432,2048]{1,0:T(8,128)(2,1)}, bf16[432,2048]{1,0:T(8,128)(2,1)}, bf16[432...) custom-call(s32[1]{0:T(128)} %bitcast.6.dp_ref, bf16[144,2048]{1,0:T(8,128)(2,1)} %copy-done.12, ...), custom_call_target="tpu_custom_call" | custom-call | tf_op jit(solution)/shard_map/layer/pallas_call | solution.py:376
  98.0 1.7 collective-permute-start.15
  99.7 0.1 pad_add_fusion.dp_ref
  99.8 3.0 %collective-permute-done.18.far_got = bf16[144,2048]{1,0:T(8,128)(2,1)} collective-permute-done((bf16[144,2048]{1,0:T(8,128)(2,1)}, bf16[144,2048]{1,0:T(8,128)(2,1)}, u32[]{:S(2)}, u32[]{:S(2)}) %collective-permute-start.18) | collective-permute-done | bytes 589856 | tf_op jit(solution)/shard_map/ppermute | solution.py:701
  102.8 0.8 copy-done.25
  103.6 0.2 copy-done.22
  103.8 14.6 %last_layer.1 = (bf16[72,2048]{1,0:T(8,128)(2,1)S(1)}, bf16[72,2048]{1,0:T(8,128)(2,1)}, bf16[144,2048]{1,0:T(8,128)(2,1)S(1)}, bf16[144,768]{1,0:T(8,128)(2,1)S...) custom-call(s32[2]{0:T(128)S(1)} %pad_add_fusion.dp_ref, ...), custom_call_target="tpu_custom_call" | custom-call | tf_op jit(solution)/shard_map/last_layer/pallas_call | solution.py:503
  118.5 1.4 collective-permute-start.22
  119.9 7.4 %outer.1 = (f32[512,1536]{1,0:T(8,128)S(1)}, f32[512,1536]{1,0:T(8,128)S(1)}, bf16[2,512,1536]{2,1,0:T(8,128)(2,1)S(1)}) custom-call(s32[1]{0:T(128)} %bitcast.6.dp_ref, bf16[432,2048]{1,0:T(8,128)(2,1)S(1)} %copy-done.3, bf16[144,2048]{1,0:T(8,128)(2,1)S(1)} %get-tuple-element.96.refs_1_, bf16[432,768]{1,0:T(8,128)(2,1)S(1)} %copy-done.10, ...), custom_call_target="tpu_custom_call" | custom-call | tf_op jit(solution)/shard_map/outer/pallas_call | solution.py:571
  127.3 0.2 collective-permute-start.21
  127.5 1.4 copy-done.1
  128.9 0.2 copy-done.9
  129.1 1.1 spread_3.1
  130.3 1.2 merge.2
  131.5 0.1 copy-done.16
  131.6 0.2 copy-done.20
  131.8 0.5 copy-done.4
  132.3 0.7 copy-done.17
  133.0 1.3 merge.3
  134.3 1.6 collective-permute-start.23
  135.9 0.5 collective-permute-start.20
  136.4 2.2 %collective-permute-start.24 = (bf16[128,2048]{1,0:T(8,128)(2,1)}, bf16[128,2048]{1,0:T(8,128)(2,1)S(1)}, u32[]{:S(2)}, u32[]{:S(2)}) collective-permute-start(bf16[128,2048]{1,0:T(8,128)(2,1)} %copy-done.20), channel_id=1, source_target_pairs={{0,16},{4,20},{8,24},{12,28},{16,0},{20,4},{24,8},{28,12},{1,17},{... | collective-permute-start | bytes 1572872 | tf_op jit(solution)/shard_map/ppermute | solution.py:701
  138.6 1.0 copy-done.18
  139.6 0.6 spread_1.1
  140.2 1.4 broadcast_select_fusion.1
  141.7 3.8 %collective-permute-start.26 = (bf16[128,2048]{1,0:T(8,128)(2,1)S(1)}, bf16[128,2048]{1,0:T(8,128)(2,1)S(1)}, u32[]{:S(2)}, u32[]{:S(2)}) collective-permute-start(bf16[128,2048]{1,0:T(8,128)(2,1)S(1)} %get-tuple-element.123), channel_id=1, source_target_pairs={{0,24},{4,28},{8,0},{12,4},{16,8},{20,12},{24,16},{28,20},{1,25},{... | collective-permute-start | bytes 1572872 | tf_op jit(solution)/shard_map/ppermute | solution.py:701
  145.5 42.5 %collective-permute-done.20.far_ref = bf16[192,2048]{1,0:T(8,128)(2,1)} collective-permute-done((bf16[192,2048]{1,0:T(8,128)(2,1)}, bf16[192,2048]{1,0:T(8,128)(2,1)}, u32[]{:S(2)}, u32[]{:S(2)}) %collective-permute-start.20) | collective-permute-done | bytes 786464 | tf_op jit(solution)/shard_map/ppermute | solution.py:20
  188.0 2.2 %finish_1.1 = bf16[192,2048]{1,0:T(8,128)(2,1)} custom-call(f32[192,2048]{1,0:T(8,128)S(1)} %copy-done.19, bf16[2,192,2048]{2,1,0:T(8,128)(2,1)S(1)} %copy-done.5, bf16[192,2048]{1,0:T(8,128)(2,1)} %collective-permute-done.20.far_ref), custom_call_target="tpu_custom_call" | custom-call | flops 6000000000 | tf_op jit(solution)/shard_map/finish_1/pallas_call | solution.py:676
  190.2 2.6 %finish_2.1 = (bf16[512,768]{1,0:T(8,128)(2,1)}, bf16[512,768]{1,0:T(8,128)(2,1)}) custom-call(f32[512,1536]{1,0:T(8,128)S(1)} %copy-done.2, bf16[2,512,1536]{2,1,0:T(8,128)(2,1)S(1)} %collective-permute-done.21.got_ref, bf16[512,1536]{1,0:T(8,128)(2,1)} %collective-permute-done.23.far_ref), custom_call_target="tpu_custom_call" | custom-call | tf_op jit(solution)/shard_map/finish_2/pallas_call | solution.py:676
  192.8 1.1 add_convert_fusion
  (67 shorter events, 0.4 us)
Async XLA Ops:
  4.2 29.7 %collective-permute-start.4 = (bf16[272,2048]{1,0:T(8,128)(2,1)}, bf16[272,2048]{1,0:T(8,128)(2,1)S(1)}, u32[]{:S(2)}, u32[]{:S(2)}) collective-permute-start(bf16[272,2048]{1,0:T(8,128)(2,1)} %prep.1.refs_0_), channel_id=1, source_target_pairs={{8,0},{12,4},{16,8},{20,12},{24,16},{28,20},{9,1},{13,5},{17,9},{2... | collective-permute-start | bytes 3342344 | tf_op jit(solution)/shard_map/ppermute | solution.py:701
  5.5 29.7 %collective-permute-start.3 = (bf16[272,2048]{1,0:T(8,128)(2,1)}, bf16[272,2048]{1,0:T(8,128)(2,1)S(1)}, u32[]{:S(2)}, u32[]{:S(2)}) collective-permute-start(bf16[272,2048]{1,0:T(8,128)(2,1)} %prep.1.refs_0_), channel_id=1, source_target_pairs={{0,8},{4,12},{8,16},{12,20},{16,24},{20,28},{1,9},{5,13},{9,17},{1... | collective-permute-start | bytes 3342344 | tf_op jit(solution)/shard_map/ppermute | solution.py:701
  11.2 3.4 %collective-permute-start = (bf16[512,768]{1,0:T(8,128)(2,1)}, bf16[512,768]{1,0:T(8,128)(2,1)}, u32[]{:S(2)}, u32[]{:S(2)}) collective-permute-start(bf16[512,768]{1,0:T(8,128)(2,1)} %bitcast.1.first_ref.refs_6_.refs_0_), channel_id=1, source_target_pairs={{0,1},{1,0},{2,3},{3,2},{4,5},{5,4},{6,7},{7,6},{8,9},{9,8},{10,11... | collective-permute-start | bytes 2359304 | tf_op jit(solution)/shard_map/ppermute | solution.py:20
  11.2 5.3 %collective-permute-start.1 = (bf16[512,768]{1,0:T(8,128)(2,1)}, bf16[512,768]{1,0:T(8,128)(2,1)}, u32[]{:S(2)}, u32[]{:S(2)}) collective-permute-start(bf16[512,768]{1,0:T(8,128)(2,1)} %bitcast.2.second_ref.refs_7_.refs_1_), channel_id=1, source_target_pairs={{0,1},{1,0},{2,3},{3,2},{4,5},{5,4},{6,7},{7,6},{8,9},{9,8},{10,11... | collective-permute-start | bytes 2359304 | tf_op jit(solution)/shard_map/ppermute | solution.py:20
  11.7 4.8 %copy-start = (bf16[272,2048]{1,0:T(8,128)(2,1)S(1)}, bf16[272,2048]{1,0:T(8,128)(2,1)}, u32[]{:S(2)}) copy-start(bf16[272,2048]{1,0:T(8,128)(2,1)} %prep.1.refs_0_) | copy-start | bytes 3342340
  11.7 4.8 %collective-permute-start.2 = (bf16[192,2048]{1,0:T(8,128)(2,1)}, bf16[192,2048]{1,0:T(8,128)(2,1)}, u32[]{:S(2)}, u32[]{:S(2)}) collective-permute-start(bf16[192,2048]{1,0:T(8,128)(2,1)} %bitcast.11), channel_id=1, source_target_pairs={{0,1},{1,0},{2,3},{3,2},{4,5},{5,4},{6,7},{7,6},{8,9},{9,8},{10,11... | collective-permute-start | bytes 2359304 | tf_op jit(solution)/shard_map/ppermute | solution.py:20
  14.6 51.2 %collective-permute-start.11 = (bf16[1024,768]{1,0:T(8,128)(2,1)}, bf16[1024,768]{1,0:T(8,128)(2,1)}, u32[]{:S(2)}, u32[]{:S(2)}) collective-permute-start(bf16[1024,768]{1,0:T(8,128)(2,1)} %stack.1), channel_id=1, source_target_pairs={{0,2},{1,3},{2,0},{3,1},{4,6},{5,7},{6,4},{7,5},{8,10},{9,11},{10,... | collective-permute-start | bytes 4718600 | tf_op jit(solution)/shard_map/ppermute | solution.py:20
  17.3 17.9 %copy-start.12 = (bf16[144,2048]{1,0:T(8,128)(2,1)}, bf16[144,2048]{1,0:T(8,128)(2,1)S(1)}, u32[]{:S(2)}) copy-start(bf16[144,2048]{1,0:T(8,128)(2,1)S(1)} %get-tuple-element.66.refs_0_) | copy-start | bytes 1769476
  18.9 19.3 %collective-permute-start.6 = (bf16[144,2048]{1,0:T(8,128)(2,1)S(1)}, bf16[144,2048]{1,0:T(8,128)(2,1)}, u32[]{:S(2)}, u32[]{:S(2)}) collective-permute-start(bf16[144,2048]{1,0:T(8,128)(2,1)S(1)} %get-tuple-element.70), channel_id=1, source_target_pairs={{0,4},{4,0},{24,28},{28,24},{1,5},{5,1},{25,29},{29,25},{2,6},{6,2... | collective-permute-start | bytes 1769480 | tf_op jit(solution)/shard_map/ppermute | solution.py:719
  22.3 26.4 %collective-permute-start.5 = (bf16[144,2048]{1,0:T(8,128)(2,1)S(1)}, bf16[144,2048]{1,0:T(8,128)(2,1)S(1)}, u32[]{:S(2)}, u32[]{:S(2)}) collective-permute-start(bf16[144,2048]{1,0:T(8,128)(2,1)S(1)} %get-tuple-element.67), channel_id=1, source_target_pairs={{0,4},{4,0},{8,12},{12,8},{16,20},{20,16},{24,28},{28,24},{1,5},{5... | collective-permute-start | bytes 1769480 | tf_op jit(solution)/shard_map/ppermute | solution.py:704
  35.2 15.1 %copy-start.21 = (bf16[1,192,2048]{2,1,0:T(8,128)(2,1)S(1)}, bf16[1,192,2048]{2,1,0:T(8,128)(2,1)}, u32[]{:S(2)}) copy-start(bf16[1,192,2048]{2,1,0:T(8,128)(2,1)} %param.13) | copy-start | bytes 2359300
  35.2 28.2 %collective-permute-start.8 = (bf16[272,2048]{1,0:T(8,128)(2,1)S(1)}, bf16[272,2048]{1,0:T(8,128)(2,1)S(1)}, u32[]{:S(2)}, u32[]{:S(2)}) collective-permute-start(bf16[272,2048]{1,0:T(8,128)(2,1)S(1)} %collective-permute-done.4.refs_1_.refs_0_), channel_id=1, source_target_pairs={{8,0},{12,4},{16,8},{20,12},{9,1},{13,5},{17,9},{21,13},{10,2},{14... | collective-permute-start | bytes 3342344 | tf_op jit(solution)/shard_map/ppermute | solution.py:701
  36.6 27.5 %collective-permute-start.9 = (bf16[272,2048]{1,0:T(8,128)(2,1)S(1)}, bf16[272,2048]{1,0:T(8,128)(2,1)S(1)}, u32[]{:S(2)}, u32[]{:S(2)}) collective-permute-start(bf16[272,2048]{1,0:T(8,128)(2,1)S(1)} %collective-permute-done.3.refs_0_.refs_1_), channel_id=1, source_target_pairs={{8,16},{12,20},{16,24},{20,28},{9,17},{13,21},{17,25},{21,29},{10,... | collective-permute-start | bytes 3342344 | tf_op jit(solution)/shard_map/ppermute | solution.py:701
  38.2 26.7 %copy-start.13 = (bf16[144,2048]{1,0:T(8,128)(2,1)}, bf16[144,2048]{1,0:T(8,128)(2,1)S(1)}, u32[]{:S(2)}) copy-start(bf16[144,2048]{1,0:T(8,128)(2,1)S(1)} %get-tuple-element.68.refs_2_) | copy-start | bytes 1769476
  48.7 28.7 %copy-start.23 = (bf16[144,2048]{1,0:T(8,128)(2,1)}, bf16[144,2048]{1,0:T(8,128)(2,1)S(1)}, u32[]{:S(2)}) copy-start(bf16[144,2048]{1,0:T(8,128)(2,1)S(1)} %collective-permute-done.5.refs_1_) | copy-start | bytes 1769476
  48.7 14.6 %collective-permute-start.7 = (bf16[144,2048]{1,0:T(8,128)(2,1)S(1)}, bf16[144,2048]{1,0:T(8,128)(2,1)S(1)}, u32[]{:S(2)}, u32[]{:S(2)}) collective-permute-start(bf16[144,2048]{1,0:T(8,128)(2,1)S(1)} %get-tuple-element.71), channel_id=1, source_target_pairs={{0,4},{4,0},{8,12},{12,8},{16,20},{20,16},{24,28},{28,24},{1,5},{5... | collective-permute-start | bytes 1769480 | tf_op jit(solution)/shard_map/ppermute | solution.py:704
  50.3 18.7 %collective-permute-start.13 = (bf16[192,2048]{1,0:T(8,128)(2,1)S(1)}, bf16[192,2048]{1,0:T(8,128)(2,1)}, u32[]{:S(2)}, u32[]{:S(2)}) collective-permute-start(bf16[192,2048]{1,0:T(8,128)(2,1)S(1)} %bitcast.14), channel_id=1, source_target_pairs={{0,2},{1,3},{2,0},{3,1},{4,6},{5,7},{6,4},{7,5},{8,10},{9,11},{10,... | collective-permute-start | bytes 2359304 | tf_op jit(solution)/shard_map/ppermute | solution.py:20
  63.3 0.8 copy-start.24
  64.9 0.8 copy-start.15
  65.7 17.5 %collective-permute-start.12 = (bf16[1024,768]{1,0:T(8,128)(2,1)}, bf16[1024,768]{1,0:T(8,128)(2,1)}, u32[]{:S(2)}, u32[]{:S(2)}) collective-permute-start(bf16[1024,768]{1,0:T(8,128)(2,1)} %collective-permute-done.11.refs_10_.refs_4_), channel_id=1, source_target_pairs={{0,1},{1,0},{2,3},{3,2},{4,5},{5,4},{6,7},{7,6},{8,9},{9,8},{10,11... | collective-permute-start | bytes 4718600 | tf_op jit(solution)/shard_map/ppermute | solution.py:20
  65.7 15.7 %collective-permute-start.10 = (bf16[144,2048]{1,0:T(8,128)(2,1)S(1)}, bf16[144,2048]{1,0:T(8,128)(2,1)S(1)}, u32[]{:S(2)}, u32[]{:S(2)}) collective-permute-start(bf16[144,2048]{1,0:T(8,128)(2,1)S(1)} %get-tuple-element.76), channel_id=1, source_target_pairs={{0,4},{4,0},{8,12},{12,8},{16,20},{20,16},{24,28},{28,24},{1,5},{5... | collective-permute-start | bytes 1769480 | tf_op jit(solution)/shard_map/ppermute | solution.py:704
  69.0 14.2 %collective-permute-start.14 = (bf16[192,2048]{1,0:T(8,128)(2,1)}, bf16[192,2048]{1,0:T(8,128)(2,1)}, u32[]{:S(2)}, u32[]{:S(2)}) collective-permute-start(bf16[192,2048]{1,0:T(8,128)(2,1)} %collective-permute-done.13.refs_14_.refs_8_), channel_id=1, source_target_pairs={{0,1},{1,0},{2,3},{3,2},{4,5},{5,4},{6,7},{7,6},{8,9},{9,8},{10,11... | collective-permute-start | bytes 2359304 | tf_op jit(solution)/shard_map/ppermute | solution.py:20
  69.0 33.8 %collective-permute-start.17 = (bf16[160,2048]{1,0:T(8,128)(2,1)}, bf16[160,2048]{1,0:T(8,128)(2,1)S(1)}, u32[]{:S(2)}, u32[]{:S(2)}) collective-permute-start(bf16[160,2048]{1,0:T(8,128)(2,1)} %get-tuple-element.90), channel_id=1, source_target_pairs={{0,24},{4,28},{24,0},{28,4},{1,25},{5,29},{25,1},{29,5},{2,26},{6,... | collective-permute-start | bytes 1966088 | tf_op jit(solution)/shard_map/ppermute | solution.py:701
  73.1 29.7 %collective-permute-start.18 = (bf16[144,2048]{1,0:T(8,128)(2,1)}, bf16[144,2048]{1,0:T(8,128)(2,1)}, u32[]{:S(2)}, u32[]{:S(2)}) collective-permute-start(bf16[144,2048]{1,0:T(8,128)(2,1)} %collective-permute-done.6), channel_id=1, source_target_pairs={{0,24},{4,28},{24,0},{28,4},{1,25},{5,29},{25,1},{29,5},{2,26},{6,... | collective-permute-start | bytes 1769480 | tf_op jit(solution)/shard_map/ppermute | solution.py:701
  77.4 0.8 copy-start.14
  81.5 0.8 copy-start.26
  82.3 20.5 %collective-permute-start.16 = (bf16[144,2048]{1,0:T(8,128)(2,1)S(1)}, bf16[144,2048]{1,0:T(8,128)(2,1)S(1)}, u32[]{:S(2)}, u32[]{:S(2)}) collective-permute-start(bf16[144,2048]{1,0:T(8,128)(2,1)S(1)} %get-tuple-element.87), channel_id=1, source_target_pairs={{8,12},{12,8},{16,20},{20,16},{9,13},{13,9},{17,21},{21,17},{10,14... | collective-permute-start | bytes 1769480 | tf_op jit(solution)/shard_map/ppermute | solution.py:732
  98.0 29.5 %collective-permute-start.15 = (bf16[216,2048]{1,0:T(8,128)(2,1)}, bf16[216,2048]{1,0:T(8,128)(2,1)S(1)}, u32[]{:S(2)}, u32[]{:S(2)}) collective-permute-start(bf16[216,2048]{1,0:T(8,128)(2,1)} %get-tuple-element.80), channel_id=1, source_target_pairs={{0,4},{4,0},{8,12},{12,8},{16,20},{20,16},{24,28},{28,24},{1,5},{5... | collective-permute-start | bytes 2654216 | tf_op jit(solution)/shard_map/ppermute | solution.py:704
  102.8 1.0 copy-start.22
  102.8 0.9 copy-start.25
  103.8 16.1 %copy-start.3 = (bf16[432,2048]{1,0:T(8,128)(2,1)S(1)}, bf16[432,2048]{1,0:T(8,128)(2,1)}, u32[]{:S(2)}) copy-start(bf16[432,2048]{1,0:T(8,128)(2,1)} %get-tuple-element.81.refs_0_) | copy-start | bytes 5308420
  103.8 16.1 %copy-start.10 = (bf16[432,768]{1,0:T(8,128)(2,1)S(1)}, bf16[432,768]{1,0:T(8,128)(2,1)}, u32[]{:S(2)}) copy-start(bf16[432,768]{1,0:T(8,128)(2,1)} %get-tuple-element.97.refs_2_) | copy-start | bytes 1990660
  103.8 16.1 %copy-start.11 = (bf16[432,768]{1,0:T(8,128)(2,1)S(1)}, bf16[432,768]{1,0:T(8,128)(2,1)}, u32[]{:S(2)}) copy-start(bf16[432,768]{1,0:T(8,128)(2,1)} %get-tuple-element.99.refs_4_) | copy-start | bytes 1990660
  118.4 11.8 %collective-permute-start.19 = (bf16[2,192,2048]{2,1,0:T(8,128)(2,1)}, bf16[2,192,2048]{2,1,0:T(8,128)(2,1)S(1)}, u32[]{:S(2)}, u32[]{:S(2)}) collective-permute-start(bf16[2,192,2048]{2,1,0:T(8,128)(2,1)} %get-tuple-element.106), channel_id=1, source_target_pairs={{0,1},{1,0},{2,3},{3,2},{4,5},{5,4},{6,7},{7,6},{8,9},{9,8},{10,11... | collective-permute-start | bytes 4718600 | tf_op jit(solution)/shard_map/ppermute | solution.py:20
  118.5 13.8 %collective-permute-start.22 = (bf16[72,2048]{1,0:T(8,128)(2,1)}, bf16[72,2048]{1,0:T(8,128)(2,1)S(1)}, u32[]{:S(2)}, u32[]{:S(2)}) collective-permute-start(bf16[72,2048]{1,0:T(8,128)(2,1)} %get-tuple-element.113), channel_id=1, source_target_pairs={{0,4},{4,0},{8,12},{12,8},{16,20},{20,16},{24,28},{28,24},{1,5},{5... | collective-permute-start | bytes 884744 | tf_op jit(solution)/shard_map/ppermute | solution.py:704
  127.3 1.6 copy-start.1
  127.3 1.8 copy-start.9
  127.3 5.8 %collective-permute-start.21 = (bf16[2,512,1536]{2,1,0:T(8,128)(2,1)S(1)}, bf16[2,512,1536]{2,1,0:T(8,128)(2,1)S(1)}, u32[]{:S(2)}, u32[]{:S(2)}) collective-permute-start(bf16[2,512,1536]{2,1,0:T(8,128)(2,1)S(1)} %get-tuple-element.101), channel_id=1, source_target_pairs={{0,1},{1,0},{2,3},{3,2},{4,5},{5,4},{6,7},{7,6},{8,9},{9,8},{10,11... | collective-permute-start | bytes 9437192 | tf_op jit(solution)/shard_map/ppermute | solution.py:20
  128.9 1.5 copy-start.6
  130.2 1.3 copy-start.7
  130.2 1.4 copy-start.16
  130.2 1.6 copy-start.20
  130.3 2.0 %copy-start.4 = (bf16[2,192,2048]{2,1,0:T(8,128)(2,1)}, bf16[2,192,2048]{2,1,0:T(8,128)(2,1)S(1)}, u32[]{:S(2)}) copy-start(bf16[2,192,2048]{2,1,0:T(8,128)(2,1)S(1)} %collective-permute-done.19.got_ref) | copy-start | bytes 4718596
  132.3 0.7 copy-start.17
  134.3 55.8 %collective-permute-start.23 = (bf16[512,1536]{1,0:T(8,128)(2,1)}, bf16[512,1536]{1,0:T(8,128)(2,1)}, u32[]{:S(2)}, u32[]{:S(2)}) collective-permute-start(bf16[512,1536]{1,0:T(8,128)(2,1)} %merge.3), channel_id=1, source_target_pairs={{0,2},{1,3},{2,0},{3,1},{4,6},{5,7},{6,4},{7,5},{8,10},{9,11},{10,... | collective-permute-start | bytes 4718600 | tf_op jit(solution)/shard_map/ppermute | solution.py:20
  135.9 52.1 %collective-permute-start.20 = (bf16[192,2048]{1,0:T(8,128)(2,1)}, bf16[192,2048]{1,0:T(8,128)(2,1)}, u32[]{:S(2)}, u32[]{:S(2)}) collective-permute-start(bf16[192,2048]{1,0:T(8,128)(2,1)} %merge.2), channel_id=1, source_target_pairs={{0,2},{1,3},{2,0},{3,1},{4,6},{5,7},{6,4},{7,5},{8,10},{9,11},{10,... | collective-permute-start | bytes 2359304 | tf_op jit(solution)/shard_map/ppermute | solution.py:20
  136.4 56.4 %collective-permute-start.24 = (bf16[128,2048]{1,0:T(8,128)(2,1)}, bf16[128,2048]{1,0:T(8,128)(2,1)S(1)}, u32[]{:S(2)}, u32[]{:S(2)}) collective-permute-start(bf16[128,2048]{1,0:T(8,128)(2,1)} %copy-done.20), channel_id=1, source_target_pairs={{0,16},{4,20},{8,24},{12,28},{16,0},{20,4},{24,8},{28,12},{1,17},{... | collective-permute-start | bytes 1572872 | tf_op jit(solution)/shard_map/ppermute | solution.py:701
  138.6 1.0 copy-start.18
  139.6 48.4 %copy-start.5 = (bf16[2,192,2048]{2,1,0:T(8,128)(2,1)S(1)}, bf16[2,192,2048]{2,1,0:T(8,128)(2,1)}, u32[]{:S(2)}) copy-start(bf16[2,192,2048]{2,1,0:T(8,128)(2,1)} %copy-done.4) | copy-start | bytes 4718596
  139.6 48.4 %copy-start.19 = (f32[192,2048]{1,0:T(8,128)S(1)}, f32[192,2048]{1,0:T(8,128)}, u32[]{:S(2)}) copy-start(f32[192,2048]{1,0:T(8,128)} %get-tuple-element.105.own_ref) | copy-start | bytes 4718596
  141.6 51.2 %collective-permute-start.25 = (bf16[128,2048]{1,0:T(8,128)(2,1)S(1)}, bf16[128,2048]{1,0:T(8,128)(2,1)S(1)}, u32[]{:S(2)}, u32[]{:S(2)}) collective-permute-start(bf16[128,2048]{1,0:T(8,128)(2,1)S(1)} %get-tuple-element.122), channel_id=1, source_target_pairs={{0,8},{4,12},{8,16},{12,20},{16,24},{20,28},{24,0},{28,4},{1,9},{5... | collective-permute-start | bytes 1572872 | tf_op jit(solution)/shard_map/ppermute | solution.py:701
  141.7 51.1 %collective-permute-start.26 = (bf16[128,2048]{1,0:T(8,128)(2,1)S(1)}, bf16[128,2048]{1,0:T(8,128)(2,1)S(1)}, u32[]{:S(2)}, u32[]{:S(2)}) collective-permute-start(bf16[128,2048]{1,0:T(8,128)(2,1)S(1)} %get-tuple-element.123), channel_id=1, source_target_pairs={{0,24},{4,28},{8,0},{12,4},{16,8},{20,12},{24,16},{28,20},{1,25},{... | collective-permute-start | bytes 1572872 | tf_op jit(solution)/shard_map/ppermute | solution.py:701
  188.0 2.2 %copy-start.2 = (f32[512,1536]{1,0:T(8,128)S(1)}, f32[512,1536]{1,0:T(8,128)}, u32[]{:S(2)}) copy-start(f32[512,1536]{1,0:T(8,128)} %copy-done.1) | copy-start | bytes 9437188
  190.2 2.6 %copy-start.8 = (f32[128,2048]{1,0:T(8,128)S(1)}, f32[128,2048]{1,0:T(8,128)}, u32[]{:S(2)}) copy-start(f32[128,2048]{1,0:T(8,128)} %copy-done.7) | copy-start | bytes 3145732

commit v5 on v4

--- a/solution.py
+++ b/solution.py
@@ -519,7 +519,7 @@
             pltpu.VMEM(packs[3].shape, jnp.bfloat16),
             pltpu.SemaphoreType.DMA((2,)),
         ],
-        compiler_params=params(52),
+        compiler_params=params(60),
         cost_estimate=cost(0),
         name="last_layer",
     )(dp, pair, *packs, *parts, act, cots)
@@ -581,7 +581,7 @@
             pltpu.SemaphoreType.DMA((6,)),
             pltpu.SemaphoreType.DMA((4,)),
         ],
-        compiler_params=params(28),
+        compiler_params=params(60),
         cost_estimate=cost(0),
         name="outer",
     )(dp, rows[0], rows[1], dgates[0], dgates[1], dups[0], dups[1])
@@ -662,14 +662,14 @@
     )(far, got)
 
 
-def finish_kernel(own_ref, got_ref, far_ref, *outs):
+def finish_kernel(own_ref, got_ref, far_ref, _, *outs):
     total = own_ref[...] + got_ref[0].astype(jnp.float32) + far_ref[...].astype(jnp.float32)
     cols = outs[0].shape[1]
     for i, ref in enumerate(outs):
         ref[...] = total[:, i * cols : (i + 1) * cols].astype(jnp.bfloat16)
 
 
-def finish(own, got, far, count):
+def finish(own, got, far, ticket, count):
     rows, cols = own.shape
     part = rows // 2
     out = jax.ShapeDtypeStruct((rows, cols // count), jnp.bfloat16)
@@ -681,12 +681,13 @@
             pl.BlockSpec((part, cols), lambda i: (i, 0)),
             pl.BlockSpec((1, part, cols), lambda i: (1, i, 0)),
             pl.BlockSpec((part, cols), lambda i: (i, 0)),
+            *anywhere(1),
         ],
         out_specs=(pl.BlockSpec((part, cols // count), lambda i: (i, 0)),) * count,
         compiler_params=params(),
-        cost_estimate=cost(6 if count == 1 else 0),
+        cost_estimate=cost(8 if count == 1 else 0),
         name=f"finish_{count}",
-    )(own, got, far)
+    )(own, got, far, ticket)
 
 
 def grid_shards(tokens, cotangent, expert_ids, gate_probs, w_gate, w_up, w_down):
@@ -754,7 +755,7 @@
     far_sum, own_sum, send = down_sums
     got = swap(send, 1)
     far_down = merge(after(far_sum, pairs[0]), got)
-    (sum_down,) = finish(own_sum, got, swap(far_down, 2), 1)
+    (sum_down,) = finish(own_sum, got, swap(far_down, 2), pairs[0], 1)
     far_sum, own_sum, send = both_sums
     got = swap(send, 1)
     here, nigh, mid = spread(
@@ -762,15 +763,16 @@
     )
     pairs[3] = pause(after(pairs[3], back_b, far_down, mid), 30)
     far_both = merge(after(far_sum, pairs[3]), got)
-    sum_gate, sum_up = finish(after(own_sum, sum_down), got, swap(far_both, 2), 2)
     (last,) = spread(cap, pairs[3:], slots_b[0], back_b, (jnp.bfloat16,))
     parts = [
         along(mid, [(a, (a + 2) % 4) for a in range(4)]),
         along(jnp.where(z >= 2, last, nigh), [(a, (a + 1) % 4) for a in range(4)]),
         along(jnp.where(z <= 1, last, nigh), [(a, (a + 3) % 4) for a in range(4)]),
     ]
-    here = after(here, sum_down, sum_gate)
+    here = after(here, sum_down)
     grad_tokens = (here + sum(part.astype(jnp.float32) for part in parts)).astype(jnp.bfloat16)
+    ticket = pause(after(pairs[2], grad_tokens), 8)
+    sum_gate, sum_up = finish(own_sum, got, swap(far_both, 2), ticket, 2)
     return grad_tokens, sum_gate[None], sum_up[None], sum_down[None]
 
 

time: 194 us -> 188 us (0.969)
  Pallas kernels: 55.4 us -> 51.7 us
    ppermute x11, waiting for transfers between devices: 44.1 us -> 27.2 us  [swap(): return lax.ppermute(value, 'dp', [(i, i ^ bit) for i in range(count)])]
    ppermute x9, waiting for transfers between devices: 15.4 us -> 32.3 us  [along(): lax.ppermute(value, 'expert', [(2 * a + x, 2 * b + x) for a, b in pairs f...]
    pallas_call x2, Pallas kernels: 4.76 us -> 2.38 us  [finish(): pl.pallas_call(finish_kernel, out_shape=(out,) * count, grid=(2,), in_spe...]
    pallas_call x2, Pallas kernels: 2.49 us -> 0.45 us  [merge(): pl.pallas_call(merge_kernel, out_shape=jax.ShapeDtypeStruct(far.shape, jn...]
    unnamed x54 -> x36, local copies, waits for them, and re-layouts: 8.35 us -> 6.57 us
  transfers between devices with their start and end apart: 27 -> 27, of which waited for: 9 -> 12; matrix products, arithmetic and copies ran while one was open for 1% -> 1% of each run, Pallas kernels for 27% -> 26%
where the time goes in v5:
time: 188 us
  waiting for transfers between devices  84.1 us (45%)
  Pallas kernels  51.7 us (28%)
  starting transfers between devices  41.2 us (22%)
  local copies, waits for them, and re-layouts  6.57 us (3%)
  other arithmetic  3.01 us (2%)
    ppermute x9, waiting for transfers between devices, along(): lax.ppermute(value, 'expert', [(2 * a + x, 2 * b + x) for a, b in pairs f...  32.3 us
    ppermute x11, waiting for transfers between devices, swap(): return lax.ppermute(value, 'dp', [(i, i ^ bit) for i in range(count)])  27.2 us
    ppermute x5, waiting for transfers between devices, across(): return lax.ppermute(value, 'expert', [(e, e ^ 1) for e in range(owners)])  24.6 us
    ppermute x9, starting transfers between devices, along(): lax.ppermute(value, 'expert', [(2 * a + x, 2 * b + x) for a, b in pairs f...  23.3 us
    pallas_call x1, Pallas kernels, layer(): pl.pallas_call(functools.partial(layer_kernel, cap, count), out_shape=(sl...  14.8 us
    pallas_call x1, Pallas kernels, last_layer(): pl.pallas_call(functools.partial(last_kernel, cap), out_shape=(slot, slot...  13.9 us
    pallas_call x1, Pallas kernels, outer(): pl.pallas_call(outer_kernel, out_shape=(block, block, send), in_specs=spe...  8.91 us
    ppermute x5, starting transfers between devices, across(): return lax.ppermute(value, 'expert', [(e, e ^ 1) for e in range(owners)])  7.14 us
  transfers between devices with their start and end apart: 27, of which 12 were waited for; matrix products, arithmetic and copies ran while one was open for 1% of the time, Pallas kernels for 26%

profile of v5, /device:TPU:0, one launch (start us, length us, event | category | flops | bytes accessed | tf_op | source)
XLA Modules:
  0.0 187.6 jit_solution(9043003354418293734)
XLA Ops:
  0.6 1.3 select_reduce_fusion.table_ref
  1.9 2.3 %prep.1.refs_0_ = bf16[272,2048]{1,0:T(8,128)(2,1)} custom-call(f32[8,128]{1,0:T(8,128)} %select_reduce_fusion.table_ref, bf16[128,2048]{1,0:T(8,128)(2,1)} %tokens_ref.1, bf16[128,2048]{1,0:T(8,128)(2,1)} %cots_ref.1), custom_call_target="tpu_custom_call" | custom-call | flops 2000000000 | tf_op jit(solution)/shard_map/prep/pallas_call | solution.py:177
  4.2 1.3 collective-permute-start.4
  5.5 5.6 %collective-permute-start.3 = (bf16[272,2048]{1,0:T(8,128)(2,1)}, bf16[272,2048]{1,0:T(8,128)(2,1)S(1)}, u32[]{:S(2)}, u32[]{:S(2)}) collective-permute-start(bf16[272,2048]{1,0:T(8,128)(2,1)} %prep.1.refs_0_), channel_id=1, source_target_pairs={{0,8},{4,12},{8,16},{12,20},{16,24},{20,28},{1,9},{5,13},{9,17},{1... | collective-permute-start | bytes 3342344 | tf_op jit(solution)/shard_map/ppermute | solution.py:702
  11.1 0.1 collective-permute-start
  11.2 0.5 collective-permute-start.1
  11.7 0.1 collective-permute-start.2
  11.8 2.7 %stack.1 = bf16[1024,768]{1,0:T(8,128)(2,1)} custom-call(bf16[512,768]{1,0:T(8,128)(2,1)} %bitcast.1.first_ref.refs_6_.refs_0_, bf16[512,768]{1,0:T(8,128)(2,1)} %bitcast.2.second_ref.refs_7_.refs_1_), custom_call_target="tpu_custom_call" | custom-call | tf_op jit(solution)/shard_map/stack/pallas_call | solution.py:195
  14.5 2.0 %collective-permute-start.11 = (bf16[1024,768]{1,0:T(8,128)(2,1)}, bf16[1024,768]{1,0:T(8,128)(2,1)}, u32[]{:S(2)}, u32[]{:S(2)}) collective-permute-start(bf16[1024,768]{1,0:T(8,128)(2,1)} %stack.1), channel_id=1, source_target_pairs={{0,2},{1,3},{2,0},{3,1},{4,6},{5,7},{6,4},{7,5},{8,10},{9,11},{10,... | collective-permute-start | bytes 4718600 | tf_op jit(solution)/shard_map/ppermute | solution.py:20
  16.5 0.7 pick_0.1
  17.2 1.6 pick_4.1
  18.8 3.4 %collective-permute-start.6 = (bf16[144,2048]{1,0:T(8,128)(2,1)S(1)}, bf16[144,2048]{1,0:T(8,128)(2,1)}, u32[]{:S(2)}, u32[]{:S(2)}) collective-permute-start(bf16[144,2048]{1,0:T(8,128)(2,1)S(1)} %get-tuple-element.70), channel_id=1, source_target_pairs={{0,4},{4,0},{24,28},{28,24},{1,5},{5,1},{25,29},{29,25},{2,6},{6,2... | collective-permute-start | bytes 1769480 | tf_op jit(solution)/shard_map/ppermute | solution.py:720
  22.3 0.6 collective-permute-start.5
  22.8 11.1 %collective-permute-done.4.refs_1_.refs_0_ = bf16[272,2048]{1,0:T(8,128)(2,1)S(1)} collective-permute-done((bf16[272,2048]{1,0:T(8,128)(2,1)}, bf16[272,2048]{1,0:T(8,128)(2,1)S(1)}, u32[]{:S(2)}, u32[]{:S(2)}) %collective-permute-start.4) | collective-permute-done | bytes 1114144 | tf_op jit(solution)/shard_map/ppermute | solution.py:702
  33.9 1.3 collective-permute-done.3.refs_0_.refs_1_
  35.2 1.4 collective-permute-start.8
  36.6 0.7 collective-permute-start.9
  37.4 0.8 pick_1.1
  38.2 10.5 %collective-permute-done.5.refs_1_ = bf16[144,2048]{1,0:T(8,128)(2,1)S(1)} collective-permute-done((bf16[144,2048]{1,0:T(8,128)(2,1)S(1)}, bf16[144,2048]{1,0:T(8,128)(2,1)S(1)}, u32[]{:S(2)}, u32[]{:S(2)}) %collective-permute-start.5) | collective-permute-done | bytes 589856 | tf_op jit(solution)/shard_map/ppermute | solution.py:705
  48.7 1.6 collective-permute-start.7
  50.3 1.5 collective-permute-start.13
  51.8 11.5 %collective-permute-done.7.refs_3_ = bf16[144,2048]{1,0:T(8,128)(2,1)S(1)} collective-permute-done((bf16[144,2048]{1,0:T(8,128)(2,1)S(1)}, bf16[144,2048]{1,0:T(8,128)(2,1)S(1)}, u32[]{:S(2)}, u32[]{:S(2)}) %collective-permute-start.7) | collective-permute-done | bytes 589856 | tf_op jit(solution)/shard_map/ppermute | solution.py:705
  63.3 0.1 collective-permute-done.8.refs_0_
  63.4 0.7 copy-done.15
  64.1 0.8 pick_2.1
  64.9 0.8 copy-done.8
  65.7 1.7 collective-permute-start.10
  67.3 1.6 collective-permute-done.13.refs_14_.refs_8_
  69.0 4.1 %collective-permute-start.17 = (bf16[160,2048]{1,0:T(8,128)(2,1)}, bf16[160,2048]{1,0:T(8,128)(2,1)}, u32[]{:S(2)}, u32[]{:S(2)}) collective-permute-start(bf16[160,2048]{1,0:T(8,128)(2,1)} %get-tuple-element.90), channel_id=1, source_target_pairs={{0,24},{4,28},{24,0},{28,4},{1,25},{5,29},{25,1},{29,5},{2,26},{6,... | collective-permute-start | bytes 1966088 | tf_op jit(solution)/shard_map/ppermute | solution.py:702
  73.1 3.5 %collective-permute-start.18 = (bf16[144,2048]{1,0:T(8,128)(2,1)}, bf16[144,2048]{1,0:T(8,128)(2,1)}, u32[]{:S(2)}, u32[]{:S(2)}) collective-permute-start(bf16[144,2048]{1,0:T(8,128)(2,1)} %collective-permute-done.6), channel_id=1, source_target_pairs={{0,24},{4,28},{24,0},{28,4},{1,25},{5,29},{25,1},{29,5},{2,26},{6,... | collective-permute-start | bytes 1769480 | tf_op jit(solution)/shard_map/ppermute | solution.py:702
  76.6 0.8 pick_3.1
  77.4 0.8 copy-done.7
  78.2 0.6 copy-done.10
  78.8 2.6 %collective-permute-done.10.refs_5_ = bf16[144,2048]{1,0:T(8,128)(2,1)S(1)} collective-permute-done((bf16[144,2048]{1,0:T(8,128)(2,1)S(1)}, bf16[144,2048]{1,0:T(8,128)(2,1)S(1)}, u32[]{:S(2)}, u32[]{:S(2)}) %collective-permute-start.10) | collective-permute-done | bytes 589856 | tf_op jit(solution)/shard_map/ppermute | solution.py:705
  81.4 0.8 copy-done.17
  82.2 0.9 collective-permute-start.16
  83.1 14.8 %layer.1 = (bf16[216,2048]{1,0:T(8,128)(2,1)}, bf16[216,2048]{1,0:T(8,128)(2,1)}, bf16[432,2048]{1,0:T(8,128)(2,1)}, bf16[432,2048]{1,0:T(8,128)(2,1)}, bf16[432...) custom-call(s32[1]{0:T(128)} %bitcast.6.dp_ref, bf16[144,2048]{1,0:T(8,128)(2,1)} %copy-done.5, ...), custom_call_target="tpu_custom_call" | custom-call | tf_op jit(solution)/shard_map/layer/pallas_call | solution.py:376
  97.9 1.7 collective-permute-start.15
  99.6 0.6 pad_add_fusion.dp_ref
  100.2 2.6 %collective-permute-done.18.far_got = bf16[144,2048]{1,0:T(8,128)(2,1)} collective-permute-done((bf16[144,2048]{1,0:T(8,128)(2,1)}, bf16[144,2048]{1,0:T(8,128)(2,1)}, u32[]{:S(2)}, u32[]{:S(2)}) %collective-permute-start.18) | collective-permute-done | bytes 589856 | tf_op jit(solution)/shard_map/ppermute | solution.py:702
  102.7 0.8 copy-done.16
  103.6 13.9 %last_layer.1 = (bf16[72,2048]{1,0:T(8,128)(2,1)}, bf16[72,2048]{1,0:T(8,128)(2,1)}, bf16[144,2048]{1,0:T(8,128)(2,1)}, bf16[144,768]{1,0:T(8,128)(2,1)}, bf16[1...) custom-call(s32[2]{0:T(128)} %pad_add_fusion.dp_ref, ...), custom_call_target="tpu_custom_call" | custom-call | tf_op jit(solution)/shard_map/last_layer/pallas_call | solution.py:503
  117.5 0.1 collective-permute-start.19
  117.5 1.6 collective-permute-start.22
  119.1 8.9 %outer.1 = (f32[512,1536]{1,0:T(8,128)}, f32[512,1536]{1,0:T(8,128)}, bf16[2,512,1536]{2,1,0:T(8,128)(2,1)}) custom-call(s32[1]{0:T(128)} %bitcast.6.dp_ref, bf16[432,2048]{1,0:T(8,128)(2,1)} %get-tuple-element.81.refs_0_, bf16[144,2048]{1,0:T(8,128)(2,1)} %get-tuple-element.96.refs_1_, bf16[432,768]{1,0:T(8,128)(2,1)} %get-tuple-element.97.refs_2_, ...), custom_call_target="tpu_custom_call" | custom-call | tf_op jit(solution)/shard_map/outer/pallas_call | solution.py:571
  128.1 0.1 collective-permute-start.25
  128.2 1.0 copy-done.4
  129.2 1.1 spread_3.1
  130.4 2.7 %collective-permute-start.21 = (bf16[128,2048]{1,0:T(8,128)(2,1)S(1)}, bf16[128,2048]{1,0:T(8,128)(2,1)S(1)}, u32[]{:S(2)}, u32[]{:S(2)}) collective-permute-start(bf16[128,2048]{1,0:T(8,128)(2,1)S(1)} %get-tuple-element.110), channel_id=1, source_target_pairs={{0,16},{4,20},{8,24},{12,28},{16,0},{20,4},{24,8},{28,12},{1,17},{... | collective-permute-start | bytes 1572872 | tf_op jit(solution)/shard_map/ppermute | solution.py:702
  133.1 0.2 merge.2
  133.3 1.6 collective-permute-start.20
  134.9 1.0 copy-done.9
  135.9 0.6 spread_1.1
  136.5 0.1 broadcast_select_fusion.1
  136.6 3.8 %collective-permute-start.24 = (bf16[128,2048]{1,0:T(8,128)(2,1)S(1)}, bf16[128,2048]{1,0:T(8,128)(2,1)S(1)}, u32[]{:S(2)}, u32[]{:S(2)}) collective-permute-start(bf16[128,2048]{1,0:T(8,128)(2,1)S(1)} %get-tuple-element.123), channel_id=1, source_target_pairs={{0,24},{4,28},{8,0},{12,4},{16,8},{20,12},{24,16},{28,20},{1,25},{... | collective-permute-start | bytes 1572872 | tf_op jit(solution)/shard_map/ppermute | solution.py:702
  140.4 0.3 merge.3
  140.7 0.6 collective-permute-start.26
  141.3 12.5 %collective-permute-done.20.far_ref = bf16[192,2048]{1,0:T(8,128)(2,1)S(1)} collective-permute-done((bf16[192,2048]{1,0:T(8,128)(2,1)S(1)}, bf16[192,2048]{1,0:T(8,128)(2,1)S(1)}, u32[]{:S(2)}, u32[]{:S(2)}) %collective-permute-start.20) | collective-permute-done | bytes 786464 | tf_op jit(solution)/shard_map/ppermute | solution.py:20
  153.8 1.0 finish_1.1
  154.8 13.1 %collective-permute-done.21 = bf16[128,2048]{1,0:T(8,128)(2,1)S(1)} collective-permute-done((bf16[128,2048]{1,0:T(8,128)(2,1)S(1)}, bf16[128,2048]{1,0:T(8,128)(2,1)S(1)}, u32[]{:S(2)}, u32[]{:S(2)}) %collective-permute-start.21) | collective-permute-done | bytes 524320 | tf_op jit(solution)/shard_map/ppermute | solution.py:702
  167.9 4.1 %collective-permute-done.24 = bf16[128,2048]{1,0:T(8,128)(2,1)S(1)} collective-permute-done((bf16[128,2048]{1,0:T(8,128)(2,1)S(1)}, bf16[128,2048]{1,0:T(8,128)(2,1)S(1)}, u32[]{:S(2)}, u32[]{:S(2)}) %collective-permute-start.24) | collective-permute-done | bytes 524320 | tf_op jit(solution)/shard_map/ppermute | solution.py:702
  172.1 1.1 add_convert_fusion
  173.2 13.0 %collective-permute-done.26.far_ref = bf16[512,1536]{1,0:T(8,128)(2,1)S(1)} collective-permute-done((bf16[512,1536]{1,0:T(8,128)(2,1)S(1)}, bf16[512,1536]{1,0:T(8,128)(2,1)S(1)}, u32[]{:S(2)}, u32[]{:S(2)}) %collective-permute-start.26) | collective-permute-done | bytes 1572896 | tf_op jit(solution)/shard_map/ppermute | solution.py:20
  186.2 1.4 finish_2.1
  (50 shorter events, 0.2 us)
Async XLA Ops:
  4.2 29.7 %collective-permute-start.4 = (bf16[272,2048]{1,0:T(8,128)(2,1)}, bf16[272,2048]{1,0:T(8,128)(2,1)S(1)}, u32[]{:S(2)}, u32[]{:S(2)}) collective-permute-start(bf16[272,2048]{1,0:T(8,128)(2,1)} %prep.1.refs_0_), channel_id=1, source_target_pairs={{8,0},{12,4},{16,8},{20,12},{24,16},{28,20},{9,1},{13,5},{17,9},{2... | collective-permute-start | bytes 3342344 | tf_op jit(solution)/shard_map/ppermute | solution.py:702
  5.5 29.7 %collective-permute-start.3 = (bf16[272,2048]{1,0:T(8,128)(2,1)}, bf16[272,2048]{1,0:T(8,128)(2,1)S(1)}, u32[]{:S(2)}, u32[]{:S(2)}) collective-permute-start(bf16[272,2048]{1,0:T(8,128)(2,1)} %prep.1.refs_0_), channel_id=1, source_target_pairs={{0,8},{4,12},{8,16},{12,20},{16,24},{20,28},{1,9},{5,13},{9,17},{1... | collective-permute-start | bytes 3342344 | tf_op jit(solution)/shard_map/ppermute | solution.py:702
  11.1 3.4 %collective-permute-start = (bf16[512,768]{1,0:T(8,128)(2,1)}, bf16[512,768]{1,0:T(8,128)(2,1)}, u32[]{:S(2)}, u32[]{:S(2)}) collective-permute-start(bf16[512,768]{1,0:T(8,128)(2,1)} %bitcast.1.first_ref.refs_6_.refs_0_), channel_id=1, source_target_pairs={{0,1},{1,0},{2,3},{3,2},{4,5},{5,4},{6,7},{7,6},{8,9},{9,8},{10,11... | collective-permute-start | bytes 2359304 | tf_op jit(solution)/shard_map/ppermute | solution.py:20
  11.2 5.3 %collective-permute-start.1 = (bf16[512,768]{1,0:T(8,128)(2,1)}, bf16[512,768]{1,0:T(8,128)(2,1)}, u32[]{:S(2)}, u32[]{:S(2)}) collective-permute-start(bf16[512,768]{1,0:T(8,128)(2,1)} %bitcast.2.second_ref.refs_7_.refs_1_), channel_id=1, source_target_pairs={{0,1},{1,0},{2,3},{3,2},{4,5},{5,4},{6,7},{7,6},{8,9},{9,8},{10,11... | collective-permute-start | bytes 2359304 | tf_op jit(solution)/shard_map/ppermute | solution.py:20
  11.7 4.8 %copy-start = (bf16[272,2048]{1,0:T(8,128)(2,1)S(1)}, bf16[272,2048]{1,0:T(8,128)(2,1)}, u32[]{:S(2)}) copy-start(bf16[272,2048]{1,0:T(8,128)(2,1)} %prep.1.refs_0_) | copy-start | bytes 3342340
  11.7 4.8 %collective-permute-start.2 = (bf16[192,2048]{1,0:T(8,128)(2,1)}, bf16[192,2048]{1,0:T(8,128)(2,1)}, u32[]{:S(2)}, u32[]{:S(2)}) collective-permute-start(bf16[192,2048]{1,0:T(8,128)(2,1)} %bitcast.11), channel_id=1, source_target_pairs={{0,1},{1,0},{2,3},{3,2},{4,5},{5,4},{6,7},{7,6},{8,9},{9,8},{10,11... | collective-permute-start | bytes 2359304 | tf_op jit(solution)/shard_map/ppermute | solution.py:20
  14.5 51.1 %collective-permute-start.11 = (bf16[1024,768]{1,0:T(8,128)(2,1)}, bf16[1024,768]{1,0:T(8,128)(2,1)}, u32[]{:S(2)}, u32[]{:S(2)}) collective-permute-start(bf16[1024,768]{1,0:T(8,128)(2,1)} %stack.1), channel_id=1, source_target_pairs={{0,2},{1,3},{2,0},{3,1},{4,6},{5,7},{6,4},{7,5},{8,10},{9,11},{10,... | collective-permute-start | bytes 4718600 | tf_op jit(solution)/shard_map/ppermute | solution.py:20
  17.2 18.0 %copy-start.5 = (bf16[144,2048]{1,0:T(8,128)(2,1)}, bf16[144,2048]{1,0:T(8,128)(2,1)S(1)}, u32[]{:S(2)}) copy-start(bf16[144,2048]{1,0:T(8,128)(2,1)S(1)} %get-tuple-element.66.refs_0_) | copy-start | bytes 1769476
  18.8 19.3 %collective-permute-start.6 = (bf16[144,2048]{1,0:T(8,128)(2,1)S(1)}, bf16[144,2048]{1,0:T(8,128)(2,1)}, u32[]{:S(2)}, u32[]{:S(2)}) collective-permute-start(bf16[144,2048]{1,0:T(8,128)(2,1)S(1)} %get-tuple-element.70), channel_id=1, source_target_pairs={{0,4},{4,0},{24,28},{28,24},{1,5},{5,1},{25,29},{29,25},{2,6},{6,2... | collective-permute-start | bytes 1769480 | tf_op jit(solution)/shard_map/ppermute | solution.py:720
  22.3 26.4 %collective-permute-start.5 = (bf16[144,2048]{1,0:T(8,128)(2,1)S(1)}, bf16[144,2048]{1,0:T(8,128)(2,1)S(1)}, u32[]{:S(2)}, u32[]{:S(2)}) collective-permute-start(bf16[144,2048]{1,0:T(8,128)(2,1)S(1)} %get-tuple-element.67), channel_id=1, source_target_pairs={{0,4},{4,0},{8,12},{12,8},{16,20},{20,16},{24,28},{28,24},{1,5},{5... | collective-permute-start | bytes 1769480 | tf_op jit(solution)/shard_map/ppermute | solution.py:705
  35.2 15.1 %copy-start.13 = (bf16[1,192,2048]{2,1,0:T(8,128)(2,1)S(1)}, bf16[1,192,2048]{2,1,0:T(8,128)(2,1)}, u32[]{:S(2)}) copy-start(bf16[1,192,2048]{2,1,0:T(8,128)(2,1)} %param.13) | copy-start | bytes 2359300
  35.2 28.2 %collective-permute-start.8 = (bf16[272,2048]{1,0:T(8,128)(2,1)S(1)}, bf16[272,2048]{1,0:T(8,128)(2,1)S(1)}, u32[]{:S(2)}, u32[]{:S(2)}) collective-permute-start(bf16[272,2048]{1,0:T(8,128)(2,1)S(1)} %collective-permute-done.4.refs_1_.refs_0_), channel_id=1, source_target_pairs={{8,0},{12,4},{16,8},{20,12},{9,1},{13,5},{17,9},{21,13},{10,2},{14... | collective-permute-start | bytes 3342344 | tf_op jit(solution)/shard_map/ppermute | solution.py:702
  36.6 27.5 %collective-permute-start.9 = (bf16[272,2048]{1,0:T(8,128)(2,1)S(1)}, bf16[272,2048]{1,0:T(8,128)(2,1)S(1)}, u32[]{:S(2)}, u32[]{:S(2)}) collective-permute-start(bf16[272,2048]{1,0:T(8,128)(2,1)S(1)} %collective-permute-done.3.refs_0_.refs_1_), channel_id=1, source_target_pairs={{8,16},{12,20},{16,24},{20,28},{9,17},{13,21},{17,25},{21,29},{10,... | collective-permute-start | bytes 3342344 | tf_op jit(solution)/shard_map/ppermute | solution.py:702
  38.1 26.7 %copy-start.6 = (bf16[144,2048]{1,0:T(8,128)(2,1)}, bf16[144,2048]{1,0:T(8,128)(2,1)S(1)}, u32[]{:S(2)}) copy-start(bf16[144,2048]{1,0:T(8,128)(2,1)S(1)} %get-tuple-element.68.refs_2_) | copy-start | bytes 1769476
  48.7 24.4 %copy-start.14 = (bf16[144,2048]{1,0:T(8,128)(2,1)}, bf16[144,2048]{1,0:T(8,128)(2,1)S(1)}, u32[]{:S(2)}) copy-start(bf16[144,2048]{1,0:T(8,128)(2,1)S(1)} %collective-permute-done.5.refs_1_) | copy-start | bytes 1769476
  48.7 14.6 %collective-permute-start.7 = (bf16[144,2048]{1,0:T(8,128)(2,1)S(1)}, bf16[144,2048]{1,0:T(8,128)(2,1)S(1)}, u32[]{:S(2)}, u32[]{:S(2)}) collective-permute-start(bf16[144,2048]{1,0:T(8,128)(2,1)S(1)} %get-tuple-element.71), channel_id=1, source_target_pairs={{0,4},{4,0},{8,12},{12,8},{16,20},{20,16},{24,28},{28,24},{1,5},{5... | collective-permute-start | bytes 1769480 | tf_op jit(solution)/shard_map/ppermute | solution.py:705
  50.3 18.7 %collective-permute-start.13 = (bf16[192,2048]{1,0:T(8,128)(2,1)S(1)}, bf16[192,2048]{1,0:T(8,128)(2,1)}, u32[]{:S(2)}, u32[]{:S(2)}) collective-permute-start(bf16[192,2048]{1,0:T(8,128)(2,1)S(1)} %bitcast.14), channel_id=1, source_target_pairs={{0,2},{1,3},{2,0},{3,1},{4,6},{5,7},{6,4},{7,5},{8,10},{9,11},{10,... | collective-permute-start | bytes 2359304 | tf_op jit(solution)/shard_map/ppermute | solution.py:20
  63.3 0.8 copy-start.15
  64.9 0.8 copy-start.8
  65.7 17.5 %collective-permute-start.12 = (bf16[1024,768]{1,0:T(8,128)(2,1)}, bf16[1024,768]{1,0:T(8,128)(2,1)}, u32[]{:S(2)}, u32[]{:S(2)}) collective-permute-start(bf16[1024,768]{1,0:T(8,128)(2,1)} %collective-permute-done.11.refs_10_.refs_4_), channel_id=1, source_target_pairs={{0,1},{1,0},{2,3},{3,2},{4,5},{5,4},{6,7},{7,6},{8,9},{9,8},{10,11... | collective-permute-start | bytes 4718600 | tf_op jit(solution)/shard_map/ppermute | solution.py:20
  65.7 15.7 %collective-permute-start.10 = (bf16[144,2048]{1,0:T(8,128)(2,1)S(1)}, bf16[144,2048]{1,0:T(8,128)(2,1)S(1)}, u32[]{:S(2)}, u32[]{:S(2)}) collective-permute-start(bf16[144,2048]{1,0:T(8,128)(2,1)S(1)} %get-tuple-element.76), channel_id=1, source_target_pairs={{0,4},{4,0},{8,12},{12,8},{16,20},{20,16},{24,28},{28,24},{1,5},{5... | collective-permute-start | bytes 1769480 | tf_op jit(solution)/shard_map/ppermute | solution.py:705
  68.9 14.2 %collective-permute-start.14 = (bf16[192,2048]{1,0:T(8,128)(2,1)}, bf16[192,2048]{1,0:T(8,128)(2,1)}, u32[]{:S(2)}, u32[]{:S(2)}) collective-permute-start(bf16[192,2048]{1,0:T(8,128)(2,1)} %collective-permute-done.13.refs_14_.refs_8_), channel_id=1, source_target_pairs={{0,1},{1,0},{2,3},{3,2},{4,5},{5,4},{6,7},{7,6},{8,9},{9,8},{10,11... | collective-permute-start | bytes 2359304 | tf_op jit(solution)/shard_map/ppermute | solution.py:20
  69.0 33.8 %collective-permute-start.17 = (bf16[160,2048]{1,0:T(8,128)(2,1)}, bf16[160,2048]{1,0:T(8,128)(2,1)}, u32[]{:S(2)}, u32[]{:S(2)}) collective-permute-start(bf16[160,2048]{1,0:T(8,128)(2,1)} %get-tuple-element.90), channel_id=1, source_target_pairs={{0,24},{4,28},{24,0},{28,4},{1,25},{5,29},{25,1},{29,5},{2,26},{6,... | collective-permute-start | bytes 1966088 | tf_op jit(solution)/shard_map/ppermute | solution.py:702
  73.1 29.7 %collective-permute-start.18 = (bf16[144,2048]{1,0:T(8,128)(2,1)}, bf16[144,2048]{1,0:T(8,128)(2,1)}, u32[]{:S(2)}, u32[]{:S(2)}) collective-permute-start(bf16[144,2048]{1,0:T(8,128)(2,1)} %collective-permute-done.6), channel_id=1, source_target_pairs={{0,24},{4,28},{24,0},{28,4},{1,25},{5,29},{25,1},{29,5},{2,26},{6,... | collective-permute-start | bytes 1769480 | tf_op jit(solution)/shard_map/ppermute | solution.py:702
  77.4 0.8 copy-start.7
  78.2 0.6 copy-start.10
  81.4 0.8 copy-start.17
  82.2 20.5 %collective-permute-start.16 = (bf16[144,2048]{1,0:T(8,128)(2,1)S(1)}, bf16[144,2048]{1,0:T(8,128)(2,1)S(1)}, u32[]{:S(2)}, u32[]{:S(2)}) collective-permute-start(bf16[144,2048]{1,0:T(8,128)(2,1)S(1)} %get-tuple-element.87), channel_id=1, source_target_pairs={{8,12},{12,8},{16,20},{20,16},{9,13},{13,9},{17,21},{21,17},{10,14... | collective-permute-start | bytes 1769480 | tf_op jit(solution)/shard_map/ppermute | solution.py:733
  97.9 30.2 %collective-permute-start.15 = (bf16[216,2048]{1,0:T(8,128)(2,1)}, bf16[216,2048]{1,0:T(8,128)(2,1)S(1)}, u32[]{:S(2)}, u32[]{:S(2)}) collective-permute-start(bf16[216,2048]{1,0:T(8,128)(2,1)} %get-tuple-element.80), channel_id=1, source_target_pairs={{0,4},{4,0},{8,12},{12,8},{16,20},{20,16},{24,28},{28,24},{1,5},{5... | collective-permute-start | bytes 2654216 | tf_op jit(solution)/shard_map/ppermute | solution.py:705
  102.7 0.8 copy-start.16
  117.5 15.7 %collective-permute-start.19 = (bf16[2,192,2048]{2,1,0:T(8,128)(2,1)}, bf16[2,192,2048]{2,1,0:T(8,128)(2,1)S(1)}, u32[]{:S(2)}, u32[]{:S(2)}) collective-permute-start(bf16[2,192,2048]{2,1,0:T(8,128)(2,1)} %get-tuple-element.106), channel_id=1, source_target_pairs={{0,1},{1,0},{2,3},{3,2},{4,5},{5,4},{6,7},{7,6},{8,9},{9,8},{10,11... | collective-permute-start | bytes 4718600 | tf_op jit(solution)/shard_map/ppermute | solution.py:20
  117.5 17.3 %collective-permute-start.22 = (bf16[72,2048]{1,0:T(8,128)(2,1)}, bf16[72,2048]{1,0:T(8,128)(2,1)S(1)}, u32[]{:S(2)}, u32[]{:S(2)}) collective-permute-start(bf16[72,2048]{1,0:T(8,128)(2,1)} %get-tuple-element.112), channel_id=1, source_target_pairs={{0,4},{4,0},{8,12},{12,8},{16,20},{20,16},{24,28},{28,24},{1,5},{5... | collective-permute-start | bytes 884744 | tf_op jit(solution)/shard_map/ppermute | solution.py:705
  128.1 1.2 copy-start.4
  128.1 12.3 %collective-permute-start.25 = (bf16[2,512,1536]{2,1,0:T(8,128)(2,1)}, bf16[2,512,1536]{2,1,0:T(8,128)(2,1)S(1)}, u32[]{:S(2)}, u32[]{:S(2)}) collective-permute-start(bf16[2,512,1536]{2,1,0:T(8,128)(2,1)} %get-tuple-element.101), channel_id=1, source_target_pairs={{0,1},{1,0},{2,3},{3,2},{4,5},{5,4},{6,7},{7,6},{8,9},{9,8},{10,11... | collective-permute-start | bytes 9437192 | tf_op jit(solution)/shard_map/ppermute | solution.py:20
  128.2 5.0 %copy-start.3 = (f32[192,2048]{1,0:T(8,128)S(1)}, f32[192,2048]{1,0:T(8,128)}, u32[]{:S(2)}) copy-start(f32[192,2048]{1,0:T(8,128)} %get-tuple-element.108.far_ref) | copy-start | bytes 4718596
  130.4 4.5 %copy-start.12 = (f32[8,128]{1,0:T(8,128)S(1)}, f32[8,128]{1,0:T(8,128)}, u32[]{:S(2)}) copy-start(f32[8,128]{1,0:T(8,128)} %get-tuple-element.113.in_ref) | copy-start | bytes 12292
  130.4 37.5 %collective-permute-start.21 = (bf16[128,2048]{1,0:T(8,128)(2,1)S(1)}, bf16[128,2048]{1,0:T(8,128)(2,1)S(1)}, u32[]{:S(2)}, u32[]{:S(2)}) collective-permute-start(bf16[128,2048]{1,0:T(8,128)(2,1)S(1)} %get-tuple-element.110), channel_id=1, source_target_pairs={{0,16},{4,20},{8,24},{12,28},{16,0},{20,4},{24,8},{28,12},{1,17},{... | collective-permute-start | bytes 1572872 | tf_op jit(solution)/shard_map/ppermute | solution.py:702
  133.3 20.5 %collective-permute-start.20 = (bf16[192,2048]{1,0:T(8,128)(2,1)S(1)}, bf16[192,2048]{1,0:T(8,128)(2,1)S(1)}, u32[]{:S(2)}, u32[]{:S(2)}) collective-permute-start(bf16[192,2048]{1,0:T(8,128)(2,1)S(1)} %merge.2), channel_id=1, source_target_pairs={{0,2},{1,3},{2,0},{3,1},{4,6},{5,7},{6,4},{7,5},{8,10},{9,11},{10,... | collective-permute-start | bytes 2359304 | tf_op jit(solution)/shard_map/ppermute | solution.py:20
  134.9 1.0 copy-start.9
  135.9 4.6 %copy-start.2 = (f32[512,1536]{1,0:T(8,128)S(1)}, f32[512,1536]{1,0:T(8,128)}, u32[]{:S(2)}) copy-start(f32[512,1536]{1,0:T(8,128)} %get-tuple-element.118.far_ref) | copy-start | bytes 9437188
  136.5 31.4 %collective-permute-start.23 = (bf16[128,2048]{1,0:T(8,128)(2,1)S(1)}, bf16[128,2048]{1,0:T(8,128)(2,1)S(1)}, u32[]{:S(2)}, u32[]{:S(2)}) collective-permute-start(bf16[128,2048]{1,0:T(8,128)(2,1)S(1)} %get-tuple-element.122), channel_id=1, source_target_pairs={{0,8},{4,12},{8,16},{12,20},{16,24},{20,28},{24,0},{28,4},{1,9},{5... | collective-permute-start | bytes 1572872 | tf_op jit(solution)/shard_map/ppermute | solution.py:702
  136.6 17.2 %copy-start.11 = (f32[192,2048]{1,0:T(8,128)S(1)}, f32[192,2048]{1,0:T(8,128)}, u32[]{:S(2)}) copy-start(f32[192,2048]{1,0:T(8,128)} %get-tuple-element.105.own_ref) | copy-start | bytes 4718596
  136.6 35.5 %collective-permute-start.24 = (bf16[128,2048]{1,0:T(8,128)(2,1)S(1)}, bf16[128,2048]{1,0:T(8,128)(2,1)S(1)}, u32[]{:S(2)}, u32[]{:S(2)}) collective-permute-start(bf16[128,2048]{1,0:T(8,128)(2,1)S(1)} %get-tuple-element.123), channel_id=1, source_target_pairs={{0,24},{4,28},{8,0},{12,4},{16,8},{20,12},{24,16},{28,20},{1,25},{... | collective-permute-start | bytes 1572872 | tf_op jit(solution)/shard_map/ppermute | solution.py:702
  140.7 45.5 %collective-permute-start.26 = (bf16[512,1536]{1,0:T(8,128)(2,1)S(1)}, bf16[512,1536]{1,0:T(8,128)(2,1)S(1)}, u32[]{:S(2)}, u32[]{:S(2)}) collective-permute-start(bf16[512,1536]{1,0:T(8,128)(2,1)S(1)} %merge.3), channel_id=1, source_target_pairs={{0,2},{1,3},{2,0},{3,1},{4,6},{5,7},{6,4},{7,5},{8,10},{9,11},{10,... | collective-permute-start | bytes 4718600 | tf_op jit(solution)/shard_map/ppermute | solution.py:20
  173.2 13.0 %copy-start.1 = (f32[512,1536]{1,0:T(8,128)S(1)}, f32[512,1536]{1,0:T(8,128)}, u32[]{:S(2)}) copy-start(f32[512,1536]{1,0:T(8,128)} %get-tuple-element.116.own_ref) | copy-start | bytes 9437188
